TPU v7x, 256 devices: a whole 4x4x8 slice. The times are simulated.
256 devices in a mesh: section: 4 (over x), lat: 32 (over y_hi, z, core), tok: 2 (over y_lo).
Axes of the slice: x: 4, y: 4 (y_hi: 2, y_lo: 2; y = y_hi * 2 + y_lo), z: 8, core: 2. Of those that a mesh axis runs over, the one named last changes fastest.
Arguments:
- residual: bfloat16 [2, 256, 8192], P('tok', 'section', 'lat'), may hold values from -6 to 6
- center: float32 [8192], P('lat'), may hold values from -5 to 5
- whiten: bfloat16 [8192, 8192], P('lat', 'section'), may hold values from -0.0625 to 0.0625
- decoder_bias: float32 [8192], P('section'), may hold values from -3 to 3
- encoder_weight: bfloat16 [8192, 32768], P(('section', 'tok'), 'lat'), may hold values from -0.0625 to 0.0625
- encoder_bias: float32 [32768], P('lat'), may hold values from -3 to 3
- decoder_weight: bfloat16 [32768, 8192], P('lat', ('section', 'tok')), may hold values from -0.75 to 0.75
- chosen: int32 [2, 256, 64], replicated, may hold values from 0 to 32767, as said below
Outputs:
- encoder_grad: bfloat16 [8192, 32768], P(('section', 'tok'), 'lat')
- decoder_grad: bfloat16 [32768, 8192], P('lat', ('section', 'tok'))
- bias_grad: float32 [32768], P(('lat', 'tok'))
Inputs may be any that keep to these rules, and one draw needn't show every extreme that they name: `chosen`: each row names 64 different latents.
All inputs are finite; a program needn't handle non-finite values.
Results may differ from a plain program's by a relative error of at most 0.0083.
Values may be sent and summed in bfloat16 or wider, within the bound.
No kernel may reach another device: no remote copies, remote signals or barrier semaphores. Data moves between devices by JAX's collectives and lax.ppermute only.
A program may use at most 128 MiB of HBM per device.

v0:
```python
import jax
import jax.numpy as jnp
from jax import lax
from jax.sharding import PartitionSpec as P

grad_scale = 0.125


def body(
    residual, center, whiten, decoder_bias, encoder_weight, encoder_bias, decoder_weight, chosen
):
    tok_place = lax.axis_index("tok")
    arrived = lax.all_gather(residual, "section", axis=1, tiled=True)
    rows_in = arrived[0]
    picks_in = lax.dynamic_index_in_dim(chosen, tok_place, 0, keepdims=False)
    encoder_full, decoder_full = (
        lax.all_gather(encoder_weight, "tok", axis=0, tiled=True),
        lax.all_gather(decoder_weight, "tok", axis=1, tiled=True),
    )
    centered = (rows_in.astype(jnp.float32) - center).astype(jnp.bfloat16)
    shard_count = lax.axis_size("lat")
    local_count = centered.shape[0] // shard_count
    own_first = lax.axis_index("lat") * local_count
    white_partial = jnp.dot(centered, whiten, preferred_element_type=jnp.float32)
    whitened = lax.psum(white_partial, "lat").astype(jnp.bfloat16)
    shifted = (whitened.astype(jnp.float32) - decoder_bias).astype(jnp.bfloat16)
    encoder_partial = jnp.dot(shifted, encoder_full, preferred_element_type=jnp.float32)
    encoded = lax.psum(encoder_partial, "section") + encoder_bias
    width_local = encoder_bias.shape[0]
    first_latent = lax.axis_index("lat") * width_local
    picked_latents = picks_in - first_latent
    in_range = (picked_latents >= 0) & (picked_latents < width_local)
    picked_latents = jnp.where(in_range, picked_latents, width_local)
    row_index = lax.broadcasted_iota(jnp.int32, picked_latents.shape, 0)
    selection = (
        jnp.zeros(encoded.shape, jnp.float32).at[row_index, picked_latents].set(1.0, mode="drop")
    )
    latent_codes = (encoded * selection).astype(jnp.bfloat16)
    rebuilt = (
        lax.psum_scatter(
            jnp.dot(latent_codes, decoder_full, preferred_element_type=jnp.float32),
            "lat",
            scatter_dimension=0,
            tiled=True,
        )
        + decoder_bias
    )
    own_whitened = lax.dynamic_slice_in_dim(whitened, own_first, local_count, 0)
    residual_error = rebuilt - own_whitened.astype(jnp.float32)
    own_grad = (grad_scale * residual_error).astype(jnp.bfloat16)
    out_grad = lax.all_gather(own_grad, "lat", axis=0, tiled=True)
    code_partial = lax.dot_general(
        out_grad, decoder_full, (((1,), (1,)), ((), ())), preferred_element_type=jnp.float32
    )
    code_grad = lax.psum(code_partial, "section")
    encoded_grad = (code_grad * selection).astype(jnp.bfloat16)
    contract_rows = (((0,), (0,)), ((), ()))
    encoder_part = lax.dot_general(
        shifted, encoded_grad, contract_rows, preferred_element_type=jnp.float32
    )
    decoder_part = lax.dot_general(
        latent_codes, out_grad, contract_rows, preferred_element_type=jnp.float32
    )
    bias_part = jnp.sum(encoded_grad.astype(jnp.float32), axis=0)
    encoder_total, decoder_total, bias_total = (
        lax.psum_scatter(encoder_part, "tok", scatter_dimension=0, tiled=True),
        lax.psum_scatter(decoder_part, "tok", scatter_dimension=1, tiled=True),
        lax.psum_scatter(bias_part, "tok", scatter_dimension=0, tiled=True),
    )
    return (encoder_total.astype(jnp.bfloat16), decoder_total.astype(jnp.bfloat16), bias_total)


def solution(mesh):
    return jax.shard_map(
        body,
        mesh=mesh,
        in_specs=(
            P("tok", "section", "lat"),
            P("lat"),
            P("lat", "section"),
            P("section"),
            P(("section", "tok"), "lat"),
            P("lat"),
            P("lat", ("section", "tok")),
            P(),
        ),
        out_specs=(P(("section", "tok"), "lat"), P("lat", ("section", "tok")), P(("lat", "tok"))),
        check_vma=False,
    )
```

profile of v0, /device:TPU:1, one launch (start us, length us, event | category | flops | bytes accessed | tf_op | source)
XLA Modules:
  0.0 777.1 jit_solution(11672113963260497797)
XLA Ops:
  7.2 0.7 all-gather.4.cloned.1.call-update
  8.0 10.5 %all_gather.12 = bf16[1,256,256]{2,1,0:T(8,128)(2,1)S(1)} all-gather(bf16[1,64,256]{2,1,0:T(8,128)(2,1)} %param.8), channel_id=1, replica_groups=mesh['section'=4,'lat'=32,'tok'=2] {'section'}, dimensions={1}, use_global_device_ids=true | all-gather | bytes 163840 | tf_op jit(solution)/shard_map/all_gather | solution.py:13
  18.5 1.1 fusion.5
  19.6 154.3 %all-reduce.8 = bf16[256,2048]{1,0:T(8,128)(2,1)} all-reduce(f32[256,2048]{1,0:T(8,128)S(1)} %fusion.5), channel_id=1, replica_groups=mesh['section'=4,'lat'=32,'tok'=2] {'lat'}, use_global_device_ids=true, to_apply=%region_0.1 | all-reduce | flops 524288 | bytes 3145728 | tf_op jit(solution)/shard_map/psum | solution.py:25
  174.0 4.8 fusion.1
  178.8 0.7 all-gather.6.cloned.1.call-update
  180.0 60.6 %scatter_custom_fusion = f32[262144]{0:T(1024)S(1)} fusion(s32[16384]{0:T(1024)S(1)} %reshape.61, f32[16384]{0:T(1024)S(1)} %broadcast.85, f32[]{:T(128)} %constant.10.clone.1), kind=kCustom, calls=%fused_computation.7 | custom fusion | bytes 1048580
  240.8 2.2 multiply_convert_fusion.1
  243.1 50.6 %all-gather.6.cloned.1.call-done = bf16[1024,2048]{1,0:T(8,128)(2,1)} async-done(((bf16[1024,1024]{1,0:T(8,128)(2,1)}), bf16[1024,2048]{1,0:T(8,128)(2,1)}) %all-gather.6.cloned.1.call-update) | async-done | bytes 4194320 | tf_op jit(solution)/shard_map/all_gather | solution.py:18
  293.7 4.9 fusion.10
  298.7 115.3 %reduce-scatter.4.cloned.1.call-done = f32[8,2048]{1,0:T(8,128)} async-done(((f32[256,2048]{1,0:T(8,128)}), f32[8,2048]{1,0:T(8,128)}) %reduce-scatter.4.cloned.1.call-update) | async-done | bytes 65552 | tf_op jit(solution)/shard_map/reduce_scatter | solution.py:40
  414.0 1.5 multiply_convert_fusion.2
  415.5 82.7 %all-gather.8.cloned.1.call-done = bf16[256,2048]{1,0:T(8,128)(2,1)} async-done(((bf16[8,2048]{1,0:T(8,128)(2,1)}), bf16[256,2048]{1,0:T(8,128)(2,1)}) %all-gather.8.cloned.1.call-update) | async-done | bytes 1048592 | tf_op jit(solution)/shard_map/all_gather | solution.py:51
  498.3 4.8 fusion.11
  503.1 5.9 fusion.12
  509.1 40.1 %all-reduce.7.cloned.1.call-done = f32[256,1024]{1,0:T(8,128)} async-done(((f32[256,1024]{1,0:T(8,128)}), f32[256,1024]{1,0:T(8,128)}) %all-reduce.7.cloned.1.call-update) | async-done | bytes 1048592 | tf_op jit(solution)/shard_map/psum | solution.py:55
  549.1 1.4 convert_reduce_fusion
  550.6 4.5 fusion
  557.0 3.8 all-reduce
  560.8 0.7 dynamic-slice.1
  561.4 97.1 %reduce-scatter.8.cloned.1.call-done = f32[1024,1024]{1,0:T(8,128)} async-done(((f32[1024,2048]{1,0:T(8,128)}), f32[1024,1024]{1,0:T(8,128)}) %reduce-scatter.8.cloned.1.call-update) | async-done | bytes 4194320 | tf_op jit(solution)/shard_map/reduce_scatter | solution.py:67
  658.5 3.8 convert_element_type.50
  662.3 104.1 %reduce-scatter.6.cloned.1.call-done = f32[1024,1024]{1,0:T(8,128)} async-done(((f32[2048,1024]{1,0:T(8,128)}), f32[1024,1024]{1,0:T(8,128)}) %reduce-scatter.6.cloned.1.call-update) | async-done | bytes 4194320 | tf_op jit(solution)/shard_map/reduce_scatter | solution.py:66
  766.4 3.8 convert_element_type.49
  (42 shorter events, 2.3 us)
Async XLA Ops:
  7.2 11.3 %copy-start = (bf16[256,2048]{1,0:T(8,128)(2,1)S(1)}, bf16[256,2048]{1,0:T(8,128)(2,1)}, u32[]{:S(2)}) copy-start(bf16[256,2048]{1,0:T(8,128)(2,1)} %param.10) | copy-start | bytes 3145732
  7.2 166.8 %copy-start.2 = (f32[2048]{0:T(1024)S(1)}, f32[2048]{0:T(1024)}, u32[]{:S(2)}) copy-start(f32[2048]{0:T(1024)} %param.11) | copy-start | bytes 24580
  7.2 166.8 %all-gather.4.cloned.1.call-start = ((), (), s32[]{:S(2)}) async-start(), calls=%async_computation.3 | async-start | bytes 6291456 | tf_op jit(solution)/shard_map/all_gather | solution.py:17
  7.9 232.9 %all-reduce.5.cloned.1.call-start = ((), (), s32[]{:S(2)}) async-start(), calls=%async_computation.4 | async-start | bytes 2097152 | tf_op jit(solution)/shard_map/psum | solution.py:28
  174.0 5.6 copy-start.3
  174.0 5.6 copy-start.6
  174.0 5.7 copy-start.5
  178.7 62.1 %copy-start.4 = (f32[1024]{0:T(1024)S(1)}, f32[1024]{0:T(1024)}, u32[]{:S(2)}) copy-start(f32[1024]{0:T(1024)} %param.13) | copy-start | bytes 12292
  178.8 114.9 %all-gather.6.cloned.1.call-start = ((), (), s32[]{:S(2)}) async-start(), calls=%async_computation.5 | async-start | bytes 6291456 | tf_op jit(solution)/shard_map/all_gather | solution.py:18
  179.5 234.5 %reduce-scatter.4.cloned.1.call-start = ((), (), s32[]{:S(2)}) async-start(), calls=%async_computation.6 | async-start | bytes 2162688 | tf_op jit(solution)/shard_map/reduce_scatter | solution.py:40
  243.1 170.9 %copy-start.1 = (bf16[256,2048]{1,0:T(8,128)(2,1)S(1)}, bf16[256,2048]{1,0:T(8,128)(2,1)}, u32[]{:S(2)}) copy-start(bf16[256,2048]{1,0:T(8,128)(2,1)} %all-reduce.8) | copy-start | bytes 3145732
  298.6 199.7 %all-gather.8.cloned.1.call-start = ((), (), s32[]{:S(2)}) async-start(), calls=%async_computation.7 | async-start | bytes 1081344 | tf_op jit(solution)/shard_map/all_gather | solution.py:51
  415.5 133.7 %all-reduce.7.cloned.1.call-start = ((), (), s32[]{:S(2)}) async-start(), calls=%async_computation.8 | async-start | bytes 2097152 | tf_op jit(solution)/shard_map/psum | solution.py:55
  503.1 155.4 %reduce-scatter.8.cloned.1.call-start = ((), (), s32[]{:S(2)}) async-start(), calls=%async_computation.10 | async-start | bytes 12582912 | tf_op jit(solution)/shard_map/reduce_scatter | solution.py:67
  509.0 257.4 %reduce-scatter.6.cloned.1.call-start = ((), (), s32[]{:S(2)}) async-start(), calls=%async_computation.9 | async-start | bytes 12582912 | tf_op jit(solution)/shard_map/reduce_scatter | solution.py:66
  555.1 0.7 copy-start.7
Sparse Core Ops, SparseCore 0:
  9.8 73.3 all-gather.3
  178.9 48.6 all-reduce.4
  229.5 64.1 all-gather.5
  298.8 115.1 reduce-scatter.3
  417.2 81.0 all-gather.7
  503.2 45.9 all-reduce.6
  551.9 106.5 reduce-scatter.7
  661.0 105.3 reduce-scatter.5
where the time goes:
time: 777 us
  waiting for transfers between devices  491 us (63%)
  blocking collectives  169 us (22%)
  local copies, waits for them, and re-layouts  62.8 us (8%)
  matrix products  26 us (3%)
  between operations  14.9 us (2%)
  other arithmetic  13 us (2%)
    psum x1, blocking collectives, body(): whitened = lax.psum(white_partial, 'lat').astype(jnp.bfloat16)  154 us
    reduce_scatter x1, waiting for transfers between devices, body(): lax.psum_scatter(jnp.dot(latent_codes, decoder_full, preferred_element_ty...  115 us
    reduce_scatter x1, waiting for transfers between devices, body(): lax.psum_scatter(encoder_part, 'tok', scatter_dimension=0, tiled=True)  104 us
    reduce_scatter x1, waiting for transfers between devices, body(): lax.psum_scatter(decoder_part, 'tok', scatter_dimension=1, tiled=True)  97.1 us
    all_gather x1, waiting for transfers between devices, body(): out_grad = lax.all_gather(own_grad, 'lat', axis=0, tiled=True)  82.7 us
    unnamed x22, local copies, waits for them, and re-layouts  62.7 us
    all_gather x1, waiting for transfers between devices, body(): lax.all_gather(decoder_weight, 'tok', axis=1, tiled=True)  50.6 us
    psum x1, waiting for transfers between devices, body(): code_grad = lax.psum(code_partial, 'section')  40.1 us
  transfers between devices with their start and end apart: 8, of which 6 were waited for; matrix products, arithmetic and copies ran while one was open for 10% of the time, Pallas kernels for 0%

commit v1 on v0

v1 whole, which is shorter than its diff:
```python
import functools

import jax
import jax.numpy as jnp
from jax import lax
from jax.experimental import pallas as pl
from jax.experimental.pallas import tpu as pltpu
from jax.sharding import Mesh
from jax.sharding import PartitionSpec as P

grad_scale = 0.125
LANES = 128
F32 = jnp.float32
BF16 = jnp.bfloat16
WHOLE = pl.BlockSpec(memory_space=pltpu.VMEM)
PARAMS = pltpu.CompilerParams(vmem_limit_bytes=24 * 1024 * 1024)


def call(kernel, out_shape, operands, flops=0, moved=0):
    return pl.pallas_call(
        kernel,
        out_shape=out_shape,
        in_specs=[WHOLE] * len(operands),
        out_specs=jax.tree.map(lambda _: WHOLE, out_shape),
        compiler_params=PARAMS,
        cost_estimate=pl.CostEstimate(flops=flops, bytes_accessed=moved, transcendentals=0),
    )(*operands)


def find_kernel(place_ref, slot_ref):
    half = LANES // 2
    width = slot_ref.shape[2]

    def step(i, carry):
        rows = pl.ds(pl.multiple_of(i * 8, 8), 8)
        place = place_ref[rows, :]
        column = lax.broadcasted_iota(jnp.int32, (8, width), 1)
        for m in range(2):
            slot = jnp.full((8, width), -1, jnp.int32)
            for k in range(m * half, (m + 1) * half):
                slot = jnp.where(place[:, k : k + 1] == column, k, slot)
            slot_ref[m, rows, :] = slot
        return carry

    lax.fori_loop(0, place_ref.shape[0] // 8, step, 0)


def pick(y, place):
    lane, chunk = place & (LANES - 1), place >> 7
    out = jnp.zeros(place.shape, F32)
    for j in range(y.shape[1] // LANES):
        found = jnp.take_along_axis(y[:, j * LANES : (j + 1) * LANES], lane, axis=1)
        out = jnp.where(chunk == j, found, out)
    return out


def product_pick_kernel(contract, x_ref, w_ref, place_ref, out_ref):
    y = lax.dot_general(
        x_ref[...], w_ref[...], (((1,), (contract,)), ((), ())), preferred_element_type=F32
    )
    out_ref[...] = pick(y, place_ref[...])


def product_join_kernel(contract, x_ref, w_ref, place_ref, own_ref, out_ref):
    y = lax.dot_general(
        x_ref[...], w_ref[...], (((1,), (contract,)), ((), ())), preferred_element_type=F32
    )
    lane = lax.broadcasted_iota(jnp.int32, out_ref.shape, 1)
    mine = own_ref[...]
    out_ref[...] = jnp.where(lane < LANES // 2, mine, pick(y, place_ref[...])).astype(BF16)


def spread_codes_kernel(m, packed_ref, slot_ref, bias_ref, w_ref, codes_ref, part_ref):
    packed = packed_ref[...]
    for j in range(codes_ref.shape[1] // LANES):
        cols = pl.ds(j * LANES, LANES)
        slot = slot_ref[m, :, cols]
        value = jnp.take_along_axis(packed, jnp.maximum(slot, 0), axis=1) + bias_ref[:, cols]
        codes_ref[:, cols] = jnp.where(slot >= 0, value, 0.0).astype(BF16)
    part_ref[...] = jnp.dot(
        codes_ref[...], w_ref[...], preferred_element_type=F32
    ).astype(part_ref.dtype)


def spread_grad_kernel(packed_ref, slot_ref, grad_ref, total_ref):
    packed = packed_ref[...]
    rows = packed.shape[0]
    for j in range(grad_ref.shape[1] // LANES):
        cols = pl.ds(j * LANES, LANES)
        total = jnp.zeros((1, LANES), F32)
        for m in range(2):
            slot = slot_ref[m, :, cols]
            value = jnp.take_along_axis(packed, jnp.maximum(slot, 0), axis=1)
            grad = jnp.where(slot >= 0, value, 0.0).astype(BF16)
            grad_ref[m * rows : (m + 1) * rows, cols] = grad
            total = total + jnp.sum(grad.astype(F32), axis=0, keepdims=True)
        total_ref[:, cols] = total


def swap_cores(x):
    return lax.ppermute(x, "core", [(0, 1), (1, 0)])


def spread_out(x, axes):
    n = lax.axis_size(axes)
    return lax.all_to_all(jnp.broadcast_to(x[None], (n,) + x.shape), axes, 0, 0)


def sum_parts(x, axes):
    n = lax.axis_size(axes)
    parts = lax.all_to_all(x.reshape((n, x.shape[0] // n) + x.shape[1:]), axes, 0, 0)
    return jnp.sum(parts.astype(F32), axis=0)


FEATURES = ("section", "tok")
COLUMN = ("yh", "z")


def body(
    residual, center, whiten, decoder_bias, encoder_weight, encoder_bias, decoder_weight, chosen
):
    core = lax.axis_index("core")
    tok = lax.axis_index("tok")
    width = encoder_weight.shape[0]
    latents = encoder_bias.shape[0]
    first = ((lax.axis_index("yh") * 8 + lax.axis_index("z")) * 2 + core) * latents

    own_picks = lax.dynamic_index_in_dim(chosen, core, 0, keepdims=False)
    other_picks = lax.dynamic_index_in_dim(chosen, 1 - core, 0, keepdims=False)
    place = jnp.concatenate([own_picks, other_picks], axis=1).astype(jnp.int32) - first
    rows = place.shape[0]

    centered = (residual[0].astype(F32) - center).astype(BF16)
    arrived = spread_out(centered, ("tok", "section")).reshape(2, rows, -1)
    own_rows = lax.dynamic_index_in_dim(arrived, core, 0, keepdims=False)
    other_rows = lax.dynamic_index_in_dim(arrived, 1 - core, 0, keepdims=False)
    whiten_cols = lax.dynamic_slice_in_dim(whiten, tok * width, width, 1)
    bias_cols = lax.dynamic_slice_in_dim(decoder_bias, tok * width, width, 0)

    slot = call(
        find_kernel,
        jax.ShapeDtypeStruct((2, rows, latents), jnp.int32),
        (place,),
        flops=2 * 64 * 2 * rows * latents,
        moved=8 * rows * latents,
    )

    other_part = jnp.dot(other_rows, whiten_cols, preferred_element_type=F32).astype(BF16)
    from_core = swap_cores(other_part)
    own_part = jnp.dot(own_rows, whiten_cols, preferred_element_type=F32)
    whitened = sum_parts((own_part + from_core.astype(F32)).astype(BF16), COLUMN).astype(BF16)
    shifted_share = (whitened.astype(F32) - bias_cols).astype(BF16)
    own_shifted = spread_out(shifted_share, COLUMN).reshape(rows, width)
    other_shifted = swap_cores(own_shifted)

    flops = 2 * rows * width * latents
    moved = 2 * width * latents + 4 * rows * width
    packed_f32 = jax.ShapeDtypeStruct((rows, LANES), F32)
    packed_bf16 = jax.ShapeDtypeStruct((rows, LANES), BF16)

    def packed_product(contract, own, other, weight):
        mine = call(
            functools.partial(product_pick_kernel, contract),
            packed_f32,
            (own, weight, place),
            flops,
            moved,
        )
        both = call(
            functools.partial(product_join_kernel, contract),
            packed_bf16,
            (other, weight, place, mine),
            flops,
            moved,
        )
        share = sum_parts(both, FEATURES).astype(BF16)
        return spread_out(share, FEATURES).reshape(rows, LANES).astype(F32)

    encoded = packed_product(0, own_shifted, other_shifted, encoder_weight)

    def decode(m, kind):
        return call(
            functools.partial(spread_codes_kernel, m),
            (
                jax.ShapeDtypeStruct((rows, latents), BF16),
                jax.ShapeDtypeStruct((rows, width), kind),
            ),
            (encoded, slot, encoder_bias[None], decoder_weight),
            flops,
            moved,
        )

    other_codes, other_part = decode(1, BF16)
    from_core = swap_cores(other_part)
    own_codes, own_part = decode(0, F32)
    rebuilt = sum_parts((own_part + from_core.astype(F32)).astype(BF16), COLUMN) + bias_cols
    own_grad_share = (grad_scale * (rebuilt - whitened.astype(F32))).astype(BF16)
    own_grad = spread_out(own_grad_share, COLUMN).reshape(rows, width)
    other_grad = swap_cores(own_grad)

    code_grad = packed_product(1, own_grad, other_grad, decoder_weight)

    contract_rows = (((0,), (0,)), ((), ()))
    codes = jnp.concatenate([own_codes, other_codes], axis=0)
    out_grad = jnp.concatenate([own_grad, other_grad], axis=0)
    decoder_grad = lax.dot_general(
        codes, out_grad, contract_rows, preferred_element_type=F32
    ).astype(BF16)

    encoded_grad, bias_total = call(
        spread_grad_kernel,
        (
            jax.ShapeDtypeStruct((2 * rows, latents), BF16),
            jax.ShapeDtypeStruct((1, latents), F32),
        ),
        (code_grad, slot),
        0,
        12 * rows * latents,
    )
    shifted = jnp.concatenate([own_shifted, other_shifted], axis=0)
    encoder_grad = lax.dot_general(
        shifted, encoded_grad, contract_rows, preferred_element_type=F32
    ).astype(BF16)
    half = latents // 2
    bias_grad = lax.dynamic_slice_in_dim(bias_total[0], tok * half, half, 0)
    return encoder_grad, decoder_grad, bias_grad


def solution(mesh):
    fine = Mesh(mesh.devices.reshape(4, 2, 8, 2, 2), ("section", "yh", "z", "core", "tok"))
    lat = ("yh", "z", "core")
    return jax.shard_map(
        body,
        mesh=fine,
        in_specs=(
            P("tok", "section", lat),
            P(lat),
            P(lat, "section"),
            P("section"),
            P(("section", "tok"), lat),
            P(lat),
            P(lat, ("section", "tok")),
            P(),
        ),
        out_specs=(P(("section", "tok"), lat), P(lat, ("section", "tok")), P(lat + ("tok",))),
        check_vma=False,
    )
```

time: 777 us -> 180 us (0.23)
  waiting for transfers between devices: 491 us -> 28.8 us
  blocking collectives: 169 us -> 70.7 us
  local copies, waits for them, and re-layouts: 62.8 us -> 7.42 us
  starting transfers between devices: 0.32 us -> 37.1 us
  Pallas kernels: 0 us -> 21.8 us
  matrix products: 26 us -> 9.49 us
  between operations: 14.9 us -> 0.99 us
  other arithmetic: 13 us -> 2.39 us
    reduce_scatter x3 -> x0, waiting for transfers between devices: 316 us -> none  [the longest x1 115 us: body(): lax.psum_scatter(jnp.dot(latent_codes, decoder_full, preferred_element_ty...]
    psum x1 -> x0, blocking collectives: 154 us -> none  [body(): whitened = lax.psum(white_partial, 'lat').astype(jnp.bfloat16)]
    all_gather x3 -> x0, waiting for transfers between devices: 133 us -> none  [the longest x1 82.7 us: body(): out_grad = lax.all_gather(own_grad, 'lat', axis=0, tiled=True)]
    all_to_all x0 -> x4, blocking collectives: none -> 70.7 us  [the longest x2 43.6 us: spread_out(): return lax.all_to_all(jnp.broadcast_to(x[None], (n,) + x.shape), axes, 0, 0)]
    unnamed x22 -> x30, local copies, waits for them, and re-layouts: 62.7 us -> 4.54 us
    psum x2 -> x0, waiting for transfers between devices: 40.1 us -> none  [the longest x1 40.1 us: body(): code_grad = lax.psum(code_partial, 'section')]
    all_to_all x0 -> x5, starting transfers between devices: none -> 28.4 us  [the longest x2 15.6 us: sum_parts(): lax.all_to_all(x.reshape((n, x.shape[0] // n) + x.shape[1:]), axes, 0, 0)]
    all_to_all x0 -> x5, waiting for transfers between devices: none -> 27.1 us  [the longest x2 20.2 us: sum_parts(): lax.all_to_all(x.reshape((n, x.shape[0] // n) + x.shape[1:]), axes, 0, 0)]
  transfers between devices with their start and end apart: 8 -> 9, of which waited for: 6 -> 6; matrix products, arithmetic and copies ran while one was open for 10% -> 3% of each run, Pallas kernels for 0% -> 9%
where the time goes in v1:
time: 180 us; the launch traced here: 179 us
  blocking collectives  70.7 us (39%)
  starting transfers between devices  37.1 us (21%)
  waiting for transfers between devices  28.8 us (16%)
  Pallas kernels  21.8 us (12%)
  matrix products  9.49 us (5%)
  local copies, waits for them, and re-layouts  7.42 us (4%)
  other arithmetic  2.39 us (1%)
    all_to_all x2, blocking collectives, spread_out(): return lax.all_to_all(jnp.broadcast_to(x[None], (n,) + x.shape), axes, 0, 0)  43.6 us
    all_to_all x2, blocking collectives, sum_parts(): lax.all_to_all(x.reshape((n, x.shape[0] // n) + x.shape[1:]), axes, 0, 0)  27.2 us
    pallas_call x8, Pallas kernels, call(): pl.pallas_call(kernel, out_shape=out_shape, in_specs=[WHOLE] * len(operan...  21.8 us
    all_to_all x2, waiting for transfers between devices, sum_parts(): lax.all_to_all(x.reshape((n, x.shape[0] // n) + x.shape[1:]), axes, 0, 0)  20.2 us
    all_to_all x2, starting transfers between devices, sum_parts(): lax.all_to_all(x.reshape((n, x.shape[0] // n) + x.shape[1:]), axes, 0, 0)  15.6 us
    all_to_all x3, starting transfers between devices, spread_out(): return lax.all_to_all(jnp.broadcast_to(x[None], (n,) + x.shape), axes, 0, 0)  12.7 us
    ppermute x4, starting transfers between devices, swap_cores(): return lax.ppermute(x, 'core', [(0, 1), (1, 0)])  8.7 us
    all_to_all x3, waiting for transfers between devices, spread_out(): return lax.all_to_all(jnp.broadcast_to(x[None], (n,) + x.shape), axes, 0, 0)  6.85 us
  transfers between devices with their start and end apart: 9, of which 6 were waited for; matrix products, arithmetic and copies ran while one was open for 3% of the time, Pallas kernels for 9%

profile of v1, /device:TPU:1, one launch (start us, length us, event | category | flops | bytes accessed | tf_op | source)
XLA Modules:
  0.0 178.7 jit_solution(5497913584268496866)
XLA Ops:
  2.2 5.9 %all-to-all-start = ((bf16[8,64,256]{2,1,0:T(8,128)(2,1)}), bf16[8,64,256]{2,1,0:T(8,128)(2,1)S(1)}, u32[]{:S(2)}, u32[]{:S(2)}) async-start(bf16[8,64,256]{2,1,0:T(8,128)(2,1)} %broadcast_in_dim.15), calls=%async_computation | async-start | bytes 524288 | tf_op jit(solution)/shard_map/all_to_all | solution.py:106
  8.1 6.3 %all-to-all-done = bf16[8,64,256]{2,1,0:T(8,128)(2,1)S(1)} async-done(((bf16[8,64,256]{2,1,0:T(8,128)(2,1)}), bf16[8,64,256]{2,1,0:T(8,128)(2,1)S(1)}, u32[]{:S(2)}, u32[]{:S(2)}) %all-to-all-start) | async-done | bytes 262176 | tf_op jit(solution)/shard_map/all_to_all | solution.py:106
  14.7 2.0 %collective-permute-start = (bf16[256,1024]{1,0:T(8,128)(2,1)S(1)}, bf16[256,1024]{1,0:T(8,128)(2,1)S(1)}, u32[]{:S(2)}, u32[]{:S(2)}) collective-permute-start(bf16[256,1024]{1,0:T(8,128)(2,1)S(1)} %convolution_convert_fusion.2), channel_id=1, source_target_pairs={{0,2},{2,0},{1,3},{3,1},{4,6},{6,4},{5,7},{7,5},{8,10},{10,8},{9,1... | collective-permute-start | bytes 1572872 | tf_op jit(solution)/shard_map/ppermute | solution.py:101
  16.7 1.5 collective-permute-done
  19.4 10.8 %all-to-all-start.1 = ((bf16[16,16,1024]{2,1,0:T(8,128)(2,1)}), bf16[16,16,1024]{2,1,0:T(8,128)(2,1)}, u32[]{:S(2)}, u32[]{:S(2)}) async-start(bf16[16,16,1024]{2,1,0:T(8,128)(2,1)} %bitcast.32), calls=%async_computation.1 | async-start | bytes 1048576 | tf_op jit(solution)/shard_map/all_to_all | solution.py:111
  30.2 15.1 %all-to-all-done.1 = bf16[16,16,1024]{2,1,0:T(8,128)(2,1)} async-done(((bf16[16,16,1024]{2,1,0:T(8,128)(2,1)}), bf16[16,16,1024]{2,1,0:T(8,128)(2,1)}, u32[]{:S(2)}, u32[]{:S(2)}) %all-to-all-start.1) | async-done | bytes 524320 | tf_op jit(solution)/shard_map/all_to_all | solution.py:111
  46.5 21.8 %all_to_all.45 = bf16[16,16,1024]{2,1,0:T(8,128)(2,1)} all-to-all(bf16[16,16,1024]{2,1,0:T(8,128)(2,1)S(1)} %broadcast_in_dim.16), channel_id=1, replica_groups=mesh['section'=4,'yh'=2,'z'=8,'core'=2,'tok'=2] {'yh','z'}, dimensions={0} | all-to-all | bytes 1048576 | tf_op jit(solution)/shard_map/all_to_all | solution.py:106
  68.4 2.8 %collective-permute-start.1 = (bf16[256,1024]{1,0:T(8,128)(2,1)}, bf16[256,1024]{1,0:T(8,128)(2,1)}, u32[]{:S(2)}, u32[]{:S(2)}) collective-permute-start(bf16[256,1024]{1,0:T(8,128)(2,1)} %bitcast.5.x_ref), channel_id=1, source_target_pairs={{0,2},{2,0},{1,3},{3,1},{4,6},{6,4},{5,7},{7,5},{8,10},{10,8},{9,1... | collective-permute-start | bytes 1572872 | tf_op jit(solution)/shard_map/ppermute | solution.py:101
  71.6 2.0 %shard_map.103.own_ref = f32[256,128]{1,0:T(8,128)S(1)} custom-call(bf16[256,1024]{1,0:T(8,128)(2,1)} %bitcast.5.x_ref, bf16[1024,1024]{1,0:T(8,128)(2,1)S(1)} %copy-done.5, s32[256,128]{1,0:T(8,128)S(1)} %add_subtract_fusion.place_ref), custom_call_target="tpu_custom_call" | custom-call | flops 536870912 | bytes 3145728 | tf_op jit(solution)/shard_map/pallas_call | solution.py:20
  73.6 1.9 %shard_map.104 = bf16[256,128]{1,0:T(8,128)(2,1)S(1)} custom-call(bf16[256,1024]{1,0:T(8,128)(2,1)} %collective-permute-done.1.x_ref, bf16[1024,1024]{1,0:T(8,128)(2,1)S(1)} %copy-done.5, s32[256,128]{1,0:T(8,128)S(1)} %add_subtract_fusion.place_ref, f32[256,128]{1,0:T(8,128)S(1)} %shard_map.103.own_ref), custom_call_target="tpu_custom_call" | custom-call | flops 536870912 | bytes 3145728 | tf_op jit(solution)/shard_map/pallas_call | solution.py:20
  75.5 7.7 %all_to_all.46 = bf16[8,32,128]{2,1,0:T(8,128)(2,1)S(1)} all-to-all(bf16[8,32,128]{2,1,0:T(8,128)(2,1)S(1)} %bitcast.29), channel_id=1, replica_groups=mesh['section'=4,'yh'=2,'z'=8,'core'=2,'tok'=2] {'section','tok'}, dimensions={0} | all-to-all | bytes 131072 | tf_op jit(solution)/shard_map/all_to_all | solution.py:111
  83.9 3.4 %all-to-all-start.4 = ((bf16[8,32,128]{2,1,0:T(8,128)(2,1)}), bf16[8,32,128]{2,1,0:T(8,128)(2,1)S(1)}, u32[]{:S(2)}, u32[]{:S(2)}) async-start(bf16[8,32,128]{2,1,0:T(8,128)(2,1)} %broadcast_in_dim.17), calls=%async_computation.4 | async-start | bytes 131072 | tf_op jit(solution)/shard_map/all_to_all | solution.py:106
  87.2 11.2 %shard_map.105.slot_ref = s32[2,256,1024]{2,1,0:T(8,128)S(1)} custom-call(s32[256,128]{1,0:T(8,128)S(1)} %add_subtract_fusion.place_ref), custom_call_target="tpu_custom_call" | custom-call | flops 67108864 | bytes 2097152 | tf_op jit(solution)/shard_map/pallas_call | solution.py:20
  99.8 1.6 copy-done.3
  106.3 19.4 %all_to_all.47 = bf16[16,16,1024]{2,1,0:T(8,128)(2,1)S(1)} all-to-all(bf16[16,16,1024]{2,1,0:T(8,128)(2,1)S(1)} %bitcast.33), channel_id=1, replica_groups=mesh['section'=4,'yh'=2,'z'=8,'core'=2,'tok'=2] {'yh','z'}, dimensions={0} | all-to-all | bytes 1048576 | tf_op jit(solution)/shard_map/all_to_all | solution.py:111
  125.9 21.7 %all_to_all.48 = bf16[16,16,1024]{2,1,0:T(8,128)(2,1)S(1)} all-to-all(bf16[16,16,1024]{2,1,0:T(8,128)(2,1)S(1)} %broadcast_in_dim.19), channel_id=1, replica_groups=mesh['section'=4,'yh'=2,'z'=8,'core'=2,'tok'=2] {'yh','z'}, dimensions={0} | all-to-all | bytes 1048576 | tf_op jit(solution)/shard_map/all_to_all | solution.py:106
  147.7 2.8 %collective-permute-start.3 = (bf16[256,1024]{1,0:T(8,128)(2,1)S(1)}, bf16[256,1024]{1,0:T(8,128)(2,1)S(1)}, u32[]{:S(2)}, u32[]{:S(2)}) collective-permute-start(bf16[256,1024]{1,0:T(8,128)(2,1)S(1)} %bitcast.26), channel_id=1, source_target_pairs={{0,2},{2,0},{1,3},{3,1},{4,6},{6,4},{5,7},{7,5},{8,10},{10,8},{9,1... | collective-permute-start | bytes 1572872 | tf_op jit(solution)/shard_map/ppermute | solution.py:101
  152.3 1.5 shard_map.109
  153.8 4.8 %all-to-all-start.7 = ((bf16[8,32,128]{2,1,0:T(8,128)(2,1)}), bf16[8,32,128]{2,1,0:T(8,128)(2,1)S(1)}, u32[]{:S(2)}, u32[]{:S(2)}) async-start(bf16[8,32,128]{2,1,0:T(8,128)(2,1)} %bitcast.14), calls=%async_computation.7 | async-start | bytes 131072 | tf_op jit(solution)/shard_map/all_to_all | solution.py:111
  158.6 5.1 %all-to-all-done.7 = bf16[8,32,128]{2,1,0:T(8,128)(2,1)S(1)} async-done(((bf16[8,32,128]{2,1,0:T(8,128)(2,1)}), bf16[8,32,128]{2,1,0:T(8,128)(2,1)S(1)}, u32[]{:S(2)}, u32[]{:S(2)}) %all-to-all-start.7) | async-done | bytes 65568 | tf_op jit(solution)/shard_map/all_to_all | solution.py:111
  164.4 3.5 %all-to-all-start.8 = ((bf16[8,32,128]{2,1,0:T(8,128)(2,1)}), bf16[8,32,128]{2,1,0:T(8,128)(2,1)S(1)}, u32[]{:S(2)}, u32[]{:S(2)}) async-start(bf16[8,32,128]{2,1,0:T(8,128)(2,1)} %broadcast_in_dim.20), calls=%async_computation.8 | async-start | bytes 131072 | tf_op jit(solution)/shard_map/all_to_all | solution.py:106
  167.9 4.3 %convolution_convert_fusion = bf16[1024,1024]{1,0:T(8,128)(2,1)} fusion(bf16[256,1024]{1,0:T(8,128)(2,1)} %copy-done.9, bf16[256,1024]{1,0:T(8,128)(2,1)} %copy-done.10, bf16[256,1024]{1,0:T(8,128)(2,1)} %copy-done.7, bf16[256,1024]{1,0:T(8,128)(2,1)} %bitcast.28), kind=kOutput, calls=%fused_computation | convolution fusion | flops 1078984704 | bytes 4194304 | tf_op jit(solution)/shard_map/dot_general | solution.py:206
  172.8 1.5 shard_map.110
  174.9 3.8 %convolution_convert_fusion.1 = bf16[1024,1024]{1,0:T(8,128)(2,1)} fusion(bf16[512,1024]{1,0:T(8,128)(2,1)S(1)} %get-tuple-element.11, bf16[256,1024]{1,0:T(8,128)(2,1)} %collective-permute-done.1.x_ref, bf16[256,1024]{1,0:T(8,128)(2,1)} %bitcast.5.x_ref), kind=kOutput, calls=%fused_computation.1 | convolution fusion | flops 1076887552 | bytes 4194304 | tf_op jit(solution)/shard_map/dot_general | solution.py:221
  (61 shorter events, 15.1 us)
Async XLA Ops:
  0.6 13.8 %copy-start = (bf16[256,2048]{1,0:T(8,128)(2,1)S(1)}, bf16[256,2048]{1,0:T(8,128)(2,1)}, u32[]{:S(2)}) copy-start(bf16[256,2048]{1,0:T(8,128)(2,1)} %param.10) | copy-start | bytes 3145732
  2.2 12.2 %all-to-all-start = ((bf16[8,64,256]{2,1,0:T(8,128)(2,1)}), bf16[8,64,256]{2,1,0:T(8,128)(2,1)S(1)}, u32[]{:S(2)}, u32[]{:S(2)}) async-start(bf16[8,64,256]{2,1,0:T(8,128)(2,1)} %broadcast_in_dim.15), calls=%async_computation | async-start | bytes 524288 | tf_op jit(solution)/shard_map/all_to_all | solution.py:106
  8.1 22.1 %copy-start.14 = (f32[2048]{0:T(1024)S(1)}, f32[2048]{0:T(1024)}, u32[]{:S(2)}) copy-start(f32[2048]{0:T(1024)} %param.11) | copy-start | bytes 24580
  14.7 3.6 %collective-permute-start = (bf16[256,1024]{1,0:T(8,128)(2,1)S(1)}, bf16[256,1024]{1,0:T(8,128)(2,1)S(1)}, u32[]{:S(2)}, u32[]{:S(2)}) collective-permute-start(bf16[256,1024]{1,0:T(8,128)(2,1)S(1)} %convolution_convert_fusion.2), channel_id=1, source_target_pairs={{0,2},{2,0},{1,3},{3,1},{4,6},{6,4},{5,7},{7,5},{8,10},{10,8},{9,1... | collective-permute-start | bytes 1572872 | tf_op jit(solution)/shard_map/ppermute | solution.py:101
  16.7 54.5 %copy-start.13 = (s32[2,256,64]{1,2,0:T(8,128)S(1)}, s32[2,256,64]{1,2,0:T(8,128)}, u32[]{:S(2)}) copy-start(s32[2,256,64]{1,2,0:T(8,128)} %param.15) | copy-start | bytes 393220
  19.4 52.2 %copy-start.5 = (bf16[1024,1024]{1,0:T(8,128)(2,1)S(1)}, bf16[1024,1024]{1,0:T(8,128)(2,1)}, u32[]{:S(2)}) copy-start(bf16[1024,1024]{1,0:T(8,128)(2,1)} %w_ref.7) | copy-start | bytes 6291460
  19.4 26.0 %all-to-all-start.1 = ((bf16[16,16,1024]{2,1,0:T(8,128)(2,1)}), bf16[16,16,1024]{2,1,0:T(8,128)(2,1)}, u32[]{:S(2)}, u32[]{:S(2)}) async-start(bf16[16,16,1024]{2,1,0:T(8,128)(2,1)} %bitcast.32), calls=%async_computation.1 | async-start | bytes 1048576 | tf_op jit(solution)/shard_map/all_to_all | solution.py:111
  46.5 25.0 %copy-start.11 = (bf16[16,1024]{1,0:T(8,128)(2,1)}, bf16[16,1024]{1,0:T(8,128)(2,1)S(1)}, u32[]{:S(2)}) copy-start(bf16[16,1024]{1,0:T(8,128)(2,1)S(1)} %reduce_sum.45) | copy-start | bytes 98308
  68.4 5.2 %collective-permute-start.1 = (bf16[256,1024]{1,0:T(8,128)(2,1)}, bf16[256,1024]{1,0:T(8,128)(2,1)}, u32[]{:S(2)}, u32[]{:S(2)}) collective-permute-start(bf16[256,1024]{1,0:T(8,128)(2,1)} %bitcast.5.x_ref), channel_id=1, source_target_pairs={{0,2},{2,0},{1,3},{3,1},{4,6},{6,4},{5,7},{7,5},{8,10},{10,8},{9,1... | collective-permute-start | bytes 1572872 | tf_op jit(solution)/shard_map/ppermute | solution.py:101
  75.5 24.3 %copy-start.1 = (bf16[1024,1024]{1,0:T(8,128)(2,1)S(1)}, bf16[1024,1024]{1,0:T(8,128)(2,1)}, u32[]{:S(2)}) copy-start(bf16[1024,1024]{1,0:T(8,128)(2,1)} %w_ref.11) | copy-start | bytes 6291460
  75.5 24.3 %copy-start.8 = (f32[1024]{0:T(1024)S(1)}, f32[1024]{0:T(1024)}, u32[]{:S(2)}) copy-start(f32[1024]{0:T(1024)} %param.13) | copy-start | bytes 12292
  83.9 15.9 %all-to-all-start.4 = ((bf16[8,32,128]{2,1,0:T(8,128)(2,1)}), bf16[8,32,128]{2,1,0:T(8,128)(2,1)S(1)}, u32[]{:S(2)}, u32[]{:S(2)}) async-start(bf16[8,32,128]{2,1,0:T(8,128)(2,1)} %broadcast_in_dim.17), calls=%async_computation.4 | async-start | bytes 131072 | tf_op jit(solution)/shard_map/all_to_all | solution.py:106
  98.4 1.3 copy-start.2
  99.8 1.6 copy-start.3
  102.8 0.8 copy-start.9
  103.6 2.6 %collective-permute-start.2 = (bf16[256,1024]{1,0:T(8,128)(2,1)S(1)}, bf16[256,1024]{1,0:T(8,128)(2,1)S(1)}, u32[]{:S(2)}, u32[]{:S(2)}) collective-permute-start(bf16[256,1024]{1,0:T(8,128)(2,1)S(1)} %get-tuple-element.10), channel_id=1, source_target_pairs={{0,2},{2,0},{1,3},{3,1},{4,6},{6,4},{5,7},{7,5},{8,10},{10,8},{9,1... | collective-permute-start | bytes 1572872 | tf_op jit(solution)/shard_map/ppermute | solution.py:101
  106.0 19.9 %copy-start.10 = (bf16[256,1024]{1,0:T(8,128)(2,1)}, bf16[256,1024]{1,0:T(8,128)(2,1)S(1)}, u32[]{:S(2)}) copy-start(bf16[256,1024]{1,0:T(8,128)(2,1)S(1)} %get-tuple-element.12) | copy-start | bytes 1572868
  106.0 19.8 %copy-start.12 = (bf16[16,1024]{1,0:T(8,128)(2,1)S(1)}, bf16[16,1024]{1,0:T(8,128)(2,1)}, u32[]{:S(2)}) copy-start(bf16[16,1024]{1,0:T(8,128)(2,1)} %copy-done.11) | copy-start | bytes 98308
  147.7 4.6 %collective-permute-start.3 = (bf16[256,1024]{1,0:T(8,128)(2,1)S(1)}, bf16[256,1024]{1,0:T(8,128)(2,1)S(1)}, u32[]{:S(2)}, u32[]{:S(2)}) collective-permute-start(bf16[256,1024]{1,0:T(8,128)(2,1)S(1)} %bitcast.26), channel_id=1, source_target_pairs={{0,2},{2,0},{1,3},{3,1},{4,6},{6,4},{5,7},{7,5},{8,10},{10,8},{9,1... | collective-permute-start | bytes 1572872 | tf_op jit(solution)/shard_map/ppermute | solution.py:101
  151.5 0.8 copy-start.6
  152.3 1.5 copy-start.7
  153.8 9.9 %all-to-all-start.7 = ((bf16[8,32,128]{2,1,0:T(8,128)(2,1)}), bf16[8,32,128]{2,1,0:T(8,128)(2,1)S(1)}, u32[]{:S(2)}, u32[]{:S(2)}) async-start(bf16[8,32,128]{2,1,0:T(8,128)(2,1)} %bitcast.14), calls=%async_computation.7 | async-start | bytes 131072 | tf_op jit(solution)/shard_map/all_to_all | solution.py:111
  164.4 8.4 %all-to-all-start.8 = ((bf16[8,32,128]{2,1,0:T(8,128)(2,1)}), bf16[8,32,128]{2,1,0:T(8,128)(2,1)S(1)}, u32[]{:S(2)}, u32[]{:S(2)}) async-start(bf16[8,32,128]{2,1,0:T(8,128)(2,1)} %broadcast_in_dim.20), calls=%async_computation.8 | async-start | bytes 131072 | tf_op jit(solution)/shard_map/all_to_all | solution.py:106
  167.9 4.9 %copy-start.4 = (s32[2,256,1024]{2,1,0:T(8,128)S(1)}, s32[2,256,1024]{2,1,0:T(8,128)}, u32[]{:S(2)}) copy-start(s32[2,256,1024]{2,1,0:T(8,128)} %copy-done.2) | copy-start | bytes 6291460

commit v2 on v1

v2 whole, which is shorter than its diff:
```python
import functools

import jax
import jax.numpy as jnp
from jax import lax
from jax.experimental import pallas as pl
from jax.experimental.pallas import tpu as pltpu
from jax.sharding import Mesh
from jax.sharding import PartitionSpec as P

grad_scale = 0.125
LANES = 128
F32 = jnp.float32
BF16 = jnp.bfloat16
WHOLE = pl.BlockSpec(memory_space=pltpu.VMEM)
PARAMS = pltpu.CompilerParams(vmem_limit_bytes=20 * 1024 * 1024)


def call(kernel, out_shape, operands, flops=0, moved=0):
    return pl.pallas_call(
        kernel,
        out_shape=out_shape,
        in_specs=[WHOLE] * len(operands),
        out_specs=jax.tree.map(lambda _: WHOLE, out_shape),
        compiler_params=PARAMS,
        cost_estimate=pl.CostEstimate(flops=flops, bytes_accessed=moved, transcendentals=0),
    )(*operands)


def find_kernel(place_ref, slot_ref):
    half = LANES // 2
    width = slot_ref.shape[2]

    def step(i, carry):
        rows = pl.ds(pl.multiple_of(i * 8, 8), 8)
        place = place_ref[rows, :]
        column = lax.broadcasted_iota(jnp.int32, (8, width), 1)
        for m in range(2):
            slot = jnp.full((8, width), -1, jnp.int32)
            for k in range(m * half, (m + 1) * half):
                slot = jnp.where(place[:, k : k + 1] == column, k, slot)
            slot_ref[m, rows, :] = slot
        return carry

    lax.fori_loop(0, place_ref.shape[0] // 8, step, 0)


def pick(y, place):
    lane, chunk = place & (LANES - 1), place >> 7
    out = jnp.zeros(place.shape, F32)
    for j in range(y.shape[1] // LANES):
        found = jnp.take_along_axis(y[:, j * LANES : (j + 1) * LANES], lane, axis=1)
        out = jnp.where(chunk == j, found, out)
    return out


def whiten_other_kernel(x_ref, center_ref, w_ref, out_ref):
    x = (x_ref[...].astype(F32) - center_ref[...]).astype(BF16)
    out_ref[...] = jnp.dot(x, w_ref[...], preferred_element_type=F32).astype(BF16)


def whiten_own_kernel(x_ref, center_ref, w_ref, add_ref, out_ref):
    x = (x_ref[...].astype(F32) - center_ref[...]).astype(BF16)
    y = jnp.dot(x, w_ref[...], preferred_element_type=F32) + add_ref[...].astype(F32)
    out_ref[...] = y.astype(BF16)


def shift_kernel(parts_ref, bias_ref, white_ref, out_ref):
    total = parts_ref[0].astype(F32)
    for i in range(1, parts_ref.shape[0]):
        total = total + parts_ref[i].astype(F32)
    white = total.astype(BF16)
    white_ref[...] = white
    shifted = (white.astype(F32) - bias_ref[...]).astype(BF16)
    for i in range(out_ref.shape[0]):
        out_ref[i] = shifted


def error_kernel(parts_ref, bias_ref, white_ref, out_ref):
    total = parts_ref[0].astype(F32)
    for i in range(1, parts_ref.shape[0]):
        total = total + parts_ref[i].astype(F32)
    error = (total + bias_ref[...]) - white_ref[...].astype(F32)
    grad = (grad_scale * error).astype(BF16)
    for i in range(out_ref.shape[0]):
        out_ref[i] = grad


def product_pick_kernel(contract, x_ref, w_ref, place_ref, out_ref):
    y = lax.dot_general(
        x_ref[...], w_ref[...], (((1,), (contract,)), ((), ())), preferred_element_type=F32
    )
    out_ref[...] = pick(y, place_ref[...])


def product_join_kernel(contract, x_ref, w_ref, place_ref, own_ref, out_ref):
    y = lax.dot_general(
        x_ref[...], w_ref[...], (((1,), (contract,)), ((), ())), preferred_element_type=F32
    )
    lane = lax.broadcasted_iota(jnp.int32, own_ref.shape, 1)
    both = jnp.where(lane < LANES // 2, own_ref[...], pick(y, place_ref[...])).astype(BF16)
    for i in range(out_ref.shape[0]):
        out_ref[i] = both


def packed_sum(parts_ref):
    total = parts_ref[0].astype(F32)
    for i in range(1, parts_ref.shape[0]):
        total = total + parts_ref[i].astype(F32)
    return total


def spread_codes(m, packed_ref, slot_ref, bias_ref, codes_ref):
    packed = packed_sum(packed_ref)
    for j in range(codes_ref.shape[1] // LANES):
        cols = pl.ds(j * LANES, LANES)
        slot = slot_ref[m, :, cols]
        value = jnp.take_along_axis(packed, jnp.maximum(slot, 0), axis=1) + bias_ref[:, cols]
        codes_ref[:, cols] = jnp.where(slot >= 0, value, 0.0).astype(BF16)


def decode_other_kernel(packed_ref, slot_ref, bias_ref, w_ref, codes_ref, part_ref):
    spread_codes(1, packed_ref, slot_ref, bias_ref, codes_ref)
    y = jnp.dot(codes_ref[...], w_ref[...], preferred_element_type=F32)
    part_ref[...] = y.astype(BF16)


def decode_own_kernel(packed_ref, slot_ref, bias_ref, w_ref, codes_ref, part_ref):
    spread_codes(0, packed_ref, slot_ref, bias_ref, codes_ref)
    part_ref[...] = jnp.dot(codes_ref[...], w_ref[...], preferred_element_type=F32)


def encoder_grad_kernel(tok_ref, packed_ref, slot_ref, x_ref, out_ref, bias_ref, sum_ref, grad_ref):
    step = pl.program_id(0)

    @pl.when(step == 0)
    def _():
        sum_ref[...] = packed_sum(packed_ref)

    packed = sum_ref[...]
    rows = packed.shape[0]
    width = grad_ref.shape[1]
    totals = []
    for j in range(width // LANES):
        cols = pl.ds(j * LANES, LANES)
        total = jnp.zeros((1, LANES), F32)
        for m in range(2):
            slot = slot_ref[m, :, cols]
            value = jnp.take_along_axis(packed, jnp.maximum(slot, 0), axis=1)
            grad = jnp.where(slot >= 0, value, 0.0).astype(BF16)
            grad_ref[m * rows : (m + 1) * rows, cols] = grad
            total = total + jnp.sum(grad.astype(F32), axis=0, keepdims=True)
        totals.append(total)
    out_ref[...] = jnp.dot(
        x_ref[...], grad_ref[...], preferred_element_type=F32
    ).astype(BF16)
    kept = bias_ref.shape[1] // width
    for i in range(kept):

        @pl.when(step == tok_ref[0] * kept + i)
        def _():
            for j, total in enumerate(totals):
                bias_ref[:, i * width + j * LANES : i * width + (j + 1) * LANES] = total


def encoder_grad_call(tok, packed, slot, shifted_t, block=256):
    rows, latents = slot.shape[1:]
    width = shifted_t.shape[0]
    return pl.pallas_call(
        encoder_grad_kernel,
        grid=(latents // block,),
        in_specs=[
            pl.BlockSpec(memory_space=pltpu.SMEM),
            pl.BlockSpec(packed.shape, lambda i: (0, 0, 0)),
            pl.BlockSpec((2, rows, block), lambda i: (0, 0, i)),
            pl.BlockSpec(shifted_t.shape, lambda i: (0, 0)),
        ],
        out_specs=(
            pl.BlockSpec((width, block), lambda i: (0, i)),
            pl.BlockSpec((1, latents // 2), lambda i: (0, 0)),
        ),
        out_shape=(
            jax.ShapeDtypeStruct((width, latents), BF16),
            jax.ShapeDtypeStruct((1, latents // 2), F32),
        ),
        scratch_shapes=[pltpu.VMEM(packed.shape[1:], F32), pltpu.VMEM((2 * rows, block), BF16)],
        compiler_params=PARAMS,
    )(tok, packed, slot, shifted_t)


def swap_cores(x):
    return lax.ppermute(x, "core", [(0, 1), (1, 0)])


def exchange(x, axes):
    return lax.all_to_all(x, axes, 0, 0)


FEATURES = ("section", "tok")
COLUMN = ("yh", "z")


def body(
    residual, center, whiten, decoder_bias, encoder_weight, encoder_bias, decoder_weight, chosen
):
    core = lax.axis_index("core")
    tok = lax.axis_index("tok")
    width = encoder_weight.shape[0]
    latents = encoder_bias.shape[0]
    features = lax.axis_size(FEATURES)
    column = lax.axis_size(COLUMN)
    first = ((lax.axis_index("yh") * 8 + lax.axis_index("z")) * 2 + core) * latents

    own_picks = lax.dynamic_index_in_dim(chosen, core, 0, keepdims=False)
    other_picks = lax.dynamic_index_in_dim(chosen, 1 - core, 0, keepdims=False)
    place = jnp.concatenate([own_picks, other_picks], axis=1).astype(jnp.int32) - first
    rows = place.shape[0]

    out = jnp.broadcast_to(residual, (features,) + residual.shape[1:])
    arrived = exchange(out, ("tok", "section")).reshape(2, rows, -1)
    own_rows = lax.dynamic_index_in_dim(arrived, core, 0, keepdims=False)
    other_rows = lax.dynamic_index_in_dim(arrived, 1 - core, 0, keepdims=False)
    whiten_cols = lax.dynamic_slice_in_dim(whiten, tok * width, width, 1)
    bias_cols = lax.dynamic_slice_in_dim(decoder_bias, tok * width, width, 0)[None]

    rows_bf16 = jax.ShapeDtypeStruct((rows, width), BF16)
    center = center[None]
    white_flops = 2 * rows * width * center.shape[1]
    other_part = call(
        whiten_other_kernel, rows_bf16, (other_rows, center, whiten_cols), white_flops, 2**21
    )
    from_core = swap_cores(other_part)
    own_part = call(
        whiten_own_kernel, rows_bf16, (own_rows, center, whiten_cols, from_core), white_flops, 2**21
    )
    own_part, place_later = lax.optimization_barrier((own_part, place))
    slot = call(
        find_kernel,
        jax.ShapeDtypeStruct((2, rows, latents), jnp.int32),
        (place_later,),
        flops=2 * 64 * 2 * rows * latents,
        moved=8 * rows * latents,
    )
    shares = (column, rows // column, width)
    parts = exchange(own_part.reshape(shares), COLUMN)
    parts, slot = lax.optimization_barrier((parts, slot))
    share_bf16 = jax.ShapeDtypeStruct(shares[1:], BF16)
    shares_bf16 = jax.ShapeDtypeStruct(shares, BF16)
    whitened, out = call(
        shift_kernel, (share_bf16, shares_bf16), (parts, bias_cols), 0, 2**20
    )
    own_shifted = exchange(out, COLUMN).reshape(rows, width)
    other_shifted = swap_cores(own_shifted)

    flops = 2 * rows * width * latents
    moved = 2 * width * latents + 4 * rows * width
    packed_f32 = jax.ShapeDtypeStruct((rows, LANES), F32)
    packed_all = jax.ShapeDtypeStruct((features, rows, LANES), BF16)

    def packed_product(contract, own, other, weight):
        mine = call(
            functools.partial(product_pick_kernel, contract),
            packed_f32,
            (own, weight, place),
            flops,
            moved,
        )
        both = call(
            functools.partial(product_join_kernel, contract),
            packed_all,
            (other, weight, place, mine),
            flops,
            moved,
        )
        return exchange(both, FEATURES)

    encoded = packed_product(0, own_shifted, other_shifted, encoder_weight)

    codes_bf16 = jax.ShapeDtypeStruct((rows, latents), BF16)
    bias_row = encoder_bias[None]
    other_codes, other_part = call(
        decode_other_kernel,
        (codes_bf16, rows_bf16),
        (encoded, slot, bias_row, decoder_weight),
        flops,
        moved,
    )
    from_core = swap_cores(other_part)
    own_codes, own_part = call(
        decode_own_kernel,
        (codes_bf16, jax.ShapeDtypeStruct((rows, width), F32)),
        (encoded, slot, bias_row, decoder_weight),
        flops,
        moved,
    )
    parts = (own_part + from_core.astype(F32)).astype(BF16)
    parts = exchange(parts.reshape(shares), COLUMN)
    out = call(error_kernel, shares_bf16, (parts, bias_cols, whitened), 0, 2**20)
    own_grad = exchange(out, COLUMN).reshape(rows, width)
    other_grad = swap_cores(own_grad)

    code_grad = packed_product(1, own_grad, other_grad, decoder_weight)

    codes = jnp.concatenate([own_codes, other_codes], axis=0)
    out_grad = jnp.concatenate([own_grad, other_grad], axis=0)
    decoder_grad = lax.dot_general(
        codes, out_grad, (((0,), (0,)), ((), ())), preferred_element_type=F32
    ).astype(BF16)

    shifted_t = jnp.concatenate([own_shifted, other_shifted], axis=0).T
    encoder_grad, bias_grad = encoder_grad_call(
        tok.astype(jnp.int32)[None], code_grad, slot, shifted_t
    )
    return encoder_grad, decoder_grad, bias_grad[0]


def solution(mesh):
    fine = Mesh(mesh.devices.reshape(4, 2, 8, 2, 2), ("section", "yh", "z", "core", "tok"))
    lat = ("yh", "z", "core")
    return jax.shard_map(
        body,
        mesh=fine,
        in_specs=(
            P("tok", "section", lat),
            P(lat),
            P(lat, "section"),
            P("section"),
            P(("section", "tok"), lat),
            P(lat),
            P(lat, ("section", "tok")),
            P(),
        ),
        out_specs=(P(("section", "tok"), lat), P(lat, ("section", "tok")), P(lat + ("tok",))),
        check_vma=False,
    )
```

time: 180 us -> 169 us (0.939)
  waiting for transfers between devices: 28.8 us -> 15.9 us
  local copies, waits for them, and re-layouts: 7.42 us -> 15.6 us
  starting transfers between devices: 37.1 us -> 29.1 us
  matrix products: 9.49 us -> 2.62 us
  blocking collectives: 70.7 us -> 75.1 us
  Pallas kernels: 21.8 us -> 26 us
    all_to_all x5 -> x3, waiting for transfers between devices: 27.1 us -> 14.6 us  [exchange(): return lax.all_to_all(x, axes, 0, 0)]
    all_to_all x5 -> x3, starting transfers between devices: 28.4 us -> 20.7 us  [exchange(): return lax.all_to_all(x, axes, 0, 0)]
    dot_general x4 -> x1, matrix products: 9.49 us -> 2.62 us  [body(): lax.dot_general(codes, out_grad, (((0,), (0,)), ((), ())), preferred_elem...]
    pallas_call x0 -> x1, Pallas kernels: none -> 5.72 us  [encoder_grad_call(): pl.pallas_call(encoder_grad_kernel, grid=(latents // block,), in_specs=[p...]
    unnamed x30 -> x40, local copies, waits for them, and re-layouts: 4.54 us -> 9.69 us
    all_to_all x4, blocking collectives: 70.7 us -> 75.1 us  [exchange(): return lax.all_to_all(x, axes, 0, 0)]
    transpose x0 -> x1, other arithmetic: none -> 2.39 us  [body(): shifted_t = jnp.concatenate([own_shifted, other_shifted], axis=0).T]
    ppermute x0 -> x1, local copies, waits for them, and re-layouts: none -> 2.04 us  [swap_cores(): return lax.ppermute(x, 'core', [(0, 1), (1, 0)])]
  transfers between devices with their start and end apart: 9 -> 7, of which waited for: 6 -> 5; matrix products, arithmetic and copies ran while one was open for 3% -> 3% of each run, Pallas kernels for 9% -> 9%
where the time goes in v2:
time: 169 us; the launch traced here: 168 us
  blocking collectives  75.1 us (44%)
  starting transfers between devices  29.1 us (17%)
  Pallas kernels  26 us (15%)
  waiting for transfers between devices  15.9 us (9%)
  local copies, waits for them, and re-layouts  15.6 us (9%)
  other arithmetic  2.64 us (2%)
  matrix products  2.62 us (2%)
    all_to_all x4, blocking collectives, exchange(): return lax.all_to_all(x, axes, 0, 0)  75.1 us
    all_to_all x3, starting transfers between devices, exchange(): return lax.all_to_all(x, axes, 0, 0)  20.7 us
    pallas_call x11, Pallas kernels, call(): pl.pallas_call(kernel, out_shape=out_shape, in_specs=[WHOLE] * len(operan...  20.3 us
    all_to_all x3, waiting for transfers between devices, exchange(): return lax.all_to_all(x, axes, 0, 0)  14.6 us
    unnamed x40, local copies, waits for them, and re-layouts  9.69 us
    ppermute x4, starting transfers between devices, swap_cores(): return lax.ppermute(x, 'core', [(0, 1), (1, 0)])  8.45 us
    pallas_call x1, Pallas kernels, encoder_grad_call(): pl.pallas_call(encoder_grad_kernel, grid=(latents // block,), in_specs=[p...  5.72 us
  transfers between devices with their start and end apart: 7, of which 5 were waited for; matrix products, arithmetic and copies ran while one was open for 3% of the time, Pallas kernels for 9%

profile of v2, /device:TPU:1, one launch (start us, length us, event | category | flops | bytes accessed | tf_op | source)
XLA Modules:
  0.0 167.9 jit_solution(10905658528741937233)
XLA Ops:
  0.7 1.6 broadcast_in_dim.21
  2.2 5.9 %all-to-all-start = ((bf16[8,64,256]{2,1,0:T(8,128)(2,1)}), bf16[8,64,256]{2,1,0:T(8,128)(2,1)S(1)}, u32[]{:S(2)}, u32[]{:S(2)}) async-start(bf16[8,64,256]{2,1,0:T(8,128)(2,1)} %broadcast_in_dim.21), calls=%async_computation | async-start | bytes 524288 | tf_op jit(solution)/shard_map/all_to_all | solution.py:196
  8.2 6.2 %all-to-all-done = bf16[8,64,256]{2,1,0:T(8,128)(2,1)S(1)} async-done(((bf16[8,64,256]{2,1,0:T(8,128)(2,1)}), bf16[8,64,256]{2,1,0:T(8,128)(2,1)S(1)}, u32[]{:S(2)}, u32[]{:S(2)}) %all-to-all-start) | async-done | bytes 262176 | tf_op jit(solution)/shard_map/all_to_all | solution.py:196
  14.7 2.0 %collective-permute-start = (bf16[256,1024]{1,0:T(8,128)(2,1)S(1)}, bf16[256,1024]{1,0:T(8,128)(2,1)S(1)}, u32[]{:S(2)}, u32[]{:S(2)}) collective-permute-start(bf16[256,1024]{1,0:T(8,128)(2,1)S(1)} %shard_map.103), channel_id=1, source_target_pairs={{0,2},{2,0},{1,3},{3,1},{4,6},{6,4},{5,7},{7,5},{8,10},{10,8},{9,1... | collective-permute-start | bytes 1572872 | tf_op jit(solution)/shard_map/ppermute | solution.py:192
  19.4 10.7 %all-to-all-start.1 = ((bf16[16,16,1024]{2,1,0:T(8,128)(2,1)}), bf16[16,16,1024]{2,1,0:T(8,128)(2,1)}, u32[]{:S(2)}, u32[]{:S(2)}) async-start(bf16[16,16,1024]{2,1,0:T(8,128)(2,1)} %bitcast.8), calls=%async_computation.1 | async-start | bytes 1048576 | tf_op jit(solution)/shard_map/all_to_all | solution.py:196
  30.1 11.2 %shard_map.105.slot_ref = s32[2,256,1024]{2,1,0:T(8,128)S(1)} custom-call(s32[256,128]{1,0:T(8,128)S(1)} %add_subtract_fusion.place_ref), custom_call_target="tpu_custom_call" | custom-call | flops 67108864 | bytes 2097152 | tf_op jit(solution)/shard_map/pallas_call | solution.py:20
  41.3 3.9 %all-to-all-done.1.parts_ref = bf16[16,16,1024]{2,1,0:T(8,128)(2,1)} async-done(((bf16[16,16,1024]{2,1,0:T(8,128)(2,1)}), bf16[16,16,1024]{2,1,0:T(8,128)(2,1)}, u32[]{:S(2)}, u32[]{:S(2)}) %all-to-all-start.1) | async-done | bytes 524320 | tf_op jit(solution)/shard_map/all_to_all | solution.py:196
  46.4 21.9 %all_to_all.35 = bf16[16,16,1024]{2,1,0:T(8,128)(2,1)} all-to-all(bf16[16,16,1024]{2,1,0:T(8,128)(2,1)S(1)} %get-tuple-element.18), channel_id=1, replica_groups=mesh['section'=4,'yh'=2,'z'=8,'core'=2,'tok'=2] {'yh','z'}, dimensions={0} | all-to-all | bytes 1048576 | tf_op jit(solution)/shard_map/all_to_all | solution.py:196
  68.3 2.0 %copy.18 = bf16[256,1024]{0,1:T(8,128)(2,1)} copy(bf16[256,1024]{1,0:T(8,128)(2,1)} %bitcast.19) | data formatting | bytes 1048576 | tf_op jit(solution)/shard_map/reshape | solution.py:252
  70.3 2.8 %collective-permute-start.1 = (bf16[256,1024]{0,1:T(8,128)(2,1)}, bf16[256,1024]{0,1:T(8,128)(2,1)}, u32[]{:S(2)}, u32[]{:S(2)}) collective-permute-start(bf16[256,1024]{0,1:T(8,128)(2,1)} %copy.18), channel_id=1, source_target_pairs={{0,2},{2,0},{1,3},{3,1},{4,6},{6,4},{5,7},{7,5},{8,10},{10,8},{9,1... | collective-permute-start | bytes 1572872 | tf_op jit(solution)/shard_map/ppermute | solution.py:192
  73.1 1.6 copy-done.2
  76.7 2.0 %copy.19.x_ref = bf16[256,1024]{1,0:T(8,128)(2,1)} copy(bf16[256,1024]{0,1:T(8,128)(2,1)} %collective-permute-done.1) | data formatting | bytes 1048576 | tf_op jit(solution)/shard_map/ppermute | solution.py:192
  78.7 1.6 copy-done.3
  82.3 12.1 %all_to_all.36.packed_ref = bf16[8,256,128]{2,1,0:T(8,128)(2,1)S(1)} all-to-all(bf16[8,256,128]{2,1,0:T(8,128)(2,1)S(1)} %shard_map.108), channel_id=1, replica_groups=mesh['section'=4,'yh'=2,'z'=8,'core'=2,'tok'=2] {'section','tok'}, dimensions={0} | all-to-all | bytes 1048576 | tf_op jit(solution)/shard_map/all_to_all | solution.py:196
  94.3 1.4 shard_map.110
  97.3 1.4 shard_map.109
  99.0 19.4 %all_to_all.37.parts_ref = bf16[16,16,1024]{2,1,0:T(8,128)(2,1)S(1)} all-to-all(bf16[16,16,1024]{2,1,0:T(8,128)(2,1)S(1)} %bitcast.30), channel_id=1, replica_groups=mesh['section'=4,'yh'=2,'z'=8,'core'=2,'tok'=2] {'yh','z'}, dimensions={0} | all-to-all | bytes 1048576 | tf_op jit(solution)/shard_map/all_to_all | solution.py:196
  118.5 21.7 %all_to_all.38 = bf16[16,16,1024]{2,1,0:T(8,128)(2,1)S(1)} all-to-all(bf16[16,16,1024]{2,1,0:T(8,128)(2,1)S(1)} %shard_map.111), channel_id=1, replica_groups=mesh['section'=4,'yh'=2,'z'=8,'core'=2,'tok'=2] {'yh','z'}, dimensions={0} | all-to-all | bytes 1048576 | tf_op jit(solution)/shard_map/all_to_all | solution.py:196
  140.3 2.8 %collective-permute-start.3 = (bf16[256,1024]{1,0:T(8,128)(2,1)S(1)}, bf16[256,1024]{1,0:T(8,128)(2,1)S(1)}, u32[]{:S(2)}, u32[]{:S(2)}) collective-permute-start(bf16[256,1024]{1,0:T(8,128)(2,1)S(1)} %bitcast.21), channel_id=1, source_target_pairs={{0,2},{2,0},{1,3},{3,1},{4,6},{6,4},{5,7},{7,5},{8,10},{10,8},{9,1... | collective-permute-start | bytes 1572872 | tf_op jit(solution)/shard_map/ppermute | solution.py:192
  147.4 4.1 %all-to-all-start.6 = ((bf16[8,256,128]{2,1,0:T(8,128)(2,1)}), bf16[8,256,128]{2,1,0:T(8,128)(2,1)}, u32[]{:S(2)}, u32[]{:S(2)}) async-start(bf16[8,256,128]{2,1,0:T(8,128)(2,1)} %copy-done.8), calls=%async_computation.6 | async-start | bytes 1048576 | tf_op jit(solution)/shard_map/all_to_all | solution.py:196
  151.6 2.4 %maximum_bitcast_fusion.x_ref = bf16[1024,512]{1,0:T(8,128)(2,1)} fusion(bf16[256,1024]{0,1:T(8,128)(2,1)} %collective-permute-done.1, bf16[256,1024]{0,1:T(8,128)(2,1)} %copy.18), kind=kLoop, calls=%fused_computation.1 | loop fusion | flops 2097152 | bytes 2097152 | tf_op jit(solution)/shard_map/transpose | solution.py:310
  154.0 2.6 %convolution_convert_fusion = bf16[1024,1024]{1,0:T(8,128)(2,1)} fusion(bf16[256,1024]{1,0:T(8,128)(2,1)S(1)} %copy-done.15, bf16[256,1024]{1,0:T(8,128)(2,1)S(1)} %copy-done.17, bf16[256,1024]{1,0:T(8,128)(2,1)S(1)} %copy-done.11, bf16[256,1024]{1,0:T(8,128)(2,1)S(1)} %bitcast.23), kind=kOutput, calls=%fused_computation | convolution fusion | flops 1078984704 | bytes 4194304 | tf_op jit(solution)/shard_map/dot_general | solution.py:306
  156.6 4.4 %all-to-all-done.6.packed_ref = bf16[8,256,128]{2,1,0:T(8,128)(2,1)} async-done(((bf16[8,256,128]{2,1,0:T(8,128)(2,1)}), bf16[8,256,128]{2,1,0:T(8,128)(2,1)}, u32[]{:S(2)}, u32[]{:S(2)}) %all-to-all-start.6) | async-done | bytes 524320 | tf_op jit(solution)/shard_map/all_to_all | solution.py:196
  162.2 5.7 %shard_map.114 = (bf16[1024,1024]{1,0:T(8,128)(2,1)}, f32[1,512]{1,0:T(1,128)}) custom-call(s32[1]{0:T(128)} %bitcast.tok_ref, bf16[8,256,128]{2,1,0:T(8,128)(2,1)} %all-to-all-done.6.packed_ref, s32[2,256,1024]{2,1,0:T(8,128)S(1)} %shard_map.105.slot_ref, bf16[1024,512]{1,0:T(8,128)(2,1)S(1)} %copy-done.5), custom_call_target="tpu_custom_call" | custom-call | tf_op jit(solution)/shard_map/pallas_call | solution.py:169
  (59 shorter events, 15.5 us)
Async XLA Ops:
  0.6 7.5 %copy-start = (bf16[256,2048]{1,0:T(8,128)(2,1)S(1)}, bf16[256,2048]{1,0:T(8,128)(2,1)}, u32[]{:S(2)}) copy-start(bf16[256,2048]{1,0:T(8,128)(2,1)} %param.10) | copy-start | bytes 3145732
  0.6 13.8 %copy-start.13 = (f32[256]{0:T(256)S(1)}, f32[256]{0:T(256)}, u32[]{:S(2)}) copy-start(f32[256]{0:T(256)} %param.9) | copy-start | bytes 3076
  0.7 16.1 %copy-start.18 = (s32[2,256,64]{1,2,0:T(8,128)S(1)}, s32[2,256,64]{1,2,0:T(8,128)}, u32[]{:S(2)}) copy-start(s32[2,256,64]{1,2,0:T(8,128)} %param.15) | copy-start | bytes 393220
  2.2 12.2 %all-to-all-start = ((bf16[8,64,256]{2,1,0:T(8,128)(2,1)}), bf16[8,64,256]{2,1,0:T(8,128)(2,1)S(1)}, u32[]{:S(2)}, u32[]{:S(2)}) async-start(bf16[8,64,256]{2,1,0:T(8,128)(2,1)} %broadcast_in_dim.21), calls=%async_computation | async-start | bytes 524288 | tf_op jit(solution)/shard_map/all_to_all | solution.py:196
  14.7 15.4 %copy-start.19 = (f32[2048]{0:T(1024)S(1)}, f32[2048]{0:T(1024)}, u32[]{:S(2)}) copy-start(f32[2048]{0:T(1024)} %param.11) | copy-start | bytes 24580
  14.7 3.6 %collective-permute-start = (bf16[256,1024]{1,0:T(8,128)(2,1)S(1)}, bf16[256,1024]{1,0:T(8,128)(2,1)S(1)}, u32[]{:S(2)}, u32[]{:S(2)}) collective-permute-start(bf16[256,1024]{1,0:T(8,128)(2,1)S(1)} %shard_map.103), channel_id=1, source_target_pairs={{0,2},{2,0},{1,3},{3,1},{4,6},{6,4},{5,7},{7,5},{8,10},{10,8},{9,1... | collective-permute-start | bytes 1572872 | tf_op jit(solution)/shard_map/ppermute | solution.py:192
  19.4 25.8 %all-to-all-start.1 = ((bf16[16,16,1024]{2,1,0:T(8,128)(2,1)}), bf16[16,16,1024]{2,1,0:T(8,128)(2,1)}, u32[]{:S(2)}, u32[]{:S(2)}) async-start(bf16[16,16,1024]{2,1,0:T(8,128)(2,1)} %bitcast.8), calls=%async_computation.1 | async-start | bytes 1048576 | tf_op jit(solution)/shard_map/all_to_all | solution.py:196
  70.3 6.4 %collective-permute-start.1 = (bf16[256,1024]{0,1:T(8,128)(2,1)}, bf16[256,1024]{0,1:T(8,128)(2,1)}, u32[]{:S(2)}, u32[]{:S(2)}) collective-permute-start(bf16[256,1024]{0,1:T(8,128)(2,1)} %copy.18), channel_id=1, source_target_pairs={{0,2},{2,0},{1,3},{3,1},{4,6},{6,4},{5,7},{7,5},{8,10},{10,8},{9,1... | collective-permute-start | bytes 1572872 | tf_op jit(solution)/shard_map/ppermute | solution.py:192
  73.1 1.6 copy-start.2
  74.7 1.0 copy-start.4
  78.7 1.6 copy-start.3
  80.3 1.0 copy-start.9
  81.4 12.9 %copy-start.1 = (bf16[1024,1024]{1,0:T(8,128)(2,1)S(1)}, bf16[1024,1024]{1,0:T(8,128)(2,1)}, u32[]{:S(2)}) copy-start(bf16[1024,1024]{1,0:T(8,128)(2,1)} %w_ref.11) | copy-start | bytes 6291460
  81.4 12.9 %copy-start.12 = (f32[1024]{0:T(1024)S(1)}, f32[1024]{0:T(1024)}, u32[]{:S(2)}) copy-start(f32[1024]{0:T(1024)} %param.13) | copy-start | bytes 12292
  96.5 2.3 %collective-permute-start.2 = (bf16[256,1024]{1,0:T(8,128)(2,1)S(1)}, bf16[256,1024]{1,0:T(8,128)(2,1)S(1)}, u32[]{:S(2)}, u32[]{:S(2)}) collective-permute-start(bf16[256,1024]{1,0:T(8,128)(2,1)S(1)} %get-tuple-element.21), channel_id=1, source_target_pairs={{0,2},{2,0},{1,3},{3,1},{4,6},{6,4},{5,7},{7,5},{8,10},{10,8},{9,1... | collective-permute-start | bytes 1572872 | tf_op jit(solution)/shard_map/ppermute | solution.py:192
  98.7 19.9 %copy-start.16 = (bf16[256,1024]{1,0:T(8,128)(2,1)}, bf16[256,1024]{1,0:T(8,128)(2,1)S(1)}, u32[]{:S(2)}) copy-start(bf16[256,1024]{1,0:T(8,128)(2,1)S(1)} %get-tuple-element.24) | copy-start | bytes 1572868
  140.3 4.6 %collective-permute-start.3 = (bf16[256,1024]{1,0:T(8,128)(2,1)S(1)}, bf16[256,1024]{1,0:T(8,128)(2,1)S(1)}, u32[]{:S(2)}, u32[]{:S(2)}) collective-permute-start(bf16[256,1024]{1,0:T(8,128)(2,1)S(1)} %bitcast.21), channel_id=1, source_target_pairs={{0,2},{2,0},{1,3},{3,1},{4,6},{6,4},{5,7},{7,5},{8,10},{10,8},{9,1... | collective-permute-start | bytes 1572872 | tf_op jit(solution)/shard_map/ppermute | solution.py:192
  145.8 0.8 copy-start.8
  147.4 13.6 %all-to-all-start.6 = ((bf16[8,256,128]{2,1,0:T(8,128)(2,1)}), bf16[8,256,128]{2,1,0:T(8,128)(2,1)}, u32[]{:S(2)}, u32[]{:S(2)}) async-start(bf16[8,256,128]{2,1,0:T(8,128)(2,1)} %copy-done.8), calls=%async_computation.6 | async-start | bytes 1048576 | tf_op jit(solution)/shard_map/all_to_all | solution.py:196
  151.5 2.4 %copy-start.7 = (bf16[16,16,1024]{2,1,0:T(8,128)(2,1)S(1)}, bf16[16,16,1024]{2,1,0:T(8,128)(2,1)}, u32[]{:S(2)}) copy-start(bf16[16,16,1024]{2,1,0:T(8,128)(2,1)} %copy-done.6) | copy-start | bytes 1572868
  151.5 2.4 %copy-start.11 = (bf16[256,1024]{1,0:T(8,128)(2,1)S(1)}, bf16[256,1024]{1,0:T(8,128)(2,1)}, u32[]{:S(2)}) copy-start(bf16[256,1024]{1,0:T(8,128)(2,1)} %copy-done.10) | copy-start | bytes 1572868
  151.5 2.4 %copy-start.15 = (bf16[256,1024]{1,0:T(8,128)(2,1)S(1)}, bf16[256,1024]{1,0:T(8,128)(2,1)}, u32[]{:S(2)}) copy-start(bf16[256,1024]{1,0:T(8,128)(2,1)} %copy-done.14) | copy-start | bytes 1572868
  151.6 2.4 %copy-start.17 = (bf16[256,1024]{1,0:T(8,128)(2,1)S(1)}, bf16[256,1024]{1,0:T(8,128)(2,1)}, u32[]{:S(2)}) copy-start(bf16[256,1024]{1,0:T(8,128)(2,1)} %copy-done.16) | copy-start | bytes 1572868
  161.0 1.2 copy-start.5
  (3 other events, 2.4 us)

commit v3 on v0

v3 whole, which is shorter than its diff:
```python
import functools

import jax
import jax.numpy as jnp
from jax import lax
from jax.experimental import pallas as pl
from jax.experimental.pallas import tpu as pltpu
from jax.sharding import Mesh
from jax.sharding import PartitionSpec as P

grad_scale = 0.125
LANES = 128
F32 = jnp.float32
BF16 = jnp.bfloat16
HERE = pl.BlockSpec(memory_space=pltpu.VMEM)
SCALARS = pl.BlockSpec(memory_space=pltpu.SMEM)
ANY = pl.BlockSpec(memory_space=pl.ANY)
HBM = pl.BlockSpec(memory_space=pltpu.HBM)
MIB = 1024 * 1024
SMALL, MIDDLE, MOST = 12, 24, 62
COPIES = pltpu.SemaphoreType.DMA
ROW_BLOCKS = 4
FEATURES = ("section", "tok")
COLUMN = ("yh", "z")
CORE, TOK, FIRST, FIRST2 = range(4)


def spec(*shape, dtype=BF16):
    return jax.ShapeDtypeStruct(shape, dtype)


def call(kernel, ins, outs, operands, scratch=(), flops=0, moved=2**20, vmem=60):
    return pl.pallas_call(
        kernel,
        in_specs=list(ins),
        out_specs=tuple(place for place, _ in outs),
        out_shape=tuple(shape for _, shape in outs),
        scratch_shapes=list(scratch),
        compiler_params=pltpu.CompilerParams(vmem_limit_bytes=vmem * MIB),
        cost_estimate=pl.CostEstimate(flops=flops, bytes_accessed=moved, transcendentals=0),
    )(*operands)


def start(source, target, sem):
    copy = pltpu.make_async_copy(source, target, sem)
    copy.start()
    return copy


def place_kernel(latents, at_ref, chosen_ref, packed_ref, wide_ref):
    picked = chosen_ref[at_ref[CORE]]
    own, other = picked - at_ref[FIRST], picked - at_ref[FIRST2]
    wide_ref[...] = jnp.concatenate([own, other], axis=1)
    place = jnp.where((other >= 0) & (other < latents), other + latents, -1)
    place = jnp.where((own >= 0) & (own < latents), own, place)
    half = place.shape[0] // 2
    packed_ref[...] = jnp.concatenate([place[:half], place[half:]], axis=1)


def find_kernel(wide_ref, slot_ref, slot2_ref, found):
    rows, width = slot_ref.shape
    half, picks = rows // 2, LANES // 2
    column = lax.broadcasted_iota(jnp.int32, (8, width), 1)

    def step(i, carry):
        own = pl.ds(pl.multiple_of(i * 8, 8), 8)
        place = wide_ref[own, :]
        for n in range(2):
            slot = jnp.full((8, width), -1, jnp.int32)
            for k in range(picks):
                at = n * picks + k
                slot = jnp.where(place[:, at : at + 1] == column, k, slot)
            found[n, own, :] = slot
        return carry

    def pack(i, carry):
        own = pl.ds(pl.multiple_of(i * 16, 16), 16)
        lane = jnp.where(i * 16 >= half, picks, 0)
        for n, out in enumerate((slot_ref, slot2_ref)):
            slot = found[n, own, :]
            out[own, :] = jnp.where(slot >= 0, slot + lane, slot).astype(F32).astype(BF16)
        return carry

    lax.fori_loop(0, rows // 8, step, 0)
    lax.fori_loop(0, rows // 16, pack, 0)


def pick(low, high, place, chunk, j, y):
    half = place.shape[0]
    here = chunk == j
    low = jnp.where(here, jnp.take_along_axis(y[:half], place, axis=1), low)
    high = jnp.where(here, jnp.take_along_axis(y[half:], place, axis=1), high)
    return low, high


def spread(packed, slot, cols):
    lane = slot[:, cols].astype(F32).astype(jnp.int32)
    half = packed.shape[0]
    value = jnp.concatenate(
        [
            jnp.take_along_axis(packed, jnp.maximum(lane[:half], 0), axis=1),
            jnp.take_along_axis(packed, jnp.maximum(lane[half:], 0), axis=1),
        ],
        axis=0,
    )
    return value, lane >= 0


def sum_of(parts_ref):
    total = parts_ref[0].astype(F32)
    for i in range(1, parts_ref.shape[0]):
        total = total + parts_ref[i].astype(F32)
    return total


def whiten_other_kernel(x_ref, w_ref, out_ref):
    out_ref[...] = jnp.dot(x_ref[...], w_ref[...], preferred_element_type=F32).astype(BF16)


def whiten_own_kernel(x_ref, w_ref, add_ref, out_ref, ready, sems):
    y = jnp.dot(x_ref[...], w_ref[...], preferred_element_type=F32) + add_ref[...].astype(F32)
    ready[...] = y.astype(BF16)
    start(ready, out_ref, sems.at[0]).wait()


def own_bias(at_ref, bias_ref, width):
    return bias_ref[:, pl.ds(pl.multiple_of(at_ref[TOK] * width, width), width)]


def shift_kernel(at_ref, parts_ref, bias_ref, white_ref, out_ref):
    white = sum_of(parts_ref).astype(BF16)
    white_ref[...] = white
    shifted = (white.astype(F32) - own_bias(at_ref, bias_ref, white.shape[1])).astype(BF16)
    for i in range(out_ref.shape[0]):
        out_ref[i] = shifted


def error_kernel(at_ref, parts_ref, bias_ref, white_ref, out_ref):
    rebuilt = sum_of(parts_ref) + own_bias(at_ref, bias_ref, white_ref.shape[1])
    grad = (grad_scale * (rebuilt - white_ref[...].astype(F32))).astype(BF16)
    for i in range(out_ref.shape[0]):
        out_ref[i] = grad


def product_kernel(contract, x_ref, place_ref, w_ref, w2_ref, out_ref, held, sems):
    copies = [start(w_ref, held.at[0], sems.at[0]), start(w2_ref, held.at[1], sems.at[1])]
    place = place_ref[...]
    lane, chunk = place & (LANES - 1), place >> 7
    low = high = jnp.zeros(place.shape, F32)
    for n in range(2):
        copies[n].wait()
        y = lax.dot_general(
            x_ref[...], held[n], (((1,), (contract,)), ((), ())), preferred_element_type=F32
        )
        blocks = y.shape[1] // LANES
        for j in range(blocks):
            part = y[:, j * LANES : (j + 1) * LANES]
            low, high = pick(low, high, lane, chunk, n * blocks + j, part)
    column = lax.broadcasted_iota(jnp.int32, place.shape, 1)
    packed = jnp.where(column < LANES // 2, low, high).astype(BF16)
    for i in range(out_ref.shape[0]):
        out_ref[i] = packed


def spread_codes(packed, slot, bias_ref, codes_ref):
    for j in range(codes_ref.shape[1] // LANES):
        cols = pl.ds(j * LANES, LANES)
        value, there = spread(packed, slot, cols)
        codes_ref[:, cols] = jnp.where(there, value + bias_ref[:, cols], 0.0).astype(BF16)


def decode_kernel(
    parts_ref,
    slot_ref,
    slot2_ref,
    bias_ref,
    bias2_ref,
    w_ref,
    w2_ref,
    packed_ref,
    out_ref,
    codes,
    slots,
    held,
    sems,
):
    found = [start(slot_ref, slots.at[0], sems.at[2]), start(slot2_ref, slots.at[1], sems.at[3])]
    copies = [start(w_ref, held.at[0], sems.at[0]), start(w2_ref, held.at[1], sems.at[1])]
    packed = sum_of(parts_ref)
    packed_ref[...] = packed
    for n, bias in enumerate((bias_ref, bias2_ref)):
        found[n].wait()
        spread_codes(packed, slots.at[n], bias, codes.at[n])
    for copy in copies:
        copy.wait()
    y = jnp.dot(codes[0], held[0], preferred_element_type=F32)
    y = y + jnp.dot(codes[1], held[1], preferred_element_type=F32)
    out_ref[...] = y.astype(BF16)


ROWS_BY_ROWS = (((0,), (0,)), ((), ()))


def codes_kernel(packed_ref, packed2_ref, slot_ref, slot2_ref, bias_ref, out_ref, out2_ref):
    spread_codes(packed_ref[...], slot_ref, bias_ref, out_ref)
    spread_codes(packed2_ref[...], slot2_ref, bias_ref, out2_ref)


def decoder_grad_kernel(codes_ref, codes2_ref, grad_ref, grad2_ref, out_ref):
    y = lax.dot_general(codes_ref[...], grad_ref[...], ROWS_BY_ROWS, preferred_element_type=F32)
    y = y + lax.dot_general(
        codes2_ref[...], grad2_ref[...], ROWS_BY_ROWS, preferred_element_type=F32
    )
    out_ref[...] = y.astype(BF16)


def spread_grad(parts_ref, slot_ref, grad):
    packed = sum_of(parts_ref)
    for j in range(grad.shape[1] // LANES):
        cols = pl.ds(j * LANES, LANES)
        value, there = spread(packed, slot_ref, cols)
        grad[:, cols] = jnp.where(there, value, 0.0).astype(BF16)


def row_sum(at_ref, grad, kept):
    ones = jnp.ones((16, grad.shape[0]), BF16)
    cols = pl.ds(pl.multiple_of(at_ref[TOK] * kept, kept), kept)
    return jnp.dot(ones, grad[:, cols], preferred_element_type=F32)[:1]


def first_grad_kernel(at_ref, parts_ref, slot_ref, x_ref, out_ref, bias_ref, grad):
    spread_grad(parts_ref, slot_ref, grad)
    bias_ref[...] = row_sum(at_ref, grad, bias_ref.shape[1])
    out_ref[...] = lax.dot_general(
        x_ref[...], grad[...], ROWS_BY_ROWS, preferred_element_type=F32
    )


def second_grad_kernel(
    at_ref, parts_ref, slot_ref, x_ref, first_ref, first_bias_ref, out_ref, bias_ref, grad, made, sems
):
    spread_grad(parts_ref, slot_ref, grad)
    bias_ref[...] = first_bias_ref[...] + row_sum(at_ref, grad, bias_ref.shape[1])
    height = made.shape[0] // ROW_BLOCKS
    copies = []
    for b in range(ROW_BLOCKS):
        own = pl.ds(b * height, height)
        y = lax.dot_general(x_ref[:, own], grad[...], ROWS_BY_ROWS, preferred_element_type=F32)
        made[own, :] = (y + first_ref[own, :]).astype(BF16)
        copies.append(start(made.at[own], out_ref.at[own], sems.at[b]))
    for copy in copies:
        copy.wait()


def swap(x):
    return lax.ppermute(x, "core", [(0, 1), (1, 0)])


def exchange(x, axes):
    return lax.all_to_all(x, axes, 0, 0)


def body(
    residual, center, whiten, decoder_bias, encoder_weight, encoder_bias, decoder_weight, chosen
):
    core = lax.axis_index("core")
    width = encoder_weight.shape[0]
    latents = encoder_bias.shape[0]
    rows, picks = chosen.shape[1:]
    inputs = center.shape[0]
    receivers = lax.axis_size(FEATURES)
    column = lax.axis_size(COLUMN)
    chip = (lax.axis_index("yh") * lax.axis_size("z") + lax.axis_index("z")) * 2
    at = jnp.stack(
        [core, lax.axis_index("tok"), (chip + core) * latents, (chip + 1 - core) * latents]
    ).astype(jnp.int32)

    centered = (residual[0].astype(F32) - center).astype(BF16)
    out = jnp.broadcast_to(centered[None], (receivers,) + centered.shape)
    arrived = exchange(out, ("tok", "section")).reshape(2, rows, inputs)
    own_rows = lax.dynamic_index_in_dim(arrived, core, 0, keepdims=False)
    other_rows = lax.dynamic_index_in_dim(arrived, 1 - core, 0, keepdims=False)
    whiten_cols = lax.dynamic_slice_in_dim(whiten, at[TOK] * width, width, 1)
    flops = 2 * rows * width * inputs
    (part,) = call(
        whiten_other_kernel,
        (HERE, HERE),
        [(HERE, spec(rows, width))],
        (other_rows, whiten_cols),
        (),
        flops,
        vmem=SMALL,
    )
    (part,) = call(
        whiten_own_kernel,
        (HERE, HERE, HERE),
        [(HBM, spec(rows, width))],
        (own_rows, whiten_cols, swap(part)),
        [pltpu.VMEM((rows, width), BF16), COPIES((1,))],
        flops,
        vmem=SMALL,
    )
    shares = (column, rows // column, width)
    share, all_shares = spec(*shares[1:]), spec(*shares)
    bias_row, decoder_bias = encoder_bias[None], decoder_bias[None]

    part, listed, encoder_weight, decoder_weight, bias_row = lax.optimization_barrier(
        (part, chosen, encoder_weight, decoder_weight, bias_row)
    )
    place, wide = call(
        functools.partial(place_kernel, latents),
        (SCALARS, HERE),
        [
            (HERE, spec(rows // 2, LANES, dtype=jnp.int32)),
            (HERE, spec(rows, LANES, dtype=jnp.int32)),
        ],
        (at, listed),
        vmem=SMALL,
    )
    slot, slot2 = call(
        find_kernel,
        (HERE,),
        [(HERE, spec(rows, latents)), (HERE, spec(rows, latents))],
        (wide,),
        [pltpu.VMEM((2, rows, latents), jnp.int32)],
        4 * picks * rows * latents,
    )
    encoder_weight2, decoder_weight2 = swap(encoder_weight), swap(decoder_weight)
    bias_row2 = swap(bias_row)
    parts, slot, slot2, place, encoder_weight2, decoder_weight2, bias_row2 = lax.optimization_barrier(
        (
            exchange(part.reshape(shares), COLUMN),
            slot,
            slot2,
            place,
            encoder_weight2,
            decoder_weight2,
            bias_row2,
        )
    )
    whitened, out = call(
        shift_kernel,
        (SCALARS, HERE, HERE),
        [(HERE, share), (HERE, all_shares)],
        (at, parts, decoder_bias),
        vmem=SMALL,
    )
    shifted = exchange(out, COLUMN).reshape(rows, width)

    flops = 4 * rows * width * latents
    moved = 4 * width * latents
    weights_held = [pltpu.VMEM((2, width, latents), BF16), COPIES((2,))]

    def chosen_product(contract, x, weight, weight2):
        (packed,) = call(
            functools.partial(product_kernel, contract),
            (HERE, HERE, ANY, ANY),
            [(HERE, spec(receivers, rows // 2, LANES))],
            (x, place, weight, weight2),
            weights_held,
            flops,
            moved,
            MOST,
        )
        return packed

    encoded = chosen_product(0, shifted, encoder_weight, encoder_weight2)
    encoded, shifted = lax.optimization_barrier((encoded, shifted))
    shifted2, other_slot = swap(shifted), swap(slot2)
    encoded = exchange(encoded, FEATURES)
    packed, part = call(
        decode_kernel,
        (HERE, ANY, ANY, HERE, HERE, ANY, ANY),
        [(HERE, spec(rows // 2, LANES, dtype=F32)), (HERE, spec(rows, width))],
        (encoded, slot, slot2, bias_row, bias_row2, decoder_weight, decoder_weight2),
        [
            pltpu.VMEM((2, rows, latents), BF16),
            pltpu.VMEM((2, rows, latents), BF16),
            pltpu.VMEM((2, width, latents), BF16),
            COPIES((4,)),
        ],
        flops,
        moved,
        MOST,
    )
    part, packed = lax.optimization_barrier((part, packed))
    codes, codes2 = call(
        codes_kernel,
        (HERE,) * 5,
        [(HERE, spec(rows, latents)), (HERE, spec(rows, latents))],
        (packed, swap(packed), slot, other_slot, bias_row),
    )
    parts, codes, codes2, shifted2, other_slot = lax.optimization_barrier(
        (exchange(part.reshape(shares), COLUMN), codes, codes2, shifted2, other_slot)
    )
    (out,) = call(
        error_kernel,
        (SCALARS, HERE, HERE, HERE),
        [(HERE, all_shares)],
        (at, parts, decoder_bias, whitened),
        vmem=SMALL,
    )
    grad = exchange(out, COLUMN).reshape(rows, width)

    packed = chosen_product(1, grad, decoder_weight, decoder_weight2)
    packed, grad = lax.optimization_barrier((packed, grad))
    (decoder_grad,) = call(
        decoder_grad_kernel,
        (HERE,) * 4,
        [(HERE, spec(latents, width))],
        (codes, codes2, grad, swap(grad)),
        (),
        flops,
        moved,
    )
    code_grad, decoder_grad = lax.optimization_barrier(
        (exchange(packed, FEATURES), decoder_grad)
    )
    code_grad2 = swap(code_grad)
    bias_half = spec(1, latents // 2, dtype=F32)
    first_grad, first_bias = call(
        first_grad_kernel,
        (SCALARS, HERE, HERE, HERE),
        [(HERE, spec(width, latents, dtype=F32)), (HERE, bias_half)],
        (at, code_grad, slot, shifted),
        [pltpu.VMEM((rows, latents), BF16)],
        flops,
        moved,
        MIDDLE,
    )
    encoder_grad, bias_grad = call(
        second_grad_kernel,
        (SCALARS, HERE, HERE, HERE, HERE, HERE),
        [(ANY, spec(width, latents)), (HERE, bias_half)],
        (at, code_grad2, other_slot, shifted2, first_grad, first_bias),
        [
            pltpu.VMEM((rows, latents), BF16),
            pltpu.VMEM((width, latents), BF16),
            COPIES((ROW_BLOCKS,)),
        ],
        flops,
        moved,
        MIDDLE,
    )
    return encoder_grad, decoder_grad, bias_grad[0]


def solution(mesh):
    fine = Mesh(mesh.devices.reshape(4, 2, 8, 2, 2), ("section", "yh", "z", "core", "tok"))
    lat = ("yh", "z", "core")
    return jax.shard_map(
        body,
        mesh=fine,
        in_specs=(
            P("tok", "section", lat),
            P(lat),
            P(lat, "section"),
            P("section"),
            P(("section", "tok"), lat),
            P(lat),
            P(lat, ("section", "tok")),
            P(),
        ),
        out_specs=(P(("section", "tok"), lat), P(lat, ("section", "tok")), P(lat + ("tok",))),
        check_vma=False,
    )
```

time: 777 us -> 162 us (0.21)
  waiting for transfers between devices: 491 us -> 15.6 us
  blocking collectives: 169 us -> 55.4 us
  local copies, waits for them, and re-layouts: 62.8 us -> 5.01 us
  Pallas kernels: 0 us -> 46.4 us
  starting transfers between devices: 0.32 us -> 36.8 us
  matrix products: 26 us -> 0 us
  between operations: 14.9 us -> 1.05 us
  other arithmetic: 13 us -> 0.93 us
    reduce_scatter x3 -> x0, waiting for transfers between devices: 316 us -> none  [the longest x1 115 us: body(): lax.psum_scatter(jnp.dot(latent_codes, decoder_full, preferred_element_ty...]
    psum x1 -> x0, blocking collectives: 154 us -> none  [body(): whitened = lax.psum(white_partial, 'lat').astype(jnp.bfloat16)]
    all_gather x3 -> x0, waiting for transfers between devices: 133 us -> none  [the longest x1 82.7 us: body(): out_grad = lax.all_gather(own_grad, 'lat', axis=0, tiled=True)]
    unnamed x22 -> x30, local copies, waits for them, and re-layouts: 62.7 us -> 4.11 us
    all_to_all x0 -> x3, blocking collectives: none -> 55.4 us  [exchange(): return lax.all_to_all(x, axes, 0, 0)]
    pallas_call x0 -> x13, Pallas kernels: none -> 46.4 us  [call(): pl.pallas_call(kernel, in_specs=list(ins), out_specs=tuple((place for pla...]
    psum x2 -> x0, waiting for transfers between devices: 40.1 us -> none  [the longest x1 40.1 us: body(): code_grad = lax.psum(code_partial, 'section')]
    all_to_all x0 -> x4, starting transfers between devices: none -> 26.2 us  [exchange(): return lax.all_to_all(x, axes, 0, 0)]
  transfers between devices with their start and end apart: 8 -> 13, of which waited for: 6 -> 6; matrix products, arithmetic and copies ran while one was open for 10% -> 0% of each run, Pallas kernels for 0% -> 15%
where the time goes in v3:
time: 162 us; the launch traced here: 161 us
  blocking collectives  55.4 us (34%)
  Pallas kernels  46.4 us (29%)
  starting transfers between devices  36.8 us (23%)
  waiting for transfers between devices  15.6 us (10%)
  local copies, waits for them, and re-layouts  5.01 us (3%)
    all_to_all x3, blocking collectives, exchange(): return lax.all_to_all(x, axes, 0, 0)  55.4 us
    pallas_call x13, Pallas kernels, call(): pl.pallas_call(kernel, in_specs=list(ins), out_specs=tuple((place for pla...  46.4 us
    all_to_all x4, starting transfers between devices, exchange(): return lax.all_to_all(x, axes, 0, 0)  26.2 us
    all_to_all x4, waiting for transfers between devices, exchange(): return lax.all_to_all(x, axes, 0, 0)  12.6 us
    ppermute x9, starting transfers between devices, swap(): return lax.ppermute(x, 'core', [(0, 1), (1, 0)])  10.6 us
    unnamed x30, local copies, waits for them, and re-layouts  4.11 us
  transfers between devices with their start and end apart: 13, of which 6 were waited for; matrix products, arithmetic and copies ran while one was open for 0% of the time, Pallas kernels for 15%

profile of v3, /device:TPU:1, one launch (start us, length us, event | category | flops | bytes accessed | tf_op | source)
XLA Modules:
  0.0 161.2 jit_solution(8299722625778309514)
XLA Ops:
  2.2 5.9 %all-to-all-start = ((bf16[8,64,256]{2,1,0:T(8,128)(2,1)}), bf16[8,64,256]{2,1,0:T(8,128)(2,1)S(1)}, u32[]{:S(2)}, u32[]{:S(2)}) async-start(bf16[8,64,256]{2,1,0:T(8,128)(2,1)} %broadcast_in_dim.16), calls=%async_computation | async-start | bytes 524288 | tf_op jit(solution)/shard_map/all_to_all | solution.py:260
  8.1 6.2 %all-to-all-done = bf16[8,64,256]{2,1,0:T(8,128)(2,1)S(1)} async-done(((bf16[8,64,256]{2,1,0:T(8,128)(2,1)}), bf16[8,64,256]{2,1,0:T(8,128)(2,1)S(1)}, u32[]{:S(2)}, u32[]{:S(2)}) %all-to-all-start) | async-done | bytes 262176 | tf_op jit(solution)/shard_map/all_to_all | solution.py:260
  14.7 2.0 %collective-permute-start = (bf16[256,1024]{1,0:T(8,128)(2,1)S(1)}, bf16[256,1024]{1,0:T(8,128)(2,1)S(1)}, u32[]{:S(2)}, u32[]{:S(2)}) collective-permute-start(bf16[256,1024]{1,0:T(8,128)(2,1)S(1)} %shard_map.103), channel_id=1, source_target_pairs={{0,2},{2,0},{1,3},{3,1},{4,6},{6,4},{5,7},{7,5},{8,10},{10,8},{9,1... | collective-permute-start | bytes 1572872 | tf_op jit(solution)/shard_map/ppermute | solution.py:256
  16.8 1.5 collective-permute-done.add_ref
  20.0 10.6 %all-to-all-start.1 = ((bf16[16,16,1024]{2,1,0:T(8,128)(2,1)}), bf16[16,16,1024]{2,1,0:T(8,128)(2,1)S(1)}, u32[]{:S(2)}, u32[]{:S(2)}) async-start(bf16[16,16,1024]{2,1,0:T(8,128)(2,1)} %bitcast.9), calls=%async_computation.1 | async-start | bytes 1048576 | tf_op jit(solution)/shard_map/all_to_all | solution.py:260
  33.5 13.5 %shard_map.106 = (bf16[256,1024]{1,0:T(8,128)(2,1)}, bf16[256,1024]{1,0:T(8,128)(2,1)}) custom-call(s32[256,128]{1,0:T(8,128)} %copy-done.9), custom_call_target="tpu_custom_call" | custom-call | flops 67108864 | bytes 1048576 | tf_op jit(solution)/shard_map/pallas_call | solution.py:33
  47.7 25.2 %all_to_all.35 = bf16[16,16,1024]{2,1,0:T(8,128)(2,1)} all-to-all(bf16[16,16,1024]{2,1,0:T(8,128)(2,1)S(1)} %get-tuple-element.52), channel_id=1, replica_groups=mesh['section'=4,'yh'=2,'z'=8,'core'=2,'tok'=2] {'yh','z'}, dimensions={0} | all-to-all | bytes 1048576 | tf_op jit(solution)/shard_map/all_to_all | solution.py:260
  72.8 5.2 %shard_map.108 = bf16[8,128,128]{2,1,0:T(8,128)(2,1)} custom-call(bf16[256,1024]{1,0:T(8,128)(2,1)} %bitcast.18, s32[128,128]{1,0:T(8,128)} %copy-done.7, bf16[1024,1024]{1,0:T(8,128)(2,1)} %w_ref, bf16[1024,1024]{1,0:T(8,128)(2,1)} %collective-permute-done.1.w2_ref), custom_call_target="tpu_custom_call" | custom-call | flops 1073741824 | bytes 4194304 | tf_op jit(solution)/shard_map/pallas_call | solution.py:33
  78.0 9.9 %all_to_all.36.parts_ref = bf16[8,128,128]{2,1,0:T(8,128)(2,1)} all-to-all(bf16[8,128,128]{2,1,0:T(8,128)(2,1)} %shard_map.108), channel_id=1, replica_groups=mesh['section'=4,'yh'=2,'z'=8,'core'=2,'tok'=2] {'section','tok'}, dimensions={0} | all-to-all | bytes 524288 | tf_op jit(solution)/shard_map/all_to_all | solution.py:260
  87.9 5.7 %shard_map.109 = (f32[128,128]{1,0:T(8,128)}, bf16[256,1024]{1,0:T(8,128)(2,1)}) custom-call(bf16[8,128,128]{2,1,0:T(8,128)(2,1)} %all_to_all.36.parts_ref, bf16[256,1024]{1,0:T(8,128)(2,1)} %get-tuple-element.56.slot_ref, bf16[256,1024]{1,0:T(8,128)(2,1)} %get-tuple-element.57.slot2_ref, f32[1,1024]{1,0:T(1,128)} %bitcast.28, f32[1,1024]{1,0:T(1,128)} %copy-done.14, ...), custom_call_target="tpu_custom_call" | custom-call | flops 1073741824 | bytes 4194304 | tf_op jit(solution)/shard_map/pallas_call | solution.py:33
  93.7 6.2 %all-to-all-start.4 = ((bf16[16,16,1024]{2,1,0:T(8,128)(2,1)}), bf16[16,16,1024]{2,1,0:T(8,128)(2,1)S(1)}, u32[]{:S(2)}, u32[]{:S(2)}) async-start(bf16[16,16,1024]{2,1,0:T(8,128)(2,1)} %bitcast.27), calls=%async_computation.4 | async-start | bytes 1048576 | tf_op jit(solution)/shard_map/all_to_all | solution.py:260
  99.9 2.2 %collective-permute-start.5 = (bf16[256,1024]{1,0:T(8,128)(2,1)}, bf16[256,1024]{1,0:T(8,128)(2,1)S(1)}, u32[]{:S(2)}, u32[]{:S(2)}) collective-permute-start(bf16[256,1024]{1,0:T(8,128)(2,1)} %get-tuple-element.57.slot2_ref), channel_id=1, source_target_pairs={{0,2},{2,0},{1,3},{3,1},{4,6},{6,4},{5,7},{7,5},{8,10},{10,8},{9,1... | collective-permute-start | bytes 1572872 | tf_op jit(solution)/shard_map/ppermute | solution.py:256
  102.6 1.2 collective-permute-done.5.slot2_ref.slot_ref
  105.2 3.6 %shard_map.110 = (bf16[256,1024]{1,0:T(8,128)(2,1)}, bf16[256,1024]{1,0:T(8,128)(2,1)}) custom-call(f32[128,128]{1,0:T(8,128)} %get-tuple-element.63.packed_ref, f32[128,128]{1,0:T(8,128)} %copy-done.12, bf16[256,1024]{1,0:T(8,128)(2,1)} %get-tuple-element.56.slot_ref, bf16[256,1024]{1,0:T(8,128)(2,1)} %copy-done.3, f32[1,1024]{1,0:T(1,128)} %bitcast.29), custom_call_target="tpu_custom_call" | custom-call | bytes 1048576 | tf_op jit(solution)/shard_map/pallas_call | solution.py:33
  109.6 4.6 %all-to-all-done.4.parts_ref = bf16[16,16,1024]{2,1,0:T(8,128)(2,1)S(1)} async-done(((bf16[16,16,1024]{2,1,0:T(8,128)(2,1)}), bf16[16,16,1024]{2,1,0:T(8,128)(2,1)S(1)}, u32[]{:S(2)}, u32[]{:S(2)}) %all-to-all-start.4) | async-done | bytes 524320 | tf_op jit(solution)/shard_map/all_to_all | solution.py:260
  114.8 20.4 %all_to_all.37 = bf16[16,16,1024]{2,1,0:T(8,128)(2,1)} all-to-all(bf16[16,16,1024]{2,1,0:T(8,128)(2,1)S(1)} %shard_map.111), channel_id=1, replica_groups=mesh['section'=4,'yh'=2,'z'=8,'core'=2,'tok'=2] {'yh','z'}, dimensions={0} | all-to-all | bytes 1048576 | tf_op jit(solution)/shard_map/all_to_all | solution.py:260
  135.2 5.3 %shard_map.112 = bf16[8,128,128]{2,1,0:T(8,128)(2,1)} custom-call(bf16[256,1024]{1,0:T(8,128)(2,1)} %bitcast.23, s32[128,128]{1,0:T(8,128)} %copy-done.7, bf16[1024,1024]{1,0:T(8,128)(2,1)} %w_ref.2, bf16[1024,1024]{1,0:T(8,128)(2,1)} %collective-permute-done.2.w2_ref), custom_call_target="tpu_custom_call" | custom-call | flops 1073741824 | bytes 4194304 | tf_op jit(solution)/shard_map/pallas_call | solution.py:33
  140.5 3.4 %collective-permute-start.7 = (bf16[256,1024]{1,0:T(8,128)(2,1)}, bf16[256,1024]{1,0:T(8,128)(2,1)S(1)}, u32[]{:S(2)}, u32[]{:S(2)}) collective-permute-start(bf16[256,1024]{1,0:T(8,128)(2,1)} %bitcast.24), channel_id=1, source_target_pairs={{0,2},{2,0},{1,3},{3,1},{4,6},{6,4},{5,7},{7,5},{8,10},{10,8},{9,1... | collective-permute-start | bytes 1572872 | tf_op jit(solution)/shard_map/ppermute | solution.py:256
  143.9 3.5 %all-to-all-start.6 = ((bf16[8,128,128]{2,1,0:T(8,128)(2,1)}), bf16[8,128,128]{2,1,0:T(8,128)(2,1)S(1)}, u32[]{:S(2)}, u32[]{:S(2)}) async-start(bf16[8,128,128]{2,1,0:T(8,128)(2,1)} %shard_map.112), calls=%async_computation.6 | async-start | bytes 524288 | tf_op jit(solution)/shard_map/all_to_all | solution.py:260
  148.2 4.1 %shard_map.113 = bf16[1024,1024]{1,0:T(8,128)(2,1)} custom-call(bf16[256,1024]{1,0:T(8,128)(2,1)} %get-tuple-element.70.codes_ref, bf16[256,1024]{1,0:T(8,128)(2,1)} %get-tuple-element.71.codes2_ref, bf16[256,1024]{1,0:T(8,128)(2,1)} %bitcast.25, bf16[256,1024]{1,0:T(8,128)(2,1)} %copy-done.10), custom_call_target="tpu_custom_call" | custom-call | flops 1073741824 | bytes 4194304 | tf_op jit(solution)/shard_map/pallas_call | solution.py:33
  152.4 1.8 %all-to-all-done.6.parts_ref = bf16[8,128,128]{2,1,0:T(8,128)(2,1)S(1)} async-done(((bf16[8,128,128]{2,1,0:T(8,128)(2,1)}), bf16[8,128,128]{2,1,0:T(8,128)(2,1)S(1)}, u32[]{:S(2)}, u32[]{:S(2)}) %all-to-all-start.6) | async-done | bytes 262176 | tf_op jit(solution)/shard_map/all_to_all | solution.py:260
  154.2 1.1 collective-permute-start.8
  155.3 2.1 %shard_map.114 = (f32[1024,1024]{1,0:T(8,128)S(1)}, f32[1,512]{1,0:T(1,128)S(1)}) custom-call(s32[4]{0:T(128)S(1)} %pad_add_fusion.at_ref, bf16[8,128,128]{2,1,0:T(8,128)(2,1)S(1)} %all-to-all-done.6.parts_ref, bf16[256,1024]{1,0:T(8,128)(2,1)S(1)} %copy-done.2, bf16[256,1024]{1,0:T(8,128)(2,1)S(1)} %bitcast.20), custom_call_target="tpu_custom_call" | custom-call | flops 1073741824 | bytes 4194304 | tf_op jit(solution)/shard_map/pallas_call | solution.py:33
  157.4 3.6 %shard_map.115 = (bf16[1024,1024]{1,0:T(8,128)(2,1)}, f32[1,512]{1,0:T(1,128)}) custom-call(s32[4]{0:T(128)S(1)} %pad_add_fusion.at_ref, bf16[8,128,128]{2,1,0:T(8,128)(2,1)S(1)} %collective-permute-done.8.parts_ref, bf16[256,1024]{1,0:T(8,128)(2,1)S(1)} %copy-done.4, bf16[256,1024]{1,0:T(8,128)(2,1)S(1)} %copy-done.6, ...), custom_call_target="tpu_custom_call" | custom-call | flops 1073741824 | bytes 4194304 | tf_op jit(solution)/shard_map/pallas_call | solution.py:33
  (54 shorter events, 11.3 us)
Async XLA Ops:
  0.6 7.5 %copy-start = (bf16[256,2048]{1,0:T(8,128)(2,1)S(1)}, bf16[256,2048]{1,0:T(8,128)(2,1)}, u32[]{:S(2)}) copy-start(bf16[256,2048]{1,0:T(8,128)(2,1)} %param.10) | copy-start | bytes 3145732
  2.2 12.2 %all-to-all-start = ((bf16[8,64,256]{2,1,0:T(8,128)(2,1)}), bf16[8,64,256]{2,1,0:T(8,128)(2,1)S(1)}, u32[]{:S(2)}, u32[]{:S(2)}) async-start(bf16[8,64,256]{2,1,0:T(8,128)(2,1)} %broadcast_in_dim.16), calls=%async_computation | async-start | bytes 524288 | tf_op jit(solution)/shard_map/all_to_all | solution.py:260
  14.4 16.4 %copy-start.13 = (f32[1024]{0:T(1024)S(1)}, f32[1024]{0:T(1024)}, u32[]{:S(2)}) copy-start(f32[1024]{0:T(1024)} %param.13) | copy-start | bytes 12292
  14.4 17.0 %copy-start.11 = (s32[2,256,64]{1,2,0:T(8,128)S(1)}, s32[2,256,64]{1,2,0:T(8,128)}, u32[]{:S(2)}) copy-start(s32[2,256,64]{1,2,0:T(8,128)} %param.15) | copy-start | bytes 393220
  14.7 32.3 %copy-start.8 = (f32[2048]{0:T(1024)S(1)}, f32[2048]{0:T(1024)}, u32[]{:S(2)}) copy-start(f32[2048]{0:T(1024)} %param.11) | copy-start | bytes 24580
  14.7 3.6 %collective-permute-start = (bf16[256,1024]{1,0:T(8,128)(2,1)S(1)}, bf16[256,1024]{1,0:T(8,128)(2,1)S(1)}, u32[]{:S(2)}, u32[]{:S(2)}) collective-permute-start(bf16[256,1024]{1,0:T(8,128)(2,1)S(1)} %shard_map.103), channel_id=1, source_target_pairs={{0,2},{2,0},{1,3},{3,1},{4,6},{6,4},{5,7},{7,5},{8,10},{10,8},{9,1... | collective-permute-start | bytes 1572872 | tf_op jit(solution)/shard_map/ppermute | solution.py:256
  19.4 27.6 %collective-permute-start.1 = (bf16[1024,1024]{1,0:T(8,128)(2,1)}, bf16[1024,1024]{1,0:T(8,128)(2,1)}, u32[]{:S(2)}, u32[]{:S(2)}) collective-permute-start(bf16[1024,1024]{1,0:T(8,128)(2,1)} %w_ref), channel_id=1, source_target_pairs={{0,2},{2,0},{1,3},{3,1},{4,6},{6,4},{5,7},{7,5},{8,10},{10,8},{9,1... | collective-permute-start | bytes 6291464 | tf_op jit(solution)/shard_map/ppermute | solution.py:256
  19.9 27.1 %collective-permute-start.2 = (bf16[1024,1024]{1,0:T(8,128)(2,1)}, bf16[1024,1024]{1,0:T(8,128)(2,1)}, u32[]{:S(2)}, u32[]{:S(2)}) collective-permute-start(bf16[1024,1024]{1,0:T(8,128)(2,1)} %w_ref.2), channel_id=1, source_target_pairs={{0,2},{2,0},{1,3},{3,1},{4,6},{6,4},{5,7},{7,5},{8,10},{10,8},{9,1... | collective-permute-start | bytes 6291464 | tf_op jit(solution)/shard_map/ppermute | solution.py:256
  20.0 27.0 %all-to-all-start.1 = ((bf16[16,16,1024]{2,1,0:T(8,128)(2,1)}), bf16[16,16,1024]{2,1,0:T(8,128)(2,1)S(1)}, u32[]{:S(2)}, u32[]{:S(2)}) async-start(bf16[16,16,1024]{2,1,0:T(8,128)(2,1)} %bitcast.9), calls=%async_computation.1 | async-start | bytes 1048576 | tf_op jit(solution)/shard_map/all_to_all | solution.py:260
  30.8 16.2 %collective-permute-start.3 = (f32[1,1024]{1,0:T(1,128)S(1)}, f32[1,1024]{1,0:T(1,128)S(1)}, u32[]{:S(2)}, u32[]{:S(2)}) collective-permute-start(f32[1,1024]{1,0:T(1,128)S(1)} %bitcast.30), channel_id=1, source_target_pairs={{0,2},{2,0},{1,3},{3,1},{4,6},{6,4},{5,7},{7,5},{8,10},{10,8},{9,1... | collective-permute-start | bytes 12296 | tf_op jit(solution)/shard_map/ppermute | solution.py:256
  47.0 31.1 %copy-start.14 = (f32[1,1024]{1,0:T(1,128)}, f32[1,1024]{1,0:T(1,128)S(1)}, u32[]{:S(2)}) copy-start(f32[1,1024]{1,0:T(1,128)S(1)} %collective-permute-done.3.bias2_ref) | copy-start | bytes 12292
  87.9 14.2 %copy-start.1 = (bf16[16,16,1024]{2,1,0:T(8,128)(2,1)S(1)}, bf16[16,16,1024]{2,1,0:T(8,128)(2,1)}, u32[]{:S(2)}) copy-start(bf16[16,16,1024]{2,1,0:T(8,128)(2,1)} %all_to_all.35) | copy-start | bytes 1572868
  93.7 20.5 %all-to-all-start.4 = ((bf16[16,16,1024]{2,1,0:T(8,128)(2,1)}), bf16[16,16,1024]{2,1,0:T(8,128)(2,1)S(1)}, u32[]{:S(2)}, u32[]{:S(2)}) async-start(bf16[16,16,1024]{2,1,0:T(8,128)(2,1)} %bitcast.27), calls=%async_computation.4 | async-start | bytes 1048576 | tf_op jit(solution)/shard_map/all_to_all | solution.py:260
  99.9 3.9 %collective-permute-start.5 = (bf16[256,1024]{1,0:T(8,128)(2,1)}, bf16[256,1024]{1,0:T(8,128)(2,1)S(1)}, u32[]{:S(2)}, u32[]{:S(2)}) collective-permute-start(bf16[256,1024]{1,0:T(8,128)(2,1)} %get-tuple-element.57.slot2_ref), channel_id=1, source_target_pairs={{0,2},{2,0},{1,3},{3,1},{4,6},{6,4},{5,7},{7,5},{8,10},{10,8},{9,1... | collective-permute-start | bytes 1572872 | tf_op jit(solution)/shard_map/ppermute | solution.py:256
  102.1 6.7 %collective-permute-start.6 = (bf16[256,1024]{1,0:T(8,128)(2,1)S(1)}, bf16[256,1024]{1,0:T(8,128)(2,1)S(1)}, u32[]{:S(2)}, u32[]{:S(2)}) collective-permute-start(bf16[256,1024]{1,0:T(8,128)(2,1)S(1)} %bitcast.19), channel_id=1, source_target_pairs={{0,2},{2,0},{1,3},{3,1},{4,6},{6,4},{5,7},{7,5},{8,10},{10,8},{9,1... | collective-permute-start | bytes 1572872 | tf_op jit(solution)/shard_map/ppermute | solution.py:256
  102.2 1.8 %collective-permute-start.4 = (f32[128,128]{1,0:T(8,128)}, f32[128,128]{1,0:T(8,128)S(1)}, u32[]{:S(2)}, u32[]{:S(2)}) collective-permute-start(f32[128,128]{1,0:T(8,128)} %get-tuple-element.63.packed_ref), channel_id=1, source_target_pairs={{0,2},{2,0},{1,3},{3,1},{4,6},{6,4},{5,7},{7,5},{8,10},{10,8},{9,1... | collective-permute-start | bytes 196616 | tf_op jit(solution)/shard_map/ppermute | solution.py:256
  103.8 0.8 copy-start.3
  140.5 6.9 %collective-permute-start.7 = (bf16[256,1024]{1,0:T(8,128)(2,1)}, bf16[256,1024]{1,0:T(8,128)(2,1)S(1)}, u32[]{:S(2)}, u32[]{:S(2)}) collective-permute-start(bf16[256,1024]{1,0:T(8,128)(2,1)} %bitcast.24), channel_id=1, source_target_pairs={{0,2},{2,0},{1,3},{3,1},{4,6},{6,4},{5,7},{7,5},{8,10},{10,8},{9,1... | collective-permute-start | bytes 1572872 | tf_op jit(solution)/shard_map/ppermute | solution.py:256
  143.9 10.3 %all-to-all-start.6 = ((bf16[8,128,128]{2,1,0:T(8,128)(2,1)}), bf16[8,128,128]{2,1,0:T(8,128)(2,1)S(1)}, u32[]{:S(2)}, u32[]{:S(2)}) async-start(bf16[8,128,128]{2,1,0:T(8,128)(2,1)} %shard_map.112), calls=%async_computation.6 | async-start | bytes 524288 | tf_op jit(solution)/shard_map/all_to_all | solution.py:260
  147.4 7.9 %copy-start.2 = (bf16[256,1024]{1,0:T(8,128)(2,1)S(1)}, bf16[256,1024]{1,0:T(8,128)(2,1)}, u32[]{:S(2)}) copy-start(bf16[256,1024]{1,0:T(8,128)(2,1)} %get-tuple-element.56.slot_ref) | copy-start | bytes 1572868
  147.4 0.8 copy-start.10
  152.4 5.1 %copy-start.4 = (bf16[256,1024]{1,0:T(8,128)(2,1)S(1)}, bf16[256,1024]{1,0:T(8,128)(2,1)}, u32[]{:S(2)}) copy-start(bf16[256,1024]{1,0:T(8,128)(2,1)} %copy-done.3) | copy-start | bytes 1572868
  154.2 3.3 %copy-start.6 = (bf16[256,1024]{1,0:T(8,128)(2,1)S(1)}, bf16[256,1024]{1,0:T(8,128)(2,1)}, u32[]{:S(2)}) copy-start(bf16[256,1024]{1,0:T(8,128)(2,1)} %copy-done.5) | copy-start | bytes 1572868
  154.2 3.2 %collective-permute-start.8 = (bf16[8,128,128]{2,1,0:T(8,128)(2,1)S(1)}, bf16[8,128,128]{2,1,0:T(8,128)(2,1)S(1)}, u32[]{:S(2)}, u32[]{:S(2)}) collective-permute-start(bf16[8,128,128]{2,1,0:T(8,128)(2,1)S(1)} %all-to-all-done.6.parts_ref), channel_id=1, source_target_pairs={{0,2},{2,0},{1,3},{3,1},{4,6},{6,4},{5,7},{7,5},{8,10},{10,8},{9,1... | collective-permute-start | bytes 786440 | tf_op jit(solution)/shard_map/ppermute | solution.py:256
  (4 other events, 2.7 us)

commit v4 on v3

--- a/solution.py
+++ b/solution.py
@@ -17,7 +17,7 @@
 ANY = pl.BlockSpec(memory_space=pl.ANY)
 HBM = pl.BlockSpec(memory_space=pltpu.HBM)
 MIB = 1024 * 1024
-SMALL, MIDDLE, MOST = 12, 24, 62
+SMALL, MIDDLE, MOST = 12, 24, 24
 COPIES = pltpu.SemaphoreType.DMA
 ROW_BLOCKS = 4
 FEATURES = ("section", "tok")
@@ -143,14 +143,15 @@
 
 
 def product_kernel(contract, x_ref, place_ref, w_ref, w2_ref, out_ref, held, sems):
-    copies = [start(w_ref, held.at[0], sems.at[0]), start(w2_ref, held.at[1], sems.at[1])]
+    copy = start(w_ref, held, sems.at[0])
     place = place_ref[...]
     lane, chunk = place & (LANES - 1), place >> 7
     low = high = jnp.zeros(place.shape, F32)
-    for n in range(2):
-        copies[n].wait()
+    for n, weight in ((1, w2_ref), (0, held)):
+        if n == 0:
+            copy.wait()
         y = lax.dot_general(
-            x_ref[...], held[n], (((1,), (contract,)), ((), ())), preferred_element_type=F32
+            x_ref[...], weight[...], (((1,), (contract,)), ((), ())), preferred_element_type=F32
         )
         blocks = y.shape[1] // LANES
         for j in range(blocks):
@@ -184,17 +185,16 @@
     held,
     sems,
 ):
-    found = [start(slot_ref, slots.at[0], sems.at[2]), start(slot2_ref, slots.at[1], sems.at[3])]
-    copies = [start(w_ref, held.at[0], sems.at[0]), start(w2_ref, held.at[1], sems.at[1])]
+    found = [start(slot_ref, slots.at[0], sems.at[1]), start(slot2_ref, slots.at[1], sems.at[2])]
+    copy = start(w_ref, held, sems.at[0])
     packed = sum_of(parts_ref)
     packed_ref[...] = packed
     for n, bias in enumerate((bias_ref, bias2_ref)):
         found[n].wait()
         spread_codes(packed, slots.at[n], bias, codes.at[n])
-    for copy in copies:
-        copy.wait()
-    y = jnp.dot(codes[0], held[0], preferred_element_type=F32)
-    y = y + jnp.dot(codes[1], held[1], preferred_element_type=F32)
+    y = jnp.dot(codes[1], w2_ref[...], preferred_element_type=F32)
+    copy.wait()
+    y = y + jnp.dot(codes[0], held[...], preferred_element_type=F32)
     out_ref[...] = y.astype(BF16)
 
 
@@ -277,7 +277,21 @@
 
     centered = (residual[0].astype(F32) - center).astype(BF16)
     out = jnp.broadcast_to(centered[None], (receivers,) + centered.shape)
-    arrived = exchange(out, ("tok", "section")).reshape(2, rows, inputs)
+    out, listed = lax.optimization_barrier((out, chosen))
+    place, wide = call(
+        functools.partial(place_kernel, latents),
+        (SCALARS, HERE),
+        [
+            (HERE, spec(rows // 2, LANES, dtype=jnp.int32)),
+            (HERE, spec(rows, LANES, dtype=jnp.int32)),
+        ],
+        (at, listed),
+        vmem=SMALL,
+    )
+    arrived, wide, place = lax.optimization_barrier(
+        (exchange(out, ("tok", "section")), wide, place)
+    )
+    arrived = arrived.reshape(2, rows, inputs)
     own_rows = lax.dynamic_index_in_dim(arrived, core, 0, keepdims=False)
     other_rows = lax.dynamic_index_in_dim(arrived, 1 - core, 0, keepdims=False)
     whiten_cols = lax.dynamic_slice_in_dim(whiten, at[TOK] * width, width, 1)
@@ -304,19 +318,7 @@
     share, all_shares = spec(*shares[1:]), spec(*shares)
     bias_row, decoder_bias = encoder_bias[None], decoder_bias[None]
 
-    part, listed, encoder_weight, decoder_weight, bias_row = lax.optimization_barrier(
-        (part, chosen, encoder_weight, decoder_weight, bias_row)
-    )
-    place, wide = call(
-        functools.partial(place_kernel, latents),
-        (SCALARS, HERE),
-        [
-            (HERE, spec(rows // 2, LANES, dtype=jnp.int32)),
-            (HERE, spec(rows, LANES, dtype=jnp.int32)),
-        ],
-        (at, listed),
-        vmem=SMALL,
-    )
+    part, wide, bias_row = lax.optimization_barrier((part, wide, bias_row))
     slot, slot2 = call(
         find_kernel,
         (HERE,),
@@ -325,18 +327,9 @@
         [pltpu.VMEM((2, rows, latents), jnp.int32)],
         4 * picks * rows * latents,
     )
-    encoder_weight2, decoder_weight2 = swap(encoder_weight), swap(decoder_weight)
     bias_row2 = swap(bias_row)
-    parts, slot, slot2, place, encoder_weight2, decoder_weight2, bias_row2 = lax.optimization_barrier(
-        (
-            exchange(part.reshape(shares), COLUMN),
-            slot,
-            slot2,
-            place,
-            encoder_weight2,
-            decoder_weight2,
-            bias_row2,
-        )
+    parts, slot, slot2, bias_row2 = lax.optimization_barrier(
+        (exchange(part.reshape(shares), COLUMN), slot, slot2, bias_row2)
     )
     whitened, out = call(
         shift_kernel,
@@ -345,19 +338,21 @@
         (at, parts, decoder_bias),
         vmem=SMALL,
     )
+    out, encoder_weight = lax.optimization_barrier((out, encoder_weight))
+    encoder_weight2 = swap(encoder_weight)
     shifted = exchange(out, COLUMN).reshape(rows, width)
 
     flops = 4 * rows * width * latents
     moved = 4 * width * latents
-    weights_held = [pltpu.VMEM((2, width, latents), BF16), COPIES((2,))]
+    weight_held = [pltpu.VMEM((width, latents), BF16), COPIES((1,))]
 
     def chosen_product(contract, x, weight, weight2):
         (packed,) = call(
             functools.partial(product_kernel, contract),
-            (HERE, HERE, ANY, ANY),
+            (HERE, HERE, ANY, HERE),
             [(HERE, spec(receivers, rows // 2, LANES))],
             (x, place, weight, weight2),
-            weights_held,
+            weight_held,
             flops,
             moved,
             MOST,
@@ -365,25 +360,27 @@
         return packed
 
     encoded = chosen_product(0, shifted, encoder_weight, encoder_weight2)
-    encoded, shifted = lax.optimization_barrier((encoded, shifted))
+    encoded, shifted, weight = lax.optimization_barrier((encoded, shifted, decoder_weight))
+    weight2 = swap(weight)
     shifted2, other_slot = swap(shifted), swap(slot2)
     encoded = exchange(encoded, FEATURES)
     packed, part = call(
         decode_kernel,
-        (HERE, ANY, ANY, HERE, HERE, ANY, ANY),
+        (HERE, ANY, ANY, HERE, HERE, ANY, HERE),
         [(HERE, spec(rows // 2, LANES, dtype=F32)), (HERE, spec(rows, width))],
-        (encoded, slot, slot2, bias_row, bias_row2, decoder_weight, decoder_weight2),
+        (encoded, slot, slot2, bias_row, bias_row2, weight, weight2),
         [
             pltpu.VMEM((2, rows, latents), BF16),
             pltpu.VMEM((2, rows, latents), BF16),
-            pltpu.VMEM((2, width, latents), BF16),
-            COPIES((4,)),
+            pltpu.VMEM((latents, width), BF16),
+            COPIES((3,)),
         ],
         flops,
         moved,
         MOST,
     )
-    part, packed = lax.optimization_barrier((part, packed))
+    part, packed, decoder_weight = lax.optimization_barrier((part, packed, decoder_weight))
+    decoder_weight2 = swap(decoder_weight)
     codes, codes2 = call(
         codes_kernel,
         (HERE,) * 5,

time: 162 us -> 159 us (0.981)
  blocking collectives: 55.4 us -> 50 us
  Pallas kernels: 46.4 us -> 41.2 us
  waiting for transfers between devices: 15.6 us -> 18.2 us
  starting transfers between devices: 36.8 us -> 39.3 us
  local copies, waits for them, and re-layouts: 5.01 us -> 7.24 us
    all_to_all x3, blocking collectives: 55.4 us -> 50 us  [exchange(): return lax.all_to_all(x, axes, 0, 0)]
    pallas_call x13, Pallas kernels: 46.4 us -> 41.2 us  [call(): pl.pallas_call(kernel, in_specs=list(ins), out_specs=tuple((place for pla...]
    ppermute x9 -> x10, starting transfers between devices: 10.6 us -> 14.7 us  [swap(): return lax.ppermute(x, 'core', [(0, 1), (1, 0)])]
    all_to_all x4, waiting for transfers between devices: 12.6 us -> 15.3 us  [exchange(): return lax.all_to_all(x, axes, 0, 0)]
    unnamed x30 -> x34, local copies, waits for them, and re-layouts: 4.11 us -> 5.44 us
  transfers between devices with their start and end apart: 13 -> 14, of which waited for: 6 -> 6; matrix products, arithmetic and copies ran while one was open for 0% -> 1% of each run, Pallas kernels for 15% -> 16%
where the time goes in v4:
time: 159 us; the launch traced here: 158 us
  blocking collectives  50 us (31%)
  Pallas kernels  41.2 us (26%)
  starting transfers between devices  39.3 us (25%)
  waiting for transfers between devices  18.2 us (11%)
  local copies, waits for them, and re-layouts  7.24 us (5%)
    all_to_all x3, blocking collectives, exchange(): return lax.all_to_all(x, axes, 0, 0)  50 us
    pallas_call x13, Pallas kernels, call(): pl.pallas_call(kernel, in_specs=list(ins), out_specs=tuple((place for pla...  41.2 us
    all_to_all x4, starting transfers between devices, exchange(): return lax.all_to_all(x, axes, 0, 0)  24.6 us
    all_to_all x4, waiting for transfers between devices, exchange(): return lax.all_to_all(x, axes, 0, 0)  15.3 us
    ppermute x10, starting transfers between devices, swap(): return lax.ppermute(x, 'core', [(0, 1), (1, 0)])  14.7 us
    unnamed x34, local copies, waits for them, and re-layouts  5.44 us
  transfers between devices with their start and end apart: 14, of which 6 were waited for; matrix products, arithmetic and copies ran while one was open for 1% of the time, Pallas kernels for 16%

profile of v4, /device:TPU:1, one launch (start us, length us, event | category | flops | bytes accessed | tf_op | source)
XLA Modules:
  0.0 158.0 jit_solution(1870043106849698223)
XLA Ops:
  2.2 5.9 %all-to-all-start = ((bf16[8,64,256]{2,1,0:T(8,128)(2,1)}), bf16[8,64,256]{2,1,0:T(8,128)(2,1)S(1)}, u32[]{:S(2)}, u32[]{:S(2)}) async-start(bf16[8,64,256]{2,1,0:T(8,128)(2,1)} %broadcast_in_dim.16), calls=%async_computation | async-start | bytes 524288 | tf_op jit(solution)/shard_map/all_to_all | solution.py:260
  10.6 3.8 %all-to-all-done = bf16[8,64,256]{2,1,0:T(8,128)(2,1)S(1)} async-done(((bf16[8,64,256]{2,1,0:T(8,128)(2,1)}), bf16[8,64,256]{2,1,0:T(8,128)(2,1)S(1)}, u32[]{:S(2)}, u32[]{:S(2)}) %all-to-all-start) | async-done | bytes 262176 | tf_op jit(solution)/shard_map/all_to_all | solution.py:260
  14.7 2.0 %collective-permute-start = (bf16[256,1024]{1,0:T(8,128)(2,1)S(1)}, bf16[256,1024]{1,0:T(8,128)(2,1)S(1)}, u32[]{:S(2)}, u32[]{:S(2)}) collective-permute-start(bf16[256,1024]{1,0:T(8,128)(2,1)S(1)} %shard_map.104), channel_id=1, source_target_pairs={{0,2},{2,0},{1,3},{3,1},{4,6},{6,4},{5,7},{7,5},{8,10},{10,8},{9,1... | collective-permute-start | bytes 1572872 | tf_op jit(solution)/shard_map/ppermute | solution.py:256
  16.8 1.5 collective-permute-done.add_ref
  19.4 10.6 %all-to-all-start.1 = ((bf16[16,16,1024]{2,1,0:T(8,128)(2,1)}), bf16[16,16,1024]{2,1,0:T(8,128)(2,1)S(1)}, u32[]{:S(2)}, u32[]{:S(2)}) async-start(bf16[16,16,1024]{2,1,0:T(8,128)(2,1)} %bitcast.9), calls=%async_computation.1 | async-start | bytes 1048576 | tf_op jit(solution)/shard_map/all_to_all | solution.py:260
  30.8 13.4 %shard_map.106 = (bf16[256,1024]{1,0:T(8,128)(2,1)}, bf16[256,1024]{1,0:T(8,128)(2,1)}) custom-call(s32[256,128]{1,0:T(8,128)} %copy-done.14), custom_call_target="tpu_custom_call" | custom-call | flops 67108864 | bytes 1048576 | tf_op jit(solution)/shard_map/pallas_call | solution.py:33
  45.8 2.9 %collective-permute-start.2 = (bf16[1024,1024]{1,0:T(8,128)(2,1)}, bf16[1024,1024]{1,0:T(8,128)(2,1)S(1)}, u32[]{:S(2)}, u32[]{:S(2)}) collective-permute-start(bf16[1024,1024]{1,0:T(8,128)(2,1)} %w_ref), channel_id=1, source_target_pairs={{0,2},{2,0},{1,3},{3,1},{4,6},{6,4},{5,7},{7,5},{8,10},{10,8},{9,1... | collective-permute-start | bytes 6291464 | tf_op jit(solution)/shard_map/ppermute | solution.py:256
  48.7 20.2 %all_to_all.35 = bf16[16,16,1024]{2,1,0:T(8,128)(2,1)S(1)} all-to-all(bf16[16,16,1024]{2,1,0:T(8,128)(2,1)S(1)} %get-tuple-element.59), channel_id=1, replica_groups=mesh['section'=4,'yh'=2,'z'=8,'core'=2,'tok'=2] {'yh','z'}, dimensions={0} | all-to-all | bytes 1048576 | tf_op jit(solution)/shard_map/all_to_all | solution.py:260
  68.9 1.8 %copy-done.4 = bf16[1024,1024]{1,0:T(8,128)(2,1)S(1)} copy-done((bf16[1024,1024]{1,0:T(8,128)(2,1)S(1)}, bf16[1024,1024]{1,0:T(8,128)(2,1)}, u32[]{:S(2)}) %copy-start.4) | copy-done | bytes 2097176
  70.7 2.0 %shard_map.108 = bf16[8,128,128]{2,1,0:T(8,128)(2,1)S(1)} custom-call(bf16[256,1024]{1,0:T(8,128)(2,1)S(1)} %bitcast.18, s32[128,128]{1,0:T(8,128)S(1)} %get-tuple-element.60.place_ref, bf16[1024,1024]{1,0:T(8,128)(2,1)S(1)} %copy-done.4, bf16[1024,1024]{1,0:T(8,128)(2,1)S(1)} %collective-permute-done.2.w2_ref), custom_call_target="tpu_custom_call" | custom-call | flops 1073741824 | bytes 4194304 | tf_op jit(solution)/shard_map/pallas_call | solution.py:33
  72.7 3.3 %collective-permute-start.3 = (bf16[1024,1024]{1,0:T(8,128)(2,1)S(1)}, bf16[1024,1024]{1,0:T(8,128)(2,1)S(1)}, u32[]{:S(2)}, u32[]{:S(2)}) collective-permute-start(bf16[1024,1024]{1,0:T(8,128)(2,1)S(1)} %copy-done.1), channel_id=1, source_target_pairs={{0,2},{2,0},{1,3},{3,1},{4,6},{6,4},{5,7},{7,5},{8,10},{10,8},{9,1... | collective-permute-start | bytes 6291464 | tf_op jit(solution)/shard_map/ppermute | solution.py:256
  76.0 9.2 %all_to_all.36.parts_ref = bf16[8,128,128]{2,1,0:T(8,128)(2,1)S(1)} all-to-all(bf16[8,128,128]{2,1,0:T(8,128)(2,1)S(1)} %shard_map.108), channel_id=1, replica_groups=mesh['section'=4,'yh'=2,'z'=8,'core'=2,'tok'=2] {'section','tok'}, dimensions={0} | all-to-all | bytes 524288 | tf_op jit(solution)/shard_map/all_to_all | solution.py:260
  85.2 3.5 %shard_map.109 = (f32[128,128]{1,0:T(8,128)S(1)}, bf16[256,1024]{1,0:T(8,128)(2,1)S(1)}) custom-call(bf16[8,128,128]{2,1,0:T(8,128)(2,1)S(1)} %all_to_all.36.parts_ref, bf16[256,1024]{1,0:T(8,128)(2,1)S(1)} %copy-done.5, bf16[256,1024]{1,0:T(8,128)(2,1)S(1)} %copy-done.10, f32[1,1024]{1,0:T(1,128)S(1)} %bitcast.26, ...), custom_call_target="tpu_custom_call" | custom-call | flops 1073741824 | bytes 4194304 | tf_op jit(solution)/shard_map/pallas_call | solution.py:33
  90.3 4.7 %all-to-all-start.4 = ((bf16[16,16,1024]{2,1,0:T(8,128)(2,1)}), bf16[16,16,1024]{2,1,0:T(8,128)(2,1)}, u32[]{:S(2)}, u32[]{:S(2)}) async-start(bf16[16,16,1024]{2,1,0:T(8,128)(2,1)} %bitcast.21), calls=%async_computation.4 | async-start | bytes 1048576 | tf_op jit(solution)/shard_map/all_to_all | solution.py:260
  98.7 3.6 %shard_map.110 = (bf16[256,1024]{1,0:T(8,128)(2,1)}, bf16[256,1024]{1,0:T(8,128)(2,1)}) custom-call(f32[128,128]{1,0:T(8,128)} %copy-done.11, f32[128,128]{1,0:T(8,128)} %copy-done.16, bf16[256,1024]{1,0:T(8,128)(2,1)} %get-tuple-element.63.slot_ref, bf16[256,1024]{1,0:T(8,128)(2,1)} %copy-done.7, f32[1,1024]{1,0:T(1,128)} %bitcast.24), custom_call_target="tpu_custom_call" | custom-call | bytes 1048576 | tf_op jit(solution)/shard_map/pallas_call | solution.py:33
  102.3 8.8 %all-to-all-done.4.parts_ref = bf16[16,16,1024]{2,1,0:T(8,128)(2,1)} async-done(((bf16[16,16,1024]{2,1,0:T(8,128)(2,1)}), bf16[16,16,1024]{2,1,0:T(8,128)(2,1)}, u32[]{:S(2)}, u32[]{:S(2)}) %all-to-all-start.4) | async-done | bytes 524320 | tf_op jit(solution)/shard_map/all_to_all | solution.py:260
  112.2 20.6 %all_to_all.37 = bf16[16,16,1024]{2,1,0:T(8,128)(2,1)} all-to-all(bf16[16,16,1024]{2,1,0:T(8,128)(2,1)S(1)} %shard_map.111), channel_id=1, replica_groups=mesh['section'=4,'yh'=2,'z'=8,'core'=2,'tok'=2] {'yh','z'}, dimensions={0} | all-to-all | bytes 1048576 | tf_op jit(solution)/shard_map/all_to_all | solution.py:260
  132.8 4.5 %shard_map.112 = bf16[8,128,128]{2,1,0:T(8,128)(2,1)} custom-call(bf16[256,1024]{1,0:T(8,128)(2,1)} %bitcast.13.x_ref.grad_ref, s32[128,128]{1,0:T(8,128)S(1)} %get-tuple-element.60.place_ref, bf16[1024,1024]{1,0:T(8,128)(2,1)S(1)} %copy-done.1, bf16[1024,1024]{1,0:T(8,128)(2,1)} %collective-permute-done.7.w2_ref), custom_call_target="tpu_custom_call" | custom-call | flops 1073741824 | bytes 4194304 | tf_op jit(solution)/shard_map/pallas_call | solution.py:33
  137.3 3.2 %collective-permute-start.8 = (bf16[256,1024]{1,0:T(8,128)(2,1)}, bf16[256,1024]{1,0:T(8,128)(2,1)S(1)}, u32[]{:S(2)}, u32[]{:S(2)}) collective-permute-start(bf16[256,1024]{1,0:T(8,128)(2,1)} %bitcast.13.x_ref.grad_ref), channel_id=1, source_target_pairs={{0,2},{2,0},{1,3},{3,1},{4,6},{6,4},{5,7},{7,5},{8,10},{10,8},{9,1... | collective-permute-start | bytes 1572872 | tf_op jit(solution)/shard_map/ppermute | solution.py:256
  140.6 3.4 %all-to-all-start.6 = ((bf16[8,128,128]{2,1,0:T(8,128)(2,1)}), bf16[8,128,128]{2,1,0:T(8,128)(2,1)S(1)}, u32[]{:S(2)}, u32[]{:S(2)}) async-start(bf16[8,128,128]{2,1,0:T(8,128)(2,1)} %shard_map.112), calls=%async_computation.6 | async-start | bytes 524288 | tf_op jit(solution)/shard_map/all_to_all | solution.py:260
  144.8 4.1 %shard_map.113 = bf16[1024,1024]{1,0:T(8,128)(2,1)} custom-call(bf16[256,1024]{1,0:T(8,128)(2,1)} %get-tuple-element.78.codes_ref, bf16[256,1024]{1,0:T(8,128)(2,1)} %get-tuple-element.79.codes2_ref, bf16[256,1024]{1,0:T(8,128)(2,1)} %bitcast.13.x_ref.grad_ref, bf16[256,1024]{1,0:T(8,128)(2,1)} %copy-done.15), custom_call_target="tpu_custom_call" | custom-call | flops 1073741824 | bytes 4194304 | tf_op jit(solution)/shard_map/pallas_call | solution.py:33
  149.0 1.8 %all-to-all-done.6.parts_ref = bf16[8,128,128]{2,1,0:T(8,128)(2,1)S(1)} async-done(((bf16[8,128,128]{2,1,0:T(8,128)(2,1)}), bf16[8,128,128]{2,1,0:T(8,128)(2,1)S(1)}, u32[]{:S(2)}, u32[]{:S(2)}) %all-to-all-start.6) | async-done | bytes 262176 | tf_op jit(solution)/shard_map/all_to_all | solution.py:260
  151.6 2.1 %shard_map.114 = (f32[1024,1024]{1,0:T(8,128)S(1)}, f32[1,512]{1,0:T(1,128)S(1)}) custom-call(s32[4]{0:T(128)S(1)} %pad_add_fusion.at_ref, bf16[8,128,128]{2,1,0:T(8,128)(2,1)S(1)} %all-to-all-done.6.parts_ref, bf16[256,1024]{1,0:T(8,128)(2,1)S(1)} %copy-done.6, bf16[256,1024]{1,0:T(8,128)(2,1)S(1)} %bitcast.20), custom_call_target="tpu_custom_call" | custom-call | flops 1073741824 | bytes 4194304 | tf_op jit(solution)/shard_map/pallas_call | solution.py:33
  153.7 4.1 %shard_map.115 = (bf16[1024,1024]{1,0:T(8,128)(2,1)}, f32[1,512]{1,0:T(1,128)}) custom-call(s32[4]{0:T(128)S(1)} %pad_add_fusion.at_ref, bf16[8,128,128]{2,1,0:T(8,128)(2,1)S(1)} %collective-permute-done.9.parts_ref, bf16[256,1024]{1,0:T(8,128)(2,1)S(1)} %copy-done.8, bf16[256,1024]{1,0:T(8,128)(2,1)} %collective-permute-done.6.x_ref, ...), custom_call_target="tpu_custom_call" | custom-call | flops 1073741824 | bytes 4194304 | tf_op jit(solution)/shard_map/pallas_call | solution.py:33
  (60 shorter events, 15.8 us)
Async XLA Ops:
  0.6 9.9 %copy-start = (bf16[256,2048]{1,0:T(8,128)(2,1)S(1)}, bf16[256,2048]{1,0:T(8,128)(2,1)}, u32[]{:S(2)}) copy-start(bf16[256,2048]{1,0:T(8,128)(2,1)} %param.10) | copy-start | bytes 3145732
  2.2 12.2 %all-to-all-start = ((bf16[8,64,256]{2,1,0:T(8,128)(2,1)}), bf16[8,64,256]{2,1,0:T(8,128)(2,1)S(1)}, u32[]{:S(2)}, u32[]{:S(2)}) async-start(bf16[8,64,256]{2,1,0:T(8,128)(2,1)} %broadcast_in_dim.16), calls=%async_computation | async-start | bytes 524288 | tf_op jit(solution)/shard_map/all_to_all | solution.py:260
  14.4 15.7 %copy-start.13 = (f32[1024]{0:T(1024)S(1)}, f32[1024]{0:T(1024)}, u32[]{:S(2)}) copy-start(f32[1024]{0:T(1024)} %param.13) | copy-start | bytes 12292
  14.4 30.8 %copy-start.12 = (f32[2048]{0:T(1024)S(1)}, f32[2048]{0:T(1024)}, u32[]{:S(2)}) copy-start(f32[2048]{0:T(1024)} %param.11) | copy-start | bytes 24580
  14.7 3.6 %collective-permute-start = (bf16[256,1024]{1,0:T(8,128)(2,1)S(1)}, bf16[256,1024]{1,0:T(8,128)(2,1)S(1)}, u32[]{:S(2)}, u32[]{:S(2)}) collective-permute-start(bf16[256,1024]{1,0:T(8,128)(2,1)S(1)} %shard_map.104), channel_id=1, source_target_pairs={{0,2},{2,0},{1,3},{3,1},{4,6},{6,4},{5,7},{7,5},{8,10},{10,8},{9,1... | collective-permute-start | bytes 1572872 | tf_op jit(solution)/shard_map/ppermute | solution.py:256
  19.4 25.7 %all-to-all-start.1 = ((bf16[16,16,1024]{2,1,0:T(8,128)(2,1)}), bf16[16,16,1024]{2,1,0:T(8,128)(2,1)S(1)}, u32[]{:S(2)}, u32[]{:S(2)}) async-start(bf16[16,16,1024]{2,1,0:T(8,128)(2,1)} %bitcast.9), calls=%async_computation.1 | async-start | bytes 1048576 | tf_op jit(solution)/shard_map/all_to_all | solution.py:260
  30.1 14.2 %collective-permute-start.1 = (f32[1,1024]{1,0:T(1,128)S(1)}, f32[1,1024]{1,0:T(1,128)S(1)}, u32[]{:S(2)}, u32[]{:S(2)}) collective-permute-start(f32[1,1024]{1,0:T(1,128)S(1)} %bitcast.25), channel_id=1, source_target_pairs={{0,2},{2,0},{1,3},{3,1},{4,6},{6,4},{5,7},{7,5},{8,10},{10,8},{9,1... | collective-permute-start | bytes 12296 | tf_op jit(solution)/shard_map/ppermute | solution.py:256
  45.8 23.1 %collective-permute-start.2 = (bf16[1024,1024]{1,0:T(8,128)(2,1)}, bf16[1024,1024]{1,0:T(8,128)(2,1)S(1)}, u32[]{:S(2)}, u32[]{:S(2)}) collective-permute-start(bf16[1024,1024]{1,0:T(8,128)(2,1)} %w_ref), channel_id=1, source_target_pairs={{0,2},{2,0},{1,3},{3,1},{4,6},{6,4},{5,7},{7,5},{8,10},{10,8},{9,1... | collective-permute-start | bytes 6291464 | tf_op jit(solution)/shard_map/ppermute | solution.py:256
  68.9 3.8 %copy-start.2 = (bf16[16,16,1024]{2,1,0:T(8,128)(2,1)}, bf16[16,16,1024]{2,1,0:T(8,128)(2,1)S(1)}, u32[]{:S(2)}) copy-start(bf16[16,16,1024]{2,1,0:T(8,128)(2,1)S(1)} %all_to_all.35) | copy-start | bytes 1572868
  70.7 14.5 %copy-start.5 = (bf16[256,1024]{1,0:T(8,128)(2,1)S(1)}, bf16[256,1024]{1,0:T(8,128)(2,1)}, u32[]{:S(2)}) copy-start(bf16[256,1024]{1,0:T(8,128)(2,1)} %get-tuple-element.63.slot_ref) | copy-start | bytes 1572868
  70.7 14.5 %copy-start.10 = (bf16[256,1024]{1,0:T(8,128)(2,1)S(1)}, bf16[256,1024]{1,0:T(8,128)(2,1)}, u32[]{:S(2)}) copy-start(bf16[256,1024]{1,0:T(8,128)(2,1)} %get-tuple-element.64.slot2_ref) | copy-start | bytes 1572868
  72.7 12.5 %collective-permute-start.3 = (bf16[1024,1024]{1,0:T(8,128)(2,1)S(1)}, bf16[1024,1024]{1,0:T(8,128)(2,1)S(1)}, u32[]{:S(2)}, u32[]{:S(2)}) collective-permute-start(bf16[1024,1024]{1,0:T(8,128)(2,1)S(1)} %copy-done.1), channel_id=1, source_target_pairs={{0,2},{2,0},{1,3},{3,1},{4,6},{6,4},{5,7},{7,5},{8,10},{10,8},{9,1... | collective-permute-start | bytes 6291464 | tf_op jit(solution)/shard_map/ppermute | solution.py:256
  89.5 7.8 %copy-start.11 = (f32[128,128]{1,0:T(8,128)}, f32[128,128]{1,0:T(8,128)S(1)}, u32[]{:S(2)}) copy-start(f32[128,128]{1,0:T(8,128)S(1)} %get-tuple-element.70.packed_ref) | copy-start | bytes 196612
  89.5 43.3 %collective-permute-start.7 = (bf16[1024,1024]{1,0:T(8,128)(2,1)S(1)}, bf16[1024,1024]{1,0:T(8,128)(2,1)}, u32[]{:S(2)}, u32[]{:S(2)}) collective-permute-start(bf16[1024,1024]{1,0:T(8,128)(2,1)S(1)} %copy-done.1), channel_id=1, source_target_pairs={{0,2},{2,0},{1,3},{3,1},{4,6},{6,4},{5,7},{7,5},{8,10},{10,8},{9,1... | collective-permute-start | bytes 6291464 | tf_op jit(solution)/shard_map/ppermute | solution.py:256
  90.3 20.7 %all-to-all-start.4 = ((bf16[16,16,1024]{2,1,0:T(8,128)(2,1)}), bf16[16,16,1024]{2,1,0:T(8,128)(2,1)}, u32[]{:S(2)}, u32[]{:S(2)}) async-start(bf16[16,16,1024]{2,1,0:T(8,128)(2,1)} %bitcast.21), calls=%async_computation.4 | async-start | bytes 1048576 | tf_op jit(solution)/shard_map/all_to_all | solution.py:260
  95.0 2.2 %collective-permute-start.5 = (bf16[256,1024]{1,0:T(8,128)(2,1)}, bf16[256,1024]{1,0:T(8,128)(2,1)S(1)}, u32[]{:S(2)}, u32[]{:S(2)}) collective-permute-start(bf16[256,1024]{1,0:T(8,128)(2,1)} %get-tuple-element.64.slot2_ref), channel_id=1, source_target_pairs={{0,2},{2,0},{1,3},{3,1},{4,6},{6,4},{5,7},{7,5},{8,10},{10,8},{9,1... | collective-permute-start | bytes 1572872 | tf_op jit(solution)/shard_map/ppermute | solution.py:256
  95.4 6.9 %collective-permute-start.6 = (bf16[256,1024]{1,0:T(8,128)(2,1)}, bf16[256,1024]{1,0:T(8,128)(2,1)}, u32[]{:S(2)}, u32[]{:S(2)}) collective-permute-start(bf16[256,1024]{1,0:T(8,128)(2,1)} %bitcast.19), channel_id=1, source_target_pairs={{0,2},{2,0},{1,3},{3,1},{4,6},{6,4},{5,7},{7,5},{8,10},{10,8},{9,1... | collective-permute-start | bytes 1572872 | tf_op jit(solution)/shard_map/ppermute | solution.py:256
  95.6 1.6 %collective-permute-start.4 = (f32[128,128]{1,0:T(8,128)S(1)}, f32[128,128]{1,0:T(8,128)S(1)}, u32[]{:S(2)}, u32[]{:S(2)}) collective-permute-start(f32[128,128]{1,0:T(8,128)S(1)} %get-tuple-element.70.packed_ref), channel_id=1, source_target_pairs={{0,2},{2,0},{1,3},{3,1},{4,6},{6,4},{5,7},{7,5},{8,10},{10,8},{9,1... | collective-permute-start | bytes 196616 | tf_op jit(solution)/shard_map/ppermute | solution.py:256
  137.3 6.7 %collective-permute-start.8 = (bf16[256,1024]{1,0:T(8,128)(2,1)}, bf16[256,1024]{1,0:T(8,128)(2,1)S(1)}, u32[]{:S(2)}, u32[]{:S(2)}) collective-permute-start(bf16[256,1024]{1,0:T(8,128)(2,1)} %bitcast.13.x_ref.grad_ref), channel_id=1, source_target_pairs={{0,2},{2,0},{1,3},{3,1},{4,6},{6,4},{5,7},{7,5},{8,10},{10,8},{9,1... | collective-permute-start | bytes 1572872 | tf_op jit(solution)/shard_map/ppermute | solution.py:256
  140.6 10.2 %all-to-all-start.6 = ((bf16[8,128,128]{2,1,0:T(8,128)(2,1)}), bf16[8,128,128]{2,1,0:T(8,128)(2,1)S(1)}, u32[]{:S(2)}, u32[]{:S(2)}) async-start(bf16[8,128,128]{2,1,0:T(8,128)(2,1)} %shard_map.112), calls=%async_computation.6 | async-start | bytes 524288 | tf_op jit(solution)/shard_map/all_to_all | solution.py:260
  144.0 7.6 %copy-start.3 = (bf16[16,16,1024]{2,1,0:T(8,128)(2,1)S(1)}, bf16[16,16,1024]{2,1,0:T(8,128)(2,1)}, u32[]{:S(2)}) copy-start(bf16[16,16,1024]{2,1,0:T(8,128)(2,1)} %copy-done.2) | copy-start | bytes 1572868
  144.0 7.6 %copy-start.6 = (bf16[256,1024]{1,0:T(8,128)(2,1)S(1)}, bf16[256,1024]{1,0:T(8,128)(2,1)}, u32[]{:S(2)}) copy-start(bf16[256,1024]{1,0:T(8,128)(2,1)} %get-tuple-element.63.slot_ref) | copy-start | bytes 1572868
  148.9 4.8 %copy-start.8 = (bf16[256,1024]{1,0:T(8,128)(2,1)S(1)}, bf16[256,1024]{1,0:T(8,128)(2,1)}, u32[]{:S(2)}) copy-start(bf16[256,1024]{1,0:T(8,128)(2,1)} %copy-done.7) | copy-start | bytes 1572868
  150.8 2.9 %collective-permute-start.9 = (bf16[8,128,128]{2,1,0:T(8,128)(2,1)S(1)}, bf16[8,128,128]{2,1,0:T(8,128)(2,1)S(1)}, u32[]{:S(2)}, u32[]{:S(2)}) collective-permute-start(bf16[8,128,128]{2,1,0:T(8,128)(2,1)S(1)} %all-to-all-done.6.parts_ref), channel_id=1, source_target_pairs={{0,2},{2,0},{1,3},{3,1},{4,6},{6,4},{5,7},{7,5},{8,10},{10,8},{9,1... | collective-permute-start | bytes 786440 | tf_op jit(solution)/shard_map/ppermute | solution.py:256
  (7 other events, 7.4 us)

commit v5 on v4

--- a/solution.py
+++ b/solution.py
@@ -19,7 +19,7 @@
 MIB = 1024 * 1024
 SMALL, MIDDLE, MOST = 12, 24, 24
 COPIES = pltpu.SemaphoreType.DMA
-ROW_BLOCKS = 4
+ROW_BLOCKS = 8
 FEATURES = ("section", "tok")
 COLUMN = ("yh", "z")
 CORE, TOK, FIRST, FIRST2 = range(4)
@@ -318,7 +318,11 @@
     share, all_shares = spec(*shares[1:]), spec(*shares)
     bias_row, decoder_bias = encoder_bias[None], decoder_bias[None]
 
-    part, wide, bias_row = lax.optimization_barrier((part, wide, bias_row))
+    part, wide, encoder_weight, decoder_weight, bias_row = lax.optimization_barrier(
+        (part, wide, encoder_weight, decoder_weight, bias_row)
+    )
+    encoder_weight2, decoder_weight2 = swap(encoder_weight), swap(decoder_weight)
+    bias_row2 = swap(bias_row)
     slot, slot2 = call(
         find_kernel,
         (HERE,),
@@ -327,7 +331,6 @@
         [pltpu.VMEM((2, rows, latents), jnp.int32)],
         4 * picks * rows * latents,
     )
-    bias_row2 = swap(bias_row)
     parts, slot, slot2, bias_row2 = lax.optimization_barrier(
         (exchange(part.reshape(shares), COLUMN), slot, slot2, bias_row2)
     )
@@ -338,8 +341,8 @@
         (at, parts, decoder_bias),
         vmem=SMALL,
     )
-    out, encoder_weight = lax.optimization_barrier((out, encoder_weight))
-    encoder_weight2 = swap(encoder_weight)
+    out, weight, weight2 = lax.optimization_barrier((out, encoder_weight, encoder_weight2))
+    weight, weight2 = swap(weight2), swap(weight)
     shifted = exchange(out, COLUMN).reshape(rows, width)
 
     flops = 4 * rows * width * latents
@@ -359,9 +362,11 @@
         )
         return packed
 
-    encoded = chosen_product(0, shifted, encoder_weight, encoder_weight2)
-    encoded, shifted, weight = lax.optimization_barrier((encoded, shifted, decoder_weight))
-    weight2 = swap(weight)
+    encoded = chosen_product(0, shifted, weight, weight2)
+    encoded, shifted, weight, weight2 = lax.optimization_barrier(
+        (encoded, shifted, decoder_weight, decoder_weight2)
+    )
+    weight, weight2 = swap(weight2), swap(weight)
     shifted2, other_slot = swap(shifted), swap(slot2)
     encoded = exchange(encoded, FEATURES)
     packed, part = call(
@@ -379,8 +384,7 @@
         moved,
         MOST,
     )
-    part, packed, decoder_weight = lax.optimization_barrier((part, packed, decoder_weight))
-    decoder_weight2 = swap(decoder_weight)
+    part, packed = lax.optimization_barrier((part, packed))
     codes, codes2 = call(
         codes_kernel,
         (HERE,) * 5,
@@ -397,9 +401,11 @@
         (at, parts, decoder_bias, whitened),
         vmem=SMALL,
     )
+    out, weight, weight2 = lax.optimization_barrier((out, decoder_weight, decoder_weight2))
+    weight, weight2 = swap(weight2), swap(weight)
     grad = exchange(out, COLUMN).reshape(rows, width)
 
-    packed = chosen_product(1, grad, decoder_weight, decoder_weight2)
+    packed = chosen_product(1, grad, weight, weight2)
     packed, grad = lax.optimization_barrier((packed, grad))
     (decoder_grad,) = call(
         decoder_grad_kernel,

time: 159 us -> 154 us (0.969)
  local copies, waits for them, and re-layouts: 7.24 us -> 2.52 us
  starting transfers between devices: 39.3 us -> 43.8 us
  Pallas kernels: 41.2 us -> 39.3 us
  blocking collectives: 50 us -> 48.3 us
    ppermute x10 -> x15, starting transfers between devices: 14.7 us -> 19.7 us  [swap(): return lax.ppermute(x, 'core', [(0, 1), (1, 0)])]
    unnamed x34 -> x32, local copies, waits for them, and re-layouts: 5.44 us -> 0.71 us
    pallas_call x13, Pallas kernels: 41.2 us -> 39.3 us  [call(): pl.pallas_call(kernel, in_specs=list(ins), out_specs=tuple((place for pla...]
    all_to_all x3, blocking collectives: 50 us -> 48.3 us  [exchange(): return lax.all_to_all(x, axes, 0, 0)]
    ppermute x10 -> x15, waiting for transfers between devices: 2.88 us -> 3.43 us  [swap(): return lax.ppermute(x, 'core', [(0, 1), (1, 0)])]
  transfers between devices with their start and end apart: 14 -> 19, of which waited for: 6 -> 7; matrix products, arithmetic and copies ran while one was open for 1% -> 1% of each run, Pallas kernels for 16% -> 17%
where the time goes in v5:
time: 154 us; the launch traced here: 153 us
  blocking collectives  48.3 us (31%)
  starting transfers between devices  43.8 us (28%)
  Pallas kernels  39.3 us (26%)
  waiting for transfers between devices  17.3 us (11%)
  local copies, waits for them, and re-layouts  2.52 us (2%)
    all_to_all x3, blocking collectives, exchange(): return lax.all_to_all(x, axes, 0, 0)  48.3 us
    pallas_call x13, Pallas kernels, call(): pl.pallas_call(kernel, in_specs=list(ins), out_specs=tuple((place for pla...  39.3 us
    all_to_all x4, starting transfers between devices, exchange(): return lax.all_to_all(x, axes, 0, 0)  24.1 us
    ppermute x15, starting transfers between devices, swap(): return lax.ppermute(x, 'core', [(0, 1), (1, 0)])  19.7 us
    all_to_all x4, waiting for transfers between devices, exchange(): return lax.all_to_all(x, axes, 0, 0)  13.8 us
    ppermute x15, waiting for transfers between devices, swap(): return lax.ppermute(x, 'core', [(0, 1), (1, 0)])  3.43 us
  transfers between devices with their start and end apart: 19, of which 7 were waited for; matrix products, arithmetic and copies ran while one was open for 1% of the time, Pallas kernels for 17%

profile of v5, /device:TPU:1, one launch (start us, length us, event | category | flops | bytes accessed | tf_op | source)
XLA Modules:
  0.0 153.3 jit_solution(17457296883999626017)
XLA Ops:
  2.2 5.9 %all-to-all-start = ((bf16[8,64,256]{2,1,0:T(8,128)(2,1)}), bf16[8,64,256]{2,1,0:T(8,128)(2,1)S(1)}, u32[]{:S(2)}, u32[]{:S(2)}) async-start(bf16[8,64,256]{2,1,0:T(8,128)(2,1)} %broadcast_in_dim.16), calls=%async_computation | async-start | bytes 524288 | tf_op jit(solution)/shard_map/all_to_all | solution.py:260
  9.9 4.4 %all-to-all-done = bf16[8,64,256]{2,1,0:T(8,128)(2,1)S(1)} async-done(((bf16[8,64,256]{2,1,0:T(8,128)(2,1)}), bf16[8,64,256]{2,1,0:T(8,128)(2,1)S(1)}, u32[]{:S(2)}, u32[]{:S(2)}) %all-to-all-start) | async-done | bytes 262176 | tf_op jit(solution)/shard_map/all_to_all | solution.py:260
  14.7 2.0 %collective-permute-start = (bf16[256,1024]{1,0:T(8,128)(2,1)S(1)}, bf16[256,1024]{1,0:T(8,128)(2,1)S(1)}, u32[]{:S(2)}, u32[]{:S(2)}) collective-permute-start(bf16[256,1024]{1,0:T(8,128)(2,1)S(1)} %shard_map.104), channel_id=1, source_target_pairs={{0,2},{2,0},{1,3},{3,1},{4,6},{6,4},{5,7},{7,5},{8,10},{10,8},{9,1... | collective-permute-start | bytes 1572872 | tf_op jit(solution)/shard_map/ppermute | solution.py:256
  19.9 10.6 %all-to-all-start.1 = ((bf16[16,16,1024]{2,1,0:T(8,128)(2,1)}), bf16[16,16,1024]{2,1,0:T(8,128)(2,1)S(1)}, u32[]{:S(2)}, u32[]{:S(2)}) async-start(bf16[16,16,1024]{2,1,0:T(8,128)(2,1)} %bitcast.9), calls=%async_computation.1 | async-start | bytes 1048576 | tf_op jit(solution)/shard_map/all_to_all | solution.py:260
  31.1 13.5 %shard_map.106 = (bf16[256,1024]{1,0:T(8,128)(2,1)}, bf16[256,1024]{1,0:T(8,128)(2,1)}) custom-call(s32[256,128]{1,0:T(8,128)} %copy-done.12), custom_call_target="tpu_custom_call" | custom-call | flops 67108864 | bytes 1048576 | tf_op jit(solution)/shard_map/pallas_call | solution.py:33
  46.5 2.7 %collective-permute-start.3 = (bf16[1024,1024]{1,0:T(8,128)(2,1)}, bf16[1024,1024]{1,0:T(8,128)(2,1)S(1)}, u32[]{:S(2)}, u32[]{:S(2)}) collective-permute-start(bf16[1024,1024]{1,0:T(8,128)(2,1)} %collective-permute-done.2), channel_id=1, source_target_pairs={{0,2},{2,0},{1,3},{3,1},{4,6},{6,4},{5,7},{7,5},{8,10},{10,8},{9,1... | collective-permute-start | bytes 6291464 | tf_op jit(solution)/shard_map/ppermute | solution.py:256
  49.7 20.1 %all_to_all.35 = bf16[16,16,1024]{2,1,0:T(8,128)(2,1)S(1)} all-to-all(bf16[16,16,1024]{2,1,0:T(8,128)(2,1)S(1)} %get-tuple-element.66), channel_id=1, replica_groups=mesh['section'=4,'yh'=2,'z'=8,'core'=2,'tok'=2] {'yh','z'}, dimensions={0} | all-to-all | bytes 1048576 | tf_op jit(solution)/shard_map/all_to_all | solution.py:260
  69.8 2.0 %shard_map.108 = bf16[8,128,128]{2,1,0:T(8,128)(2,1)S(1)} custom-call(bf16[256,1024]{1,0:T(8,128)(2,1)S(1)} %bitcast.21, s32[128,128]{1,0:T(8,128)S(1)} %get-tuple-element.67.place_ref, bf16[1024,1024]{1,0:T(8,128)(2,1)S(1)} %collective-permute-done.3.w_ref, bf16[1024,1024]{1,0:T(8,128)(2,1)S(1)} %collective-permute-done.4.w2_ref), custom_call_target="tpu_custom_call" | custom-call | flops 1073741824 | bytes 4194304 | tf_op jit(solution)/shard_map/pallas_call | solution.py:33
  71.8 3.2 %collective-permute-start.6 = (bf16[1024,1024]{1,0:T(8,128)(2,1)S(1)}, bf16[1024,1024]{1,0:T(8,128)(2,1)S(1)}, u32[]{:S(2)}, u32[]{:S(2)}) collective-permute-start(bf16[1024,1024]{1,0:T(8,128)(2,1)S(1)} %collective-permute-done.5), channel_id=1, source_target_pairs={{0,2},{2,0},{1,3},{3,1},{4,6},{6,4},{5,7},{7,5},{8,10},{10,8},{9,1... | collective-permute-start | bytes 6291464 | tf_op jit(solution)/shard_map/ppermute | solution.py:256
  75.2 8.8 %all_to_all.36.parts_ref = bf16[8,128,128]{2,1,0:T(8,128)(2,1)S(1)} all-to-all(bf16[8,128,128]{2,1,0:T(8,128)(2,1)S(1)} %shard_map.108), channel_id=1, replica_groups=mesh['section'=4,'yh'=2,'z'=8,'core'=2,'tok'=2] {'section','tok'}, dimensions={0} | all-to-all | bytes 524288 | tf_op jit(solution)/shard_map/all_to_all | solution.py:260
  84.0 4.3 %shard_map.109 = (f32[128,128]{1,0:T(8,128)S(1)}, bf16[256,1024]{1,0:T(8,128)(2,1)}) custom-call(bf16[8,128,128]{2,1,0:T(8,128)(2,1)S(1)} %all_to_all.36.parts_ref, bf16[256,1024]{1,0:T(8,128)(2,1)S(1)} %copy-done.2, bf16[256,1024]{1,0:T(8,128)(2,1)S(1)} %copy-done.8, f32[1,1024]{1,0:T(1,128)S(1)} %bitcast.28, ...), custom_call_target="tpu_custom_call" | custom-call | flops 1073741824 | bytes 4194304 | tf_op jit(solution)/shard_map/pallas_call | solution.py:33
  88.3 4.2 %all-to-all-start.4 = ((bf16[16,16,1024]{2,1,0:T(8,128)(2,1)}), bf16[16,16,1024]{2,1,0:T(8,128)(2,1)S(1)}, u32[]{:S(2)}, u32[]{:S(2)}) async-start(bf16[16,16,1024]{2,1,0:T(8,128)(2,1)} %bitcast.12), calls=%async_computation.4 | async-start | bytes 1048576 | tf_op jit(solution)/shard_map/all_to_all | solution.py:260
  92.5 2.2 %collective-permute-start.9 = (bf16[256,1024]{1,0:T(8,128)(2,1)S(1)}, bf16[256,1024]{1,0:T(8,128)(2,1)S(1)}, u32[]{:S(2)}, u32[]{:S(2)}) collective-permute-start(bf16[256,1024]{1,0:T(8,128)(2,1)S(1)} %copy-done.8), channel_id=1, source_target_pairs={{0,2},{2,0},{1,3},{3,1},{4,6},{6,4},{5,7},{7,5},{8,10},{10,8},{9,1... | collective-permute-start | bytes 1572872 | tf_op jit(solution)/shard_map/ppermute | solution.py:256
  97.7 3.6 %shard_map.110 = (bf16[256,1024]{1,0:T(8,128)(2,1)}, bf16[256,1024]{1,0:T(8,128)(2,1)}) custom-call(f32[128,128]{1,0:T(8,128)} %copy-done.9, f32[128,128]{1,0:T(8,128)} %copy-done.13, bf16[256,1024]{1,0:T(8,128)(2,1)} %get-tuple-element.72.slot_ref, bf16[256,1024]{1,0:T(8,128)(2,1)} %copy-done.4, f32[1,1024]{1,0:T(1,128)} %bitcast.26), custom_call_target="tpu_custom_call" | custom-call | bytes 1048576 | tf_op jit(solution)/shard_map/pallas_call | solution.py:33
  101.3 5.5 %all-to-all-done.4.parts_ref = bf16[16,16,1024]{2,1,0:T(8,128)(2,1)S(1)} async-done(((bf16[16,16,1024]{2,1,0:T(8,128)(2,1)}), bf16[16,16,1024]{2,1,0:T(8,128)(2,1)S(1)}, u32[]{:S(2)}, u32[]{:S(2)}) %all-to-all-start.4) | async-done | bytes 524320 | tf_op jit(solution)/shard_map/all_to_all | solution.py:260
  107.5 3.3 %collective-permute-start.11 = (bf16[1024,1024]{1,0:T(8,128)(2,1)}, bf16[1024,1024]{1,0:T(8,128)(2,1)S(1)}, u32[]{:S(2)}, u32[]{:S(2)}) collective-permute-start(bf16[1024,1024]{1,0:T(8,128)(2,1)} %copy-done.15), channel_id=1, source_target_pairs={{0,2},{2,0},{1,3},{3,1},{4,6},{6,4},{5,7},{7,5},{8,10},{10,8},{9,1... | collective-permute-start | bytes 6291464 | tf_op jit(solution)/shard_map/ppermute | solution.py:256
  110.9 19.4 %all_to_all.37 = bf16[16,16,1024]{2,1,0:T(8,128)(2,1)S(1)} all-to-all(bf16[16,16,1024]{2,1,0:T(8,128)(2,1)S(1)} %shard_map.111), channel_id=1, replica_groups=mesh['section'=4,'yh'=2,'z'=8,'core'=2,'tok'=2] {'yh','z'}, dimensions={0} | all-to-all | bytes 1048576 | tf_op jit(solution)/shard_map/all_to_all | solution.py:260
  130.3 2.8 %shard_map.112 = bf16[8,128,128]{2,1,0:T(8,128)(2,1)} custom-call(bf16[256,1024]{1,0:T(8,128)(2,1)S(1)} %bitcast.18, s32[128,128]{1,0:T(8,128)S(1)} %get-tuple-element.67.place_ref, bf16[1024,1024]{1,0:T(8,128)(2,1)S(1)} %collective-permute-done.11.w_ref, bf16[1024,1024]{1,0:T(8,128)(2,1)S(1)} %collective-permute-done.12.w2_ref), custom_call_target="tpu_custom_call" | custom-call | flops 1073741824 | bytes 4194304 | tf_op jit(solution)/shard_map/pallas_call | solution.py:33
  133.1 3.2 %collective-permute-start.13 = (bf16[256,1024]{1,0:T(8,128)(2,1)S(1)}, bf16[256,1024]{1,0:T(8,128)(2,1)}, u32[]{:S(2)}, u32[]{:S(2)}) collective-permute-start(bf16[256,1024]{1,0:T(8,128)(2,1)S(1)} %bitcast.19), channel_id=1, source_target_pairs={{0,2},{2,0},{1,3},{3,1},{4,6},{6,4},{5,7},{7,5},{8,10},{10,8},{9,1... | collective-permute-start | bytes 1572872 | tf_op jit(solution)/shard_map/ppermute | solution.py:256
  136.3 3.4 %all-to-all-start.6 = ((bf16[8,128,128]{2,1,0:T(8,128)(2,1)}), bf16[8,128,128]{2,1,0:T(8,128)(2,1)S(1)}, u32[]{:S(2)}, u32[]{:S(2)}) async-start(bf16[8,128,128]{2,1,0:T(8,128)(2,1)} %shard_map.112), calls=%async_computation.6 | async-start | bytes 524288 | tf_op jit(solution)/shard_map/all_to_all | solution.py:260
  139.8 4.2 %shard_map.113 = bf16[1024,1024]{1,0:T(8,128)(2,1)} custom-call(bf16[256,1024]{1,0:T(8,128)(2,1)} %get-tuple-element.90.codes_ref, bf16[256,1024]{1,0:T(8,128)(2,1)} %get-tuple-element.91.codes2_ref, bf16[256,1024]{1,0:T(8,128)(2,1)} %bitcast.20, bf16[256,1024]{1,0:T(8,128)(2,1)} %collective-permute-done.13.grad2_ref), custom_call_target="tpu_custom_call" | custom-call | flops 1073741824 | bytes 4194304 | tf_op jit(solution)/shard_map/pallas_call | solution.py:33
  144.0 2.6 %all-to-all-done.6.parts_ref = bf16[8,128,128]{2,1,0:T(8,128)(2,1)S(1)} async-done(((bf16[8,128,128]{2,1,0:T(8,128)(2,1)}), bf16[8,128,128]{2,1,0:T(8,128)(2,1)S(1)}, u32[]{:S(2)}, u32[]{:S(2)}) %all-to-all-start.6) | async-done | bytes 262176 | tf_op jit(solution)/shard_map/all_to_all | solution.py:260
  147.4 2.1 %shard_map.114 = (f32[1024,1024]{1,0:T(8,128)S(1)}, f32[1,512]{1,0:T(1,128)S(1)}) custom-call(s32[4]{0:T(128)S(1)} %pad_add_fusion.at_ref, bf16[8,128,128]{2,1,0:T(8,128)(2,1)S(1)} %all-to-all-done.6.parts_ref, bf16[256,1024]{1,0:T(8,128)(2,1)S(1)} %copy-done.3, bf16[256,1024]{1,0:T(8,128)(2,1)S(1)} %bitcast.23), custom_call_target="tpu_custom_call" | custom-call | flops 1073741824 | bytes 4194304 | tf_op jit(solution)/shard_map/pallas_call | solution.py:33
  149.5 3.6 %shard_map.115 = (bf16[1024,1024]{1,0:T(8,128)(2,1)}, f32[1,512]{1,0:T(1,128)}) custom-call(s32[4]{0:T(128)S(1)} %pad_add_fusion.at_ref, bf16[8,128,128]{2,1,0:T(8,128)(2,1)S(1)} %collective-permute-done.14.parts_ref, bf16[256,1024]{1,0:T(8,128)(2,1)S(1)} %copy-done.5, bf16[256,1024]{1,0:T(8,128)(2,1)S(1)} %copy-done.7, ...), custom_call_target="tpu_custom_call" | custom-call | flops 1073741824 | bytes 4194304 | tf_op jit(solution)/shard_map/pallas_call | solution.py:33
  (68 shorter events, 14.6 us)
Async XLA Ops:
  2.2 12.2 %all-to-all-start = ((bf16[8,64,256]{2,1,0:T(8,128)(2,1)}), bf16[8,64,256]{2,1,0:T(8,128)(2,1)S(1)}, u32[]{:S(2)}, u32[]{:S(2)}) async-start(bf16[8,64,256]{2,1,0:T(8,128)(2,1)} %broadcast_in_dim.16), calls=%async_computation | async-start | bytes 524288 | tf_op jit(solution)/shard_map/all_to_all | solution.py:260
  14.4 16.1 %copy-start.11 = (f32[1024]{0:T(1024)S(1)}, f32[1024]{0:T(1024)}, u32[]{:S(2)}) copy-start(f32[1024]{0:T(1024)} %param.13) | copy-start | bytes 12292
  14.4 31.4 %copy-start.10 = (f32[2048]{0:T(1024)S(1)}, f32[2048]{0:T(1024)}, u32[]{:S(2)}) copy-start(f32[2048]{0:T(1024)} %param.11) | copy-start | bytes 24580
  14.7 3.6 %collective-permute-start = (bf16[256,1024]{1,0:T(8,128)(2,1)S(1)}, bf16[256,1024]{1,0:T(8,128)(2,1)S(1)}, u32[]{:S(2)}, u32[]{:S(2)}) collective-permute-start(bf16[256,1024]{1,0:T(8,128)(2,1)S(1)} %shard_map.104), channel_id=1, source_target_pairs={{0,2},{2,0},{1,3},{3,1},{4,6},{6,4},{5,7},{7,5},{8,10},{10,8},{9,1... | collective-permute-start | bytes 1572872 | tf_op jit(solution)/shard_map/ppermute | solution.py:256
  19.4 27.1 %collective-permute-start.2 = (bf16[1024,1024]{1,0:T(8,128)(2,1)}, bf16[1024,1024]{1,0:T(8,128)(2,1)}, u32[]{:S(2)}, u32[]{:S(2)}) collective-permute-start(bf16[1024,1024]{1,0:T(8,128)(2,1)} %param.12), channel_id=1, source_target_pairs={{0,2},{2,0},{1,3},{3,1},{4,6},{6,4},{5,7},{7,5},{8,10},{10,8},{9,1... | collective-permute-start | bytes 6291464 | tf_op jit(solution)/shard_map/ppermute | solution.py:256
  19.9 25.9 %all-to-all-start.1 = ((bf16[16,16,1024]{2,1,0:T(8,128)(2,1)}), bf16[16,16,1024]{2,1,0:T(8,128)(2,1)S(1)}, u32[]{:S(2)}, u32[]{:S(2)}) async-start(bf16[16,16,1024]{2,1,0:T(8,128)(2,1)} %bitcast.9), calls=%async_computation.1 | async-start | bytes 1048576 | tf_op jit(solution)/shard_map/all_to_all | solution.py:260
  30.5 14.0 %collective-permute-start.1 = (f32[1,1024]{1,0:T(1,128)S(1)}, f32[1,1024]{1,0:T(1,128)S(1)}, u32[]{:S(2)}, u32[]{:S(2)}) collective-permute-start(f32[1,1024]{1,0:T(1,128)S(1)} %bitcast.27), channel_id=1, source_target_pairs={{0,2},{2,0},{1,3},{3,1},{4,6},{6,4},{5,7},{7,5},{8,10},{10,8},{9,1... | collective-permute-start | bytes 12296 | tf_op jit(solution)/shard_map/ppermute | solution.py:256
  46.5 23.3 %collective-permute-start.3 = (bf16[1024,1024]{1,0:T(8,128)(2,1)}, bf16[1024,1024]{1,0:T(8,128)(2,1)S(1)}, u32[]{:S(2)}, u32[]{:S(2)}) collective-permute-start(bf16[1024,1024]{1,0:T(8,128)(2,1)} %collective-permute-done.2), channel_id=1, source_target_pairs={{0,2},{2,0},{1,3},{3,1},{4,6},{6,4},{5,7},{7,5},{8,10},{10,8},{9,1... | collective-permute-start | bytes 6291464 | tf_op jit(solution)/shard_map/ppermute | solution.py:256
  49.2 20.6 %collective-permute-start.4 = (bf16[1024,1024]{1,0:T(8,128)(2,1)}, bf16[1024,1024]{1,0:T(8,128)(2,1)S(1)}, u32[]{:S(2)}, u32[]{:S(2)}) collective-permute-start(bf16[1024,1024]{1,0:T(8,128)(2,1)} %param.12), channel_id=1, source_target_pairs={{0,2},{2,0},{1,3},{3,1},{4,6},{6,4},{5,7},{7,5},{8,10},{10,8},{9,1... | collective-permute-start | bytes 6291464 | tf_op jit(solution)/shard_map/ppermute | solution.py:256
  49.3 22.5 %collective-permute-start.5 = (bf16[1024,1024]{1,0:T(8,128)(2,1)}, bf16[1024,1024]{1,0:T(8,128)(2,1)S(1)}, u32[]{:S(2)}, u32[]{:S(2)}) collective-permute-start(bf16[1024,1024]{1,0:T(8,128)(2,1)} %param.14), channel_id=1, source_target_pairs={{0,2},{2,0},{1,3},{3,1},{4,6},{6,4},{5,7},{7,5},{8,10},{10,8},{9,1... | collective-permute-start | bytes 6291464 | tf_op jit(solution)/shard_map/ppermute | solution.py:256
  69.8 14.2 %copy-start.2 = (bf16[256,1024]{1,0:T(8,128)(2,1)S(1)}, bf16[256,1024]{1,0:T(8,128)(2,1)}, u32[]{:S(2)}) copy-start(bf16[256,1024]{1,0:T(8,128)(2,1)} %get-tuple-element.72.slot_ref) | copy-start | bytes 1572868
  71.8 16.5 %copy-start.15 = (bf16[1024,1024]{1,0:T(8,128)(2,1)}, bf16[1024,1024]{1,0:T(8,128)(2,1)S(1)}, u32[]{:S(2)}) copy-start(bf16[1024,1024]{1,0:T(8,128)(2,1)S(1)} %collective-permute-done.5) | copy-start | bytes 6291460
  71.8 12.2 %collective-permute-start.6 = (bf16[1024,1024]{1,0:T(8,128)(2,1)S(1)}, bf16[1024,1024]{1,0:T(8,128)(2,1)S(1)}, u32[]{:S(2)}, u32[]{:S(2)}) collective-permute-start(bf16[1024,1024]{1,0:T(8,128)(2,1)S(1)} %collective-permute-done.5), channel_id=1, source_target_pairs={{0,2},{2,0},{1,3},{3,1},{4,6},{6,4},{5,7},{7,5},{8,10},{10,8},{9,1... | collective-permute-start | bytes 6291464 | tf_op jit(solution)/shard_map/ppermute | solution.py:256
  75.1 8.9 %collective-permute-start.7 = (bf16[1024,1024]{1,0:T(8,128)(2,1)S(1)}, bf16[1024,1024]{1,0:T(8,128)(2,1)S(1)}, u32[]{:S(2)}, u32[]{:S(2)}) collective-permute-start(bf16[1024,1024]{1,0:T(8,128)(2,1)S(1)} %copy-done.14), channel_id=1, source_target_pairs={{0,2},{2,0},{1,3},{3,1},{4,6},{6,4},{5,7},{7,5},{8,10},{10,8},{9,1... | collective-permute-start | bytes 6291464 | tf_op jit(solution)/shard_map/ppermute | solution.py:256
  88.3 18.5 %all-to-all-start.4 = ((bf16[16,16,1024]{2,1,0:T(8,128)(2,1)}), bf16[16,16,1024]{2,1,0:T(8,128)(2,1)S(1)}, u32[]{:S(2)}, u32[]{:S(2)}) async-start(bf16[16,16,1024]{2,1,0:T(8,128)(2,1)} %bitcast.12), calls=%async_computation.4 | async-start | bytes 1048576 | tf_op jit(solution)/shard_map/all_to_all | solution.py:260
  92.5 3.7 %collective-permute-start.9 = (bf16[256,1024]{1,0:T(8,128)(2,1)S(1)}, bf16[256,1024]{1,0:T(8,128)(2,1)S(1)}, u32[]{:S(2)}, u32[]{:S(2)}) collective-permute-start(bf16[256,1024]{1,0:T(8,128)(2,1)S(1)} %copy-done.8), channel_id=1, source_target_pairs={{0,2},{2,0},{1,3},{3,1},{4,6},{6,4},{5,7},{7,5},{8,10},{10,8},{9,1... | collective-permute-start | bytes 1572872 | tf_op jit(solution)/shard_map/ppermute | solution.py:256
  94.7 6.6 %collective-permute-start.10 = (bf16[256,1024]{1,0:T(8,128)(2,1)S(1)}, bf16[256,1024]{1,0:T(8,128)(2,1)S(1)}, u32[]{:S(2)}, u32[]{:S(2)}) collective-permute-start(bf16[256,1024]{1,0:T(8,128)(2,1)S(1)} %bitcast.22), channel_id=1, source_target_pairs={{0,2},{2,0},{1,3},{3,1},{4,6},{6,4},{5,7},{7,5},{8,10},{10,8},{9,1... | collective-permute-start | bytes 1572872 | tf_op jit(solution)/shard_map/ppermute | solution.py:256
  94.8 2.3 %collective-permute-start.8 = (f32[128,128]{1,0:T(8,128)S(1)}, f32[128,128]{1,0:T(8,128)S(1)}, u32[]{:S(2)}, u32[]{:S(2)}) collective-permute-start(f32[128,128]{1,0:T(8,128)S(1)} %get-tuple-element.80.packed_ref), channel_id=1, source_target_pairs={{0,2},{2,0},{1,3},{3,1},{4,6},{6,4},{5,7},{7,5},{8,10},{10,8},{9,1... | collective-permute-start | bytes 196616 | tf_op jit(solution)/shard_map/ppermute | solution.py:256
  101.3 31.8 %copy-start.6 = (bf16[256,1024]{1,0:T(8,128)(2,1)}, bf16[256,1024]{1,0:T(8,128)(2,1)S(1)}, u32[]{:S(2)}) copy-start(bf16[256,1024]{1,0:T(8,128)(2,1)S(1)} %collective-permute-done.10.x_ref) | copy-start | bytes 1572868
  107.5 22.8 %collective-permute-start.11 = (bf16[1024,1024]{1,0:T(8,128)(2,1)}, bf16[1024,1024]{1,0:T(8,128)(2,1)S(1)}, u32[]{:S(2)}, u32[]{:S(2)}) collective-permute-start(bf16[1024,1024]{1,0:T(8,128)(2,1)} %copy-done.15), channel_id=1, source_target_pairs={{0,2},{2,0},{1,3},{3,1},{4,6},{6,4},{5,7},{7,5},{8,10},{10,8},{9,1... | collective-permute-start | bytes 6291464 | tf_op jit(solution)/shard_map/ppermute | solution.py:256
  110.8 19.5 %collective-permute-start.12 = (bf16[1024,1024]{1,0:T(8,128)(2,1)}, bf16[1024,1024]{1,0:T(8,128)(2,1)S(1)}, u32[]{:S(2)}, u32[]{:S(2)}) collective-permute-start(bf16[1024,1024]{1,0:T(8,128)(2,1)} %param.14), channel_id=1, source_target_pairs={{0,2},{2,0},{1,3},{3,1},{4,6},{6,4},{5,7},{7,5},{8,10},{10,8},{9,1... | collective-permute-start | bytes 6291464 | tf_op jit(solution)/shard_map/ppermute | solution.py:256
  133.1 6.7 %collective-permute-start.13 = (bf16[256,1024]{1,0:T(8,128)(2,1)S(1)}, bf16[256,1024]{1,0:T(8,128)(2,1)}, u32[]{:S(2)}, u32[]{:S(2)}) collective-permute-start(bf16[256,1024]{1,0:T(8,128)(2,1)S(1)} %bitcast.19), channel_id=1, source_target_pairs={{0,2},{2,0},{1,3},{3,1},{4,6},{6,4},{5,7},{7,5},{8,10},{10,8},{9,1... | collective-permute-start | bytes 1572872 | tf_op jit(solution)/shard_map/ppermute | solution.py:256
  136.3 10.2 %all-to-all-start.6 = ((bf16[8,128,128]{2,1,0:T(8,128)(2,1)}), bf16[8,128,128]{2,1,0:T(8,128)(2,1)S(1)}, u32[]{:S(2)}, u32[]{:S(2)}) async-start(bf16[8,128,128]{2,1,0:T(8,128)(2,1)} %shard_map.112), calls=%async_computation.6 | async-start | bytes 524288 | tf_op jit(solution)/shard_map/all_to_all | solution.py:260
  146.5 2.9 %collective-permute-start.14 = (bf16[8,128,128]{2,1,0:T(8,128)(2,1)S(1)}, bf16[8,128,128]{2,1,0:T(8,128)(2,1)S(1)}, u32[]{:S(2)}, u32[]{:S(2)}) collective-permute-start(bf16[8,128,128]{2,1,0:T(8,128)(2,1)S(1)} %all-to-all-done.6.parts_ref), channel_id=1, source_target_pairs={{0,2},{2,0},{1,3},{3,1},{4,6},{6,4},{5,7},{7,5},{8,10},{10,8},{9,1... | collective-permute-start | bytes 786440 | tf_op jit(solution)/shard_map/ppermute | solution.py:256
  (11 other events, 64.9 us)

commit v6 on v5

--- a/solution.py
+++ b/solution.py
@@ -62,26 +62,25 @@
     half, picks = rows // 2, LANES // 2
     column = lax.broadcasted_iota(jnp.int32, (8, width), 1)
 
-    def step(i, carry):
+    def step(base, i, carry):
         own = pl.ds(pl.multiple_of(i * 8, 8), 8)
         place = wide_ref[own, :]
         for n in range(2):
             slot = jnp.full((8, width), -1, jnp.int32)
             for k in range(picks):
                 at = n * picks + k
-                slot = jnp.where(place[:, at : at + 1] == column, k, slot)
+                slot = jnp.where(place[:, at : at + 1] == column, base + k, slot)
             found[n, own, :] = slot
         return carry
 
     def pack(i, carry):
         own = pl.ds(pl.multiple_of(i * 16, 16), 16)
-        lane = jnp.where(i * 16 >= half, picks, 0)
         for n, out in enumerate((slot_ref, slot2_ref)):
-            slot = found[n, own, :]
-            out[own, :] = jnp.where(slot >= 0, slot + lane, slot).astype(F32).astype(BF16)
+            out[own, :] = found[n, own, :].astype(F32).astype(BF16)
         return carry
 
-    lax.fori_loop(0, rows // 8, step, 0)
+    lax.fori_loop(0, half // 8, functools.partial(step, 0), 0)
+    lax.fori_loop(half // 8, rows // 8, functools.partial(step, picks), 0)
     lax.fori_loop(0, rows // 16, pack, 0)
 
 
@@ -142,14 +141,11 @@
         out_ref[i] = grad
 
 
-def product_kernel(contract, x_ref, place_ref, w_ref, w2_ref, out_ref, held, sems):
-    copy = start(w_ref, held, sems.at[0])
+def product_kernel(contract, x_ref, place_ref, w_ref, w2_ref, out_ref):
     place = place_ref[...]
     lane, chunk = place & (LANES - 1), place >> 7
     low = high = jnp.zeros(place.shape, F32)
-    for n, weight in ((1, w2_ref), (0, held)):
-        if n == 0:
-            copy.wait()
+    for n, weight in enumerate((w_ref, w2_ref)):
         y = lax.dot_general(
             x_ref[...], weight[...], (((1,), (contract,)), ((), ())), preferred_element_type=F32
         )
@@ -171,30 +167,14 @@
 
 
 def decode_kernel(
-    parts_ref,
-    slot_ref,
-    slot2_ref,
-    bias_ref,
-    bias2_ref,
-    w_ref,
-    w2_ref,
-    packed_ref,
-    out_ref,
-    codes,
-    slots,
-    held,
-    sems,
+    parts_ref, slot_ref, slot2_ref, bias_ref, bias2_ref, w_ref, w2_ref, packed_ref, out_ref, codes
 ):
-    found = [start(slot_ref, slots.at[0], sems.at[1]), start(slot2_ref, slots.at[1], sems.at[2])]
-    copy = start(w_ref, held, sems.at[0])
     packed = sum_of(parts_ref)
     packed_ref[...] = packed
-    for n, bias in enumerate((bias_ref, bias2_ref)):
-        found[n].wait()
-        spread_codes(packed, slots.at[n], bias, codes.at[n])
-    y = jnp.dot(codes[1], w2_ref[...], preferred_element_type=F32)
-    copy.wait()
-    y = y + jnp.dot(codes[0], held[...], preferred_element_type=F32)
+    spread_codes(packed, slot_ref, bias_ref, codes.at[0])
+    spread_codes(packed, slot2_ref, bias2_ref, codes.at[1])
+    y = jnp.dot(codes[0], w_ref[...], preferred_element_type=F32)
+    y = y + jnp.dot(codes[1], w2_ref[...], preferred_element_type=F32)
     out_ref[...] = y.astype(BF16)
 
 
@@ -347,15 +327,14 @@
 
     flops = 4 * rows * width * latents
     moved = 4 * width * latents
-    weight_held = [pltpu.VMEM((width, latents), BF16), COPIES((1,))]
 
     def chosen_product(contract, x, weight, weight2):
         (packed,) = call(
             functools.partial(product_kernel, contract),
-            (HERE, HERE, ANY, HERE),
+            (HERE, HERE, HERE, HERE),
             [(HERE, spec(receivers, rows // 2, LANES))],
             (x, place, weight, weight2),
-            weight_held,
+            (),
             flops,
             moved,
             MOST,
@@ -371,15 +350,10 @@
     encoded = exchange(encoded, FEATURES)
     packed, part = call(
         decode_kernel,
-        (HERE, ANY, ANY, HERE, HERE, ANY, HERE),
+        (HERE,) * 7,
         [(HERE, spec(rows // 2, LANES, dtype=F32)), (HERE, spec(rows, width))],
         (encoded, slot, slot2, bias_row, bias_row2, weight, weight2),
-        [
-            pltpu.VMEM((2, rows, latents), BF16),
-            pltpu.VMEM((2, rows, latents), BF16),
-            pltpu.VMEM((latents, width), BF16),
-            COPIES((3,)),
-        ],
+        [pltpu.VMEM((2, rows, latents), BF16)],
         flops,
         moved,
         MOST,

time: 154 us -> 151 us (0.981)
  Pallas kernels: 39.3 us -> 36.8 us
    pallas_call x13, Pallas kernels: 39.3 us -> 36.8 us  [call(): pl.pallas_call(kernel, in_specs=list(ins), out_specs=tuple((place for pla...]
where the time goes in v6:
time: 151 us
  blocking collectives  48.1 us (32%)
  starting transfers between devices  43.7 us (29%)
  Pallas kernels  36.8 us (24%)
  waiting for transfers between devices  17.5 us (12%)
  local copies, waits for them, and re-layouts  2.52 us (2%)
    all_to_all x3, blocking collectives, exchange(): return lax.all_to_all(x, axes, 0, 0)  48.1 us
    pallas_call x13, Pallas kernels, call(): pl.pallas_call(kernel, in_specs=list(ins), out_specs=tuple((place for pla...  36.8 us
    all_to_all x4, starting transfers between devices, exchange(): return lax.all_to_all(x, axes, 0, 0)  24.1 us
    ppermute x15, starting transfers between devices, swap(): return lax.ppermute(x, 'core', [(0, 1), (1, 0)])  19.6 us
    all_to_all x4, waiting for transfers between devices, exchange(): return lax.all_to_all(x, axes, 0, 0)  14.1 us
    ppermute x15, waiting for transfers between devices, swap(): return lax.ppermute(x, 'core', [(0, 1), (1, 0)])  3.43 us
  transfers between devices with their start and end apart: 19, of which 7 were waited for; matrix products, arithmetic and copies ran while one was open for 1% of the time, Pallas kernels for 17%

profile of v6, /device:TPU:1, one launch (start us, length us, event | category | flops | bytes accessed | tf_op | source)
XLA Modules:
  0.0 150.6 jit_solution(9251553674824768856)
XLA Ops:
  2.2 5.9 %all-to-all-start = ((bf16[8,64,256]{2,1,0:T(8,128)(2,1)}), bf16[8,64,256]{2,1,0:T(8,128)(2,1)S(1)}, u32[]{:S(2)}, u32[]{:S(2)}) async-start(bf16[8,64,256]{2,1,0:T(8,128)(2,1)} %broadcast_in_dim.16), calls=%async_computation | async-start | bytes 524288 | tf_op jit(solution)/shard_map/all_to_all | solution.py:240
  9.9 4.4 %all-to-all-done = bf16[8,64,256]{2,1,0:T(8,128)(2,1)S(1)} async-done(((bf16[8,64,256]{2,1,0:T(8,128)(2,1)}), bf16[8,64,256]{2,1,0:T(8,128)(2,1)S(1)}, u32[]{:S(2)}, u32[]{:S(2)}) %all-to-all-start) | async-done | bytes 262176 | tf_op jit(solution)/shard_map/all_to_all | solution.py:240
  14.7 2.0 %collective-permute-start = (bf16[256,1024]{1,0:T(8,128)(2,1)S(1)}, bf16[256,1024]{1,0:T(8,128)(2,1)S(1)}, u32[]{:S(2)}, u32[]{:S(2)}) collective-permute-start(bf16[256,1024]{1,0:T(8,128)(2,1)S(1)} %shard_map.104), channel_id=1, source_target_pairs={{0,2},{2,0},{1,3},{3,1},{4,6},{6,4},{5,7},{7,5},{8,10},{10,8},{9,1... | collective-permute-start | bytes 1572872 | tf_op jit(solution)/shard_map/ppermute | solution.py:236
  16.8 1.5 %collective-permute-done.add_ref = bf16[256,1024]{1,0:T(8,128)(2,1)S(1)} collective-permute-done((bf16[256,1024]{1,0:T(8,128)(2,1)S(1)}, bf16[256,1024]{1,0:T(8,128)(2,1)S(1)}, u32[]{:S(2)}, u32[]{:S(2)}) %collective-permute-start) | collective-permute-done | bytes 524320 | tf_op jit(solution)/shard_map/ppermute | solution.py:236
  19.9 10.6 %all-to-all-start.1 = ((bf16[16,16,1024]{2,1,0:T(8,128)(2,1)}), bf16[16,16,1024]{2,1,0:T(8,128)(2,1)S(1)}, u32[]{:S(2)}, u32[]{:S(2)}) async-start(bf16[16,16,1024]{2,1,0:T(8,128)(2,1)} %bitcast.9), calls=%async_computation.1 | async-start | bytes 1048576 | tf_op jit(solution)/shard_map/all_to_all | solution.py:240
  31.1 13.3 %shard_map.106 = (bf16[256,1024]{1,0:T(8,128)(2,1)}, bf16[256,1024]{1,0:T(8,128)(2,1)}) custom-call(s32[256,128]{1,0:T(8,128)} %copy-done.12), custom_call_target="tpu_custom_call" | custom-call | flops 67108864 | bytes 1048576 | tf_op jit(solution)/shard_map/pallas_call | solution.py:33
  46.5 2.7 %collective-permute-start.3 = (bf16[1024,1024]{1,0:T(8,128)(2,1)}, bf16[1024,1024]{1,0:T(8,128)(2,1)S(1)}, u32[]{:S(2)}, u32[]{:S(2)}) collective-permute-start(bf16[1024,1024]{1,0:T(8,128)(2,1)} %collective-permute-done.2), channel_id=1, source_target_pairs={{0,2},{2,0},{1,3},{3,1},{4,6},{6,4},{5,7},{7,5},{8,10},{10,8},{9,1... | collective-permute-start | bytes 6291464 | tf_op jit(solution)/shard_map/ppermute | solution.py:236
  49.7 19.9 %all_to_all.35 = bf16[16,16,1024]{2,1,0:T(8,128)(2,1)S(1)} all-to-all(bf16[16,16,1024]{2,1,0:T(8,128)(2,1)S(1)} %get-tuple-element.66), channel_id=1, replica_groups=mesh['section'=4,'yh'=2,'z'=8,'core'=2,'tok'=2] {'yh','z'}, dimensions={0} | all-to-all | bytes 1048576 | tf_op jit(solution)/shard_map/all_to_all | solution.py:240
  71.1 3.2 %collective-permute-start.6 = (bf16[1024,1024]{1,0:T(8,128)(2,1)S(1)}, bf16[1024,1024]{1,0:T(8,128)(2,1)S(1)}, u32[]{:S(2)}, u32[]{:S(2)}) collective-permute-start(bf16[1024,1024]{1,0:T(8,128)(2,1)S(1)} %collective-permute-done.5), channel_id=1, source_target_pairs={{0,2},{2,0},{1,3},{3,1},{4,6},{6,4},{5,7},{7,5},{8,10},{10,8},{9,1... | collective-permute-start | bytes 6291464 | tf_op jit(solution)/shard_map/ppermute | solution.py:236
  74.4 8.8 %all_to_all.36.parts_ref = bf16[8,128,128]{2,1,0:T(8,128)(2,1)S(1)} all-to-all(bf16[8,128,128]{2,1,0:T(8,128)(2,1)S(1)} %shard_map.108), channel_id=1, replica_groups=mesh['section'=4,'yh'=2,'z'=8,'core'=2,'tok'=2] {'section','tok'}, dimensions={0} | all-to-all | bytes 524288 | tf_op jit(solution)/shard_map/all_to_all | solution.py:240
  83.3 3.0 %shard_map.109 = (f32[128,128]{1,0:T(8,128)S(1)}, bf16[256,1024]{1,0:T(8,128)(2,1)}) custom-call(bf16[8,128,128]{2,1,0:T(8,128)(2,1)S(1)} %all_to_all.36.parts_ref, bf16[256,1024]{1,0:T(8,128)(2,1)S(1)} %copy-done.2, bf16[256,1024]{1,0:T(8,128)(2,1)S(1)} %copy-done.8, f32[1,1024]{1,0:T(1,128)S(1)} %bitcast.28, ...), custom_call_target="tpu_custom_call" | custom-call | flops 1073741824 | bytes 4194304 | tf_op jit(solution)/shard_map/pallas_call | solution.py:33
  86.3 4.2 %all-to-all-start.4 = ((bf16[16,16,1024]{2,1,0:T(8,128)(2,1)}), bf16[16,16,1024]{2,1,0:T(8,128)(2,1)S(1)}, u32[]{:S(2)}, u32[]{:S(2)}) async-start(bf16[16,16,1024]{2,1,0:T(8,128)(2,1)} %bitcast.12), calls=%async_computation.4 | async-start | bytes 1048576 | tf_op jit(solution)/shard_map/all_to_all | solution.py:240
  90.5 2.2 %collective-permute-start.9 = (bf16[256,1024]{1,0:T(8,128)(2,1)S(1)}, bf16[256,1024]{1,0:T(8,128)(2,1)S(1)}, u32[]{:S(2)}, u32[]{:S(2)}) collective-permute-start(bf16[256,1024]{1,0:T(8,128)(2,1)S(1)} %copy-done.8), channel_id=1, source_target_pairs={{0,2},{2,0},{1,3},{3,1},{4,6},{6,4},{5,7},{7,5},{8,10},{10,8},{9,1... | collective-permute-start | bytes 1572872 | tf_op jit(solution)/shard_map/ppermute | solution.py:236
  95.7 3.6 %shard_map.110 = (bf16[256,1024]{1,0:T(8,128)(2,1)}, bf16[256,1024]{1,0:T(8,128)(2,1)}) custom-call(f32[128,128]{1,0:T(8,128)} %copy-done.9, f32[128,128]{1,0:T(8,128)} %copy-done.13, bf16[256,1024]{1,0:T(8,128)(2,1)} %get-tuple-element.72.slot_ref, bf16[256,1024]{1,0:T(8,128)(2,1)} %copy-done.4, f32[1,1024]{1,0:T(1,128)} %bitcast.26), custom_call_target="tpu_custom_call" | custom-call | bytes 1048576 | tf_op jit(solution)/shard_map/pallas_call | solution.py:33
  99.2 5.5 %all-to-all-done.4.parts_ref = bf16[16,16,1024]{2,1,0:T(8,128)(2,1)S(1)} async-done(((bf16[16,16,1024]{2,1,0:T(8,128)(2,1)}), bf16[16,16,1024]{2,1,0:T(8,128)(2,1)S(1)}, u32[]{:S(2)}, u32[]{:S(2)}) %all-to-all-start.4) | async-done | bytes 524320 | tf_op jit(solution)/shard_map/all_to_all | solution.py:240
  105.4 3.3 %collective-permute-start.11 = (bf16[1024,1024]{1,0:T(8,128)(2,1)}, bf16[1024,1024]{1,0:T(8,128)(2,1)S(1)}, u32[]{:S(2)}, u32[]{:S(2)}) collective-permute-start(bf16[1024,1024]{1,0:T(8,128)(2,1)} %copy-done.15), channel_id=1, source_target_pairs={{0,2},{2,0},{1,3},{3,1},{4,6},{6,4},{5,7},{7,5},{8,10},{10,8},{9,1... | collective-permute-start | bytes 6291464 | tf_op jit(solution)/shard_map/ppermute | solution.py:236
  108.9 19.4 %all_to_all.37 = bf16[16,16,1024]{2,1,0:T(8,128)(2,1)S(1)} all-to-all(bf16[16,16,1024]{2,1,0:T(8,128)(2,1)S(1)} %shard_map.111), channel_id=1, replica_groups=mesh['section'=4,'yh'=2,'z'=8,'core'=2,'tok'=2] {'yh','z'}, dimensions={0} | all-to-all | bytes 1048576 | tf_op jit(solution)/shard_map/all_to_all | solution.py:240
  128.3 2.2 %shard_map.112 = bf16[8,128,128]{2,1,0:T(8,128)(2,1)} custom-call(bf16[256,1024]{1,0:T(8,128)(2,1)S(1)} %bitcast.18, s32[128,128]{1,0:T(8,128)S(1)} %get-tuple-element.67.place_ref, bf16[1024,1024]{1,0:T(8,128)(2,1)S(1)} %collective-permute-done.11.w_ref, bf16[1024,1024]{1,0:T(8,128)(2,1)S(1)} %collective-permute-done.12.w2_ref), custom_call_target="tpu_custom_call" | custom-call | flops 1073741824 | bytes 4194304 | tf_op jit(solution)/shard_map/pallas_call | solution.py:33
  130.5 3.1 %collective-permute-start.13 = (bf16[256,1024]{1,0:T(8,128)(2,1)S(1)}, bf16[256,1024]{1,0:T(8,128)(2,1)}, u32[]{:S(2)}, u32[]{:S(2)}) collective-permute-start(bf16[256,1024]{1,0:T(8,128)(2,1)S(1)} %bitcast.19), channel_id=1, source_target_pairs={{0,2},{2,0},{1,3},{3,1},{4,6},{6,4},{5,7},{7,5},{8,10},{10,8},{9,1... | collective-permute-start | bytes 1572872 | tf_op jit(solution)/shard_map/ppermute | solution.py:236
  133.6 3.4 %all-to-all-start.6 = ((bf16[8,128,128]{2,1,0:T(8,128)(2,1)}), bf16[8,128,128]{2,1,0:T(8,128)(2,1)S(1)}, u32[]{:S(2)}, u32[]{:S(2)}) async-start(bf16[8,128,128]{2,1,0:T(8,128)(2,1)} %shard_map.112), calls=%async_computation.6 | async-start | bytes 524288 | tf_op jit(solution)/shard_map/all_to_all | solution.py:240
  137.1 4.2 %shard_map.113 = bf16[1024,1024]{1,0:T(8,128)(2,1)} custom-call(bf16[256,1024]{1,0:T(8,128)(2,1)} %get-tuple-element.90.codes_ref, bf16[256,1024]{1,0:T(8,128)(2,1)} %get-tuple-element.91.codes2_ref, bf16[256,1024]{1,0:T(8,128)(2,1)} %bitcast.20, bf16[256,1024]{1,0:T(8,128)(2,1)} %collective-permute-done.13.grad2_ref), custom_call_target="tpu_custom_call" | custom-call | flops 1073741824 | bytes 4194304 | tf_op jit(solution)/shard_map/pallas_call | solution.py:33
  141.3 2.6 %all-to-all-done.6.parts_ref = bf16[8,128,128]{2,1,0:T(8,128)(2,1)S(1)} async-done(((bf16[8,128,128]{2,1,0:T(8,128)(2,1)}), bf16[8,128,128]{2,1,0:T(8,128)(2,1)S(1)}, u32[]{:S(2)}, u32[]{:S(2)}) %all-to-all-start.6) | async-done | bytes 262176 | tf_op jit(solution)/shard_map/all_to_all | solution.py:240
  144.6 2.1 %shard_map.114 = (f32[1024,1024]{1,0:T(8,128)S(1)}, f32[1,512]{1,0:T(1,128)S(1)}) custom-call(s32[4]{0:T(128)S(1)} %pad_add_fusion.at_ref, bf16[8,128,128]{2,1,0:T(8,128)(2,1)S(1)} %all-to-all-done.6.parts_ref, bf16[256,1024]{1,0:T(8,128)(2,1)S(1)} %copy-done.3, bf16[256,1024]{1,0:T(8,128)(2,1)S(1)} %bitcast.23), custom_call_target="tpu_custom_call" | custom-call | flops 1073741824 | bytes 4194304 | tf_op jit(solution)/shard_map/pallas_call | solution.py:33
  146.8 3.6 %shard_map.115 = (bf16[1024,1024]{1,0:T(8,128)(2,1)}, f32[1,512]{1,0:T(1,128)}) custom-call(s32[4]{0:T(128)S(1)} %pad_add_fusion.at_ref, bf16[8,128,128]{2,1,0:T(8,128)(2,1)S(1)} %collective-permute-done.14.parts_ref, bf16[256,1024]{1,0:T(8,128)(2,1)S(1)} %copy-done.5, bf16[256,1024]{1,0:T(8,128)(2,1)S(1)} %copy-done.7, ...), custom_call_target="tpu_custom_call" | custom-call | flops 1073741824 | bytes 4194304 | tf_op jit(solution)/shard_map/pallas_call | solution.py:33
  (68 shorter events, 14.7 us)
Async XLA Ops:
  2.2 12.2 %all-to-all-start = ((bf16[8,64,256]{2,1,0:T(8,128)(2,1)}), bf16[8,64,256]{2,1,0:T(8,128)(2,1)S(1)}, u32[]{:S(2)}, u32[]{:S(2)}) async-start(bf16[8,64,256]{2,1,0:T(8,128)(2,1)} %broadcast_in_dim.16), calls=%async_computation | async-start | bytes 524288 | tf_op jit(solution)/shard_map/all_to_all | solution.py:240
  14.4 16.1 %copy-start.11 = (f32[1024]{0:T(1024)S(1)}, f32[1024]{0:T(1024)}, u32[]{:S(2)}) copy-start(f32[1024]{0:T(1024)} %param.13) | copy-start | bytes 12292
  14.4 31.4 %copy-start.10 = (f32[2048]{0:T(1024)S(1)}, f32[2048]{0:T(1024)}, u32[]{:S(2)}) copy-start(f32[2048]{0:T(1024)} %param.11) | copy-start | bytes 24580
  14.7 3.6 %collective-permute-start = (bf16[256,1024]{1,0:T(8,128)(2,1)S(1)}, bf16[256,1024]{1,0:T(8,128)(2,1)S(1)}, u32[]{:S(2)}, u32[]{:S(2)}) collective-permute-start(bf16[256,1024]{1,0:T(8,128)(2,1)S(1)} %shard_map.104), channel_id=1, source_target_pairs={{0,2},{2,0},{1,3},{3,1},{4,6},{6,4},{5,7},{7,5},{8,10},{10,8},{9,1... | collective-permute-start | bytes 1572872 | tf_op jit(solution)/shard_map/ppermute | solution.py:236
  19.4 27.1 %collective-permute-start.2 = (bf16[1024,1024]{1,0:T(8,128)(2,1)}, bf16[1024,1024]{1,0:T(8,128)(2,1)}, u32[]{:S(2)}, u32[]{:S(2)}) collective-permute-start(bf16[1024,1024]{1,0:T(8,128)(2,1)} %param.12), channel_id=1, source_target_pairs={{0,2},{2,0},{1,3},{3,1},{4,6},{6,4},{5,7},{7,5},{8,10},{10,8},{9,1... | collective-permute-start | bytes 6291464 | tf_op jit(solution)/shard_map/ppermute | solution.py:236
  19.9 25.9 %all-to-all-start.1 = ((bf16[16,16,1024]{2,1,0:T(8,128)(2,1)}), bf16[16,16,1024]{2,1,0:T(8,128)(2,1)S(1)}, u32[]{:S(2)}, u32[]{:S(2)}) async-start(bf16[16,16,1024]{2,1,0:T(8,128)(2,1)} %bitcast.9), calls=%async_computation.1 | async-start | bytes 1048576 | tf_op jit(solution)/shard_map/all_to_all | solution.py:240
  30.5 13.8 %collective-permute-start.1 = (f32[1,1024]{1,0:T(1,128)S(1)}, f32[1,1024]{1,0:T(1,128)S(1)}, u32[]{:S(2)}, u32[]{:S(2)}) collective-permute-start(f32[1,1024]{1,0:T(1,128)S(1)} %bitcast.27), channel_id=1, source_target_pairs={{0,2},{2,0},{1,3},{3,1},{4,6},{6,4},{5,7},{7,5},{8,10},{10,8},{9,1... | collective-permute-start | bytes 12296 | tf_op jit(solution)/shard_map/ppermute | solution.py:236
  46.5 23.1 %collective-permute-start.3 = (bf16[1024,1024]{1,0:T(8,128)(2,1)}, bf16[1024,1024]{1,0:T(8,128)(2,1)S(1)}, u32[]{:S(2)}, u32[]{:S(2)}) collective-permute-start(bf16[1024,1024]{1,0:T(8,128)(2,1)} %collective-permute-done.2), channel_id=1, source_target_pairs={{0,2},{2,0},{1,3},{3,1},{4,6},{6,4},{5,7},{7,5},{8,10},{10,8},{9,1... | collective-permute-start | bytes 6291464 | tf_op jit(solution)/shard_map/ppermute | solution.py:236
  49.2 20.4 %collective-permute-start.4 = (bf16[1024,1024]{1,0:T(8,128)(2,1)}, bf16[1024,1024]{1,0:T(8,128)(2,1)S(1)}, u32[]{:S(2)}, u32[]{:S(2)}) collective-permute-start(bf16[1024,1024]{1,0:T(8,128)(2,1)} %param.12), channel_id=1, source_target_pairs={{0,2},{2,0},{1,3},{3,1},{4,6},{6,4},{5,7},{7,5},{8,10},{10,8},{9,1... | collective-permute-start | bytes 6291464 | tf_op jit(solution)/shard_map/ppermute | solution.py:236
  49.3 21.8 %collective-permute-start.5 = (bf16[1024,1024]{1,0:T(8,128)(2,1)}, bf16[1024,1024]{1,0:T(8,128)(2,1)S(1)}, u32[]{:S(2)}, u32[]{:S(2)}) collective-permute-start(bf16[1024,1024]{1,0:T(8,128)(2,1)} %param.14), channel_id=1, source_target_pairs={{0,2},{2,0},{1,3},{3,1},{4,6},{6,4},{5,7},{7,5},{8,10},{10,8},{9,1... | collective-permute-start | bytes 6291464 | tf_op jit(solution)/shard_map/ppermute | solution.py:236
  69.6 13.7 %copy-start.2 = (bf16[256,1024]{1,0:T(8,128)(2,1)S(1)}, bf16[256,1024]{1,0:T(8,128)(2,1)}, u32[]{:S(2)}) copy-start(bf16[256,1024]{1,0:T(8,128)(2,1)} %get-tuple-element.72.slot_ref) | copy-start | bytes 1572868
  71.1 15.2 %copy-start.15 = (bf16[1024,1024]{1,0:T(8,128)(2,1)}, bf16[1024,1024]{1,0:T(8,128)(2,1)S(1)}, u32[]{:S(2)}) copy-start(bf16[1024,1024]{1,0:T(8,128)(2,1)S(1)} %collective-permute-done.5) | copy-start | bytes 6291460
  71.1 12.2 %collective-permute-start.6 = (bf16[1024,1024]{1,0:T(8,128)(2,1)S(1)}, bf16[1024,1024]{1,0:T(8,128)(2,1)S(1)}, u32[]{:S(2)}, u32[]{:S(2)}) collective-permute-start(bf16[1024,1024]{1,0:T(8,128)(2,1)S(1)} %collective-permute-done.5), channel_id=1, source_target_pairs={{0,2},{2,0},{1,3},{3,1},{4,6},{6,4},{5,7},{7,5},{8,10},{10,8},{9,1... | collective-permute-start | bytes 6291464 | tf_op jit(solution)/shard_map/ppermute | solution.py:236
  74.3 8.9 %collective-permute-start.7 = (bf16[1024,1024]{1,0:T(8,128)(2,1)S(1)}, bf16[1024,1024]{1,0:T(8,128)(2,1)S(1)}, u32[]{:S(2)}, u32[]{:S(2)}) collective-permute-start(bf16[1024,1024]{1,0:T(8,128)(2,1)S(1)} %copy-done.14), channel_id=1, source_target_pairs={{0,2},{2,0},{1,3},{3,1},{4,6},{6,4},{5,7},{7,5},{8,10},{10,8},{9,1... | collective-permute-start | bytes 6291464 | tf_op jit(solution)/shard_map/ppermute | solution.py:236
  86.3 18.5 %all-to-all-start.4 = ((bf16[16,16,1024]{2,1,0:T(8,128)(2,1)}), bf16[16,16,1024]{2,1,0:T(8,128)(2,1)S(1)}, u32[]{:S(2)}, u32[]{:S(2)}) async-start(bf16[16,16,1024]{2,1,0:T(8,128)(2,1)} %bitcast.12), calls=%async_computation.4 | async-start | bytes 1048576 | tf_op jit(solution)/shard_map/all_to_all | solution.py:240
  90.5 3.7 %collective-permute-start.9 = (bf16[256,1024]{1,0:T(8,128)(2,1)S(1)}, bf16[256,1024]{1,0:T(8,128)(2,1)S(1)}, u32[]{:S(2)}, u32[]{:S(2)}) collective-permute-start(bf16[256,1024]{1,0:T(8,128)(2,1)S(1)} %copy-done.8), channel_id=1, source_target_pairs={{0,2},{2,0},{1,3},{3,1},{4,6},{6,4},{5,7},{7,5},{8,10},{10,8},{9,1... | collective-permute-start | bytes 1572872 | tf_op jit(solution)/shard_map/ppermute | solution.py:236
  92.6 6.6 %collective-permute-start.10 = (bf16[256,1024]{1,0:T(8,128)(2,1)S(1)}, bf16[256,1024]{1,0:T(8,128)(2,1)S(1)}, u32[]{:S(2)}, u32[]{:S(2)}) collective-permute-start(bf16[256,1024]{1,0:T(8,128)(2,1)S(1)} %bitcast.22), channel_id=1, source_target_pairs={{0,2},{2,0},{1,3},{3,1},{4,6},{6,4},{5,7},{7,5},{8,10},{10,8},{9,1... | collective-permute-start | bytes 1572872 | tf_op jit(solution)/shard_map/ppermute | solution.py:236
  92.7 2.3 %collective-permute-start.8 = (f32[128,128]{1,0:T(8,128)S(1)}, f32[128,128]{1,0:T(8,128)S(1)}, u32[]{:S(2)}, u32[]{:S(2)}) collective-permute-start(f32[128,128]{1,0:T(8,128)S(1)} %get-tuple-element.80.packed_ref), channel_id=1, source_target_pairs={{0,2},{2,0},{1,3},{3,1},{4,6},{6,4},{5,7},{7,5},{8,10},{10,8},{9,1... | collective-permute-start | bytes 196616 | tf_op jit(solution)/shard_map/ppermute | solution.py:236
  99.2 31.3 %copy-start.6 = (bf16[256,1024]{1,0:T(8,128)(2,1)}, bf16[256,1024]{1,0:T(8,128)(2,1)S(1)}, u32[]{:S(2)}) copy-start(bf16[256,1024]{1,0:T(8,128)(2,1)S(1)} %collective-permute-done.10.x_ref) | copy-start | bytes 1572868
  105.4 22.8 %collective-permute-start.11 = (bf16[1024,1024]{1,0:T(8,128)(2,1)}, bf16[1024,1024]{1,0:T(8,128)(2,1)S(1)}, u32[]{:S(2)}, u32[]{:S(2)}) collective-permute-start(bf16[1024,1024]{1,0:T(8,128)(2,1)} %copy-done.15), channel_id=1, source_target_pairs={{0,2},{2,0},{1,3},{3,1},{4,6},{6,4},{5,7},{7,5},{8,10},{10,8},{9,1... | collective-permute-start | bytes 6291464 | tf_op jit(solution)/shard_map/ppermute | solution.py:236
  108.8 19.5 %collective-permute-start.12 = (bf16[1024,1024]{1,0:T(8,128)(2,1)}, bf16[1024,1024]{1,0:T(8,128)(2,1)S(1)}, u32[]{:S(2)}, u32[]{:S(2)}) collective-permute-start(bf16[1024,1024]{1,0:T(8,128)(2,1)} %param.14), channel_id=1, source_target_pairs={{0,2},{2,0},{1,3},{3,1},{4,6},{6,4},{5,7},{7,5},{8,10},{10,8},{9,1... | collective-permute-start | bytes 6291464 | tf_op jit(solution)/shard_map/ppermute | solution.py:236
  130.5 6.6 %collective-permute-start.13 = (bf16[256,1024]{1,0:T(8,128)(2,1)S(1)}, bf16[256,1024]{1,0:T(8,128)(2,1)}, u32[]{:S(2)}, u32[]{:S(2)}) collective-permute-start(bf16[256,1024]{1,0:T(8,128)(2,1)S(1)} %bitcast.19), channel_id=1, source_target_pairs={{0,2},{2,0},{1,3},{3,1},{4,6},{6,4},{5,7},{7,5},{8,10},{10,8},{9,1... | collective-permute-start | bytes 1572872 | tf_op jit(solution)/shard_map/ppermute | solution.py:236
  133.6 10.2 %all-to-all-start.6 = ((bf16[8,128,128]{2,1,0:T(8,128)(2,1)}), bf16[8,128,128]{2,1,0:T(8,128)(2,1)S(1)}, u32[]{:S(2)}, u32[]{:S(2)}) async-start(bf16[8,128,128]{2,1,0:T(8,128)(2,1)} %shard_map.112), calls=%async_computation.6 | async-start | bytes 524288 | tf_op jit(solution)/shard_map/all_to_all | solution.py:240
  143.8 2.9 %collective-permute-start.14 = (bf16[8,128,128]{2,1,0:T(8,128)(2,1)S(1)}, bf16[8,128,128]{2,1,0:T(8,128)(2,1)S(1)}, u32[]{:S(2)}, u32[]{:S(2)}) collective-permute-start(bf16[8,128,128]{2,1,0:T(8,128)(2,1)S(1)} %all-to-all-done.6.parts_ref), channel_id=1, source_target_pairs={{0,2},{2,0},{1,3},{3,1},{4,6},{6,4},{5,7},{7,5},{8,10},{10,8},{9,1... | collective-permute-start | bytes 786440 | tf_op jit(solution)/shard_map/ppermute | solution.py:236
  (11 other events, 63.2 us)

commit v7 on v6

--- a/solution.py
+++ b/solution.py
@@ -20,6 +20,7 @@
 SMALL, MIDDLE, MOST = 12, 24, 24
 COPIES = pltpu.SemaphoreType.DMA
 ROW_BLOCKS = 8
+EARLY_ROWS = 32
 FEATURES = ("section", "tok")
 COLUMN = ("yh", "z")
 CORE, TOK, FIRST, FIRST2 = range(4)
@@ -57,9 +58,10 @@
     packed_ref[...] = jnp.concatenate([place[:half], place[half:]], axis=1)
 
 
-def find_kernel(wide_ref, slot_ref, slot2_ref, found):
+def find_kernel(done, wide_ref, *refs):
+    given, (slot_ref, slot2_ref, found) = refs[:-3], refs[-3:]
     rows, width = slot_ref.shape
-    half, picks = rows // 2, LANES // 2
+    half, picks = wide_ref.shape[0] // 2, LANES // 2
     column = lax.broadcasted_iota(jnp.int32, (8, width), 1)
 
     def step(base, i, carry):
@@ -79,9 +81,12 @@
             out[own, :] = found[n, own, :].astype(F32).astype(BF16)
         return carry
 
-    lax.fori_loop(0, half // 8, functools.partial(step, 0), 0)
-    lax.fori_loop(half // 8, rows // 8, functools.partial(step, picks), 0)
-    lax.fori_loop(0, rows // 16, pack, 0)
+    for before, out in zip(given, (slot_ref, slot2_ref)):
+        out[:done, :] = before[...]
+    lax.fori_loop(done // 8, min(rows, half) // 8, functools.partial(step, 0), 0)
+    if rows > half:
+        lax.fori_loop(half // 8, rows // 8, functools.partial(step, picks), 0)
+    lax.fori_loop(done // 16, rows // 16, pack, 0)
 
 
 def pick(low, high, place, chunk, j, y):
@@ -112,12 +117,9 @@
     return total
 
 
-def whiten_other_kernel(x_ref, w_ref, out_ref):
-    out_ref[...] = jnp.dot(x_ref[...], w_ref[...], preferred_element_type=F32).astype(BF16)
-
-
-def whiten_own_kernel(x_ref, w_ref, add_ref, out_ref, ready, sems):
-    y = jnp.dot(x_ref[...], w_ref[...], preferred_element_type=F32) + add_ref[...].astype(F32)
+def whiten_kernel(x_ref, w_ref, x2_ref, w2_ref, out_ref, ready, sems):
+    y = jnp.dot(x_ref[...], w_ref[...], preferred_element_type=F32)
+    y = y + jnp.dot(x2_ref[...], w2_ref[...], preferred_element_type=F32)
     ready[...] = y.astype(BF16)
     start(ready, out_ref, sems.at[0]).wait()
 
@@ -257,7 +259,8 @@
 
     centered = (residual[0].astype(F32) - center).astype(BF16)
     out = jnp.broadcast_to(centered[None], (receivers,) + centered.shape)
-    out, listed = lax.optimization_barrier((out, chosen))
+    whiten_cols = lax.dynamic_slice_in_dim(whiten, at[TOK] * width, width, 1)
+    out, listed, whiten_cols = lax.optimization_barrier((out, chosen, whiten_cols))
     place, wide = call(
         functools.partial(place_kernel, latents),
         (SCALARS, HERE),
@@ -268,30 +271,32 @@
         (at, listed),
         vmem=SMALL,
     )
-    arrived, wide, place = lax.optimization_barrier(
-        (exchange(out, ("tok", "section")), wide, place)
+
+    def find(done, count, operands):
+        return call(
+            functools.partial(find_kernel, done),
+            (HERE,) * len(operands),
+            [(HERE, spec(count, latents))] * 2,
+            operands,
+            [pltpu.VMEM((2, count, latents), jnp.int32)],
+            4 * picks * (count - done) * latents,
+        )
+
+    early = find(0, EARLY_ROWS, (wide,))
+    whiten_cols2 = swap(whiten_cols)
+    arrived, wide, place, early = lax.optimization_barrier(
+        (exchange(out, ("tok", "section")), wide, place, early)
     )
     arrived = arrived.reshape(2, rows, inputs)
     own_rows = lax.dynamic_index_in_dim(arrived, core, 0, keepdims=False)
     other_rows = lax.dynamic_index_in_dim(arrived, 1 - core, 0, keepdims=False)
-    whiten_cols = lax.dynamic_slice_in_dim(whiten, at[TOK] * width, width, 1)
-    flops = 2 * rows * width * inputs
     (part,) = call(
-        whiten_other_kernel,
-        (HERE, HERE),
-        [(HERE, spec(rows, width))],
-        (other_rows, whiten_cols),
-        (),
-        flops,
-        vmem=SMALL,
-    )
-    (part,) = call(
-        whiten_own_kernel,
-        (HERE, HERE, HERE),
+        whiten_kernel,
+        (HERE,) * 4,
         [(HBM, spec(rows, width))],
-        (own_rows, whiten_cols, swap(part)),
+        (own_rows, whiten_cols, swap(other_rows), whiten_cols2),
         [pltpu.VMEM((rows, width), BF16), COPIES((1,))],
-        flops,
+        4 * rows * width * inputs,
         vmem=SMALL,
     )
     shares = (column, rows // column, width)
@@ -303,14 +308,7 @@
     )
     encoder_weight2, decoder_weight2 = swap(encoder_weight), swap(decoder_weight)
     bias_row2 = swap(bias_row)
-    slot, slot2 = call(
-        find_kernel,
-        (HERE,),
-        [(HERE, spec(rows, latents)), (HERE, spec(rows, latents))],
-        (wide,),
-        [pltpu.VMEM((2, rows, latents), jnp.int32)],
-        4 * picks * rows * latents,
-    )
+    slot, slot2 = find(EARLY_ROWS, rows, (wide, *early))
     parts, slot, slot2, bias_row2 = lax.optimization_barrier(
         (exchange(part.reshape(shares), COLUMN), slot, slot2, bias_row2)
     )

time: 151 us -> 152 us (level)
  waiting for transfers between devices: 17.5 us -> 15.2 us
  local copies, waits for them, and re-layouts: 2.52 us -> 4.37 us
    all_to_all x4, starting transfers between devices: 24.1 us -> 21.8 us  [exchange(): return lax.all_to_all(x, axes, 0, 0)]
    unnamed x32, local copies, waits for them, and re-layouts: 0.71 us -> 2.56 us
    all_to_all x4, waiting for transfers between devices: 14.1 us -> 12.3 us  [exchange(): return lax.all_to_all(x, axes, 0, 0)]
    ppermute x15 -> x16, starting transfers between devices: 19.6 us -> 21 us  [swap(): return lax.ppermute(x, 'core', [(0, 1), (1, 0)])]
    ppermute x15 -> x16, waiting for transfers between devices: 3.43 us -> 2.89 us  [swap(): return lax.ppermute(x, 'core', [(0, 1), (1, 0)])]
  transfers between devices with their start and end apart: 19 -> 20, of which waited for: 7 -> 7; matrix products, arithmetic and copies ran while one was open for 1% -> 1% of each run, Pallas kernels for 17% -> 18%
where the time goes in v7:
time: 152 us; the launch traced here: 151 us
  blocking collectives  48.5 us (32%)
  starting transfers between devices  42.8 us (28%)
  Pallas kernels  38.2 us (25%)
  waiting for transfers between devices  15.2 us (10%)
  local copies, waits for them, and re-layouts  4.37 us (3%)
    all_to_all x3, blocking collectives, exchange(): return lax.all_to_all(x, axes, 0, 0)  48.5 us
    pallas_call x13, Pallas kernels, call(): pl.pallas_call(kernel, in_specs=list(ins), out_specs=tuple((place for pla...  38.2 us
    all_to_all x4, starting transfers between devices, exchange(): return lax.all_to_all(x, axes, 0, 0)  21.8 us
    ppermute x16, starting transfers between devices, swap(): return lax.ppermute(x, 'core', [(0, 1), (1, 0)])  21 us
    all_to_all x4, waiting for transfers between devices, exchange(): return lax.all_to_all(x, axes, 0, 0)  12.3 us
  transfers between devices with their start and end apart: 20, of which 7 were waited for; matrix products, arithmetic and copies ran while one was open for 1% of the time, Pallas kernels for 18%

profile of v7, /device:TPU:1, one launch (start us, length us, event | category | flops | bytes accessed | tf_op | source)
XLA Modules:
  0.0 151.1 jit_solution(2477480965506926494)
XLA Ops:
  3.4 3.2 %collective-permute-start.1 = (bf16[256,1024]{1,0:T(8,128)(2,1)S(1)}, bf16[256,1024]{1,0:T(8,128)(2,1)S(1)}, u32[]{:S(2)}, u32[]{:S(2)}) collective-permute-start(bf16[256,1024]{1,0:T(8,128)(2,1)S(1)} %constant_dynamic-slice_fusion.w_ref), channel_id=1, source_target_pairs={{0,2},{2,0},{1,3},{3,1},{4,6},{6,4},{5,7},{7,5},{8,10},{10,8},{9,1... | collective-permute-start | bytes 1572872 | tf_op jit(solution)/shard_map/ppermute | solution.py:238
  6.6 3.4 %all-to-all-start = ((bf16[8,64,256]{2,1,0:T(8,128)(2,1)}), bf16[8,64,256]{2,1,0:T(8,128)(2,1)S(1)}, u32[]{:S(2)}, u32[]{:S(2)}) async-start(bf16[8,64,256]{2,1,0:T(8,128)(2,1)} %broadcast_in_dim.16), calls=%async_computation | async-start | bytes 524288 | tf_op jit(solution)/shard_map/all_to_all | solution.py:242
  12.6 3.0 %shard_map.104 = (bf16[32,1024]{1,0:T(8,128)(2,1)}, bf16[32,1024]{1,0:T(8,128)(2,1)}) custom-call(s32[256,128]{1,0:T(8,128)} %copy-done.6), custom_call_target="tpu_custom_call" | custom-call | flops 8388608 | bytes 1048576 | tf_op jit(solution)/shard_map/pallas_call | solution.py:34
  21.0 10.6 %all-to-all-start.1 = ((bf16[16,16,1024]{2,1,0:T(8,128)(2,1)}), bf16[16,16,1024]{2,1,0:T(8,128)(2,1)S(1)}, u32[]{:S(2)}, u32[]{:S(2)}) async-start(bf16[16,16,1024]{2,1,0:T(8,128)(2,1)} %bitcast.9), calls=%async_computation.1 | async-start | bytes 1048576 | tf_op jit(solution)/shard_map/all_to_all | solution.py:242
  32.1 11.9 %shard_map.106 = (bf16[256,1024]{1,0:T(8,128)(2,1)}, bf16[256,1024]{1,0:T(8,128)(2,1)}) custom-call(s32[256,128]{1,0:T(8,128)} %copy-done.6, bf16[32,1024]{1,0:T(8,128)(2,1)} %get-tuple-element.68.refs_0_, bf16[32,1024]{1,0:T(8,128)(2,1)} %get-tuple-element.69.refs_1_), custom_call_target="tpu_custom_call" | custom-call | flops 58720256 | bytes 1048576 | tf_op jit(solution)/shard_map/pallas_call | solution.py:34
  44.0 2.8 %all-to-all-done.1.parts_ref = bf16[16,16,1024]{2,1,0:T(8,128)(2,1)S(1)} async-done(((bf16[16,16,1024]{2,1,0:T(8,128)(2,1)}), bf16[16,16,1024]{2,1,0:T(8,128)(2,1)S(1)}, u32[]{:S(2)}, u32[]{:S(2)}) %all-to-all-start.1) | async-done | bytes 524320 | tf_op jit(solution)/shard_map/all_to_all | solution.py:242
  47.5 2.7 %collective-permute-start.4 = (bf16[1024,1024]{1,0:T(8,128)(2,1)}, bf16[1024,1024]{1,0:T(8,128)(2,1)S(1)}, u32[]{:S(2)}, u32[]{:S(2)}) collective-permute-start(bf16[1024,1024]{1,0:T(8,128)(2,1)} %collective-permute-done.3), channel_id=1, source_target_pairs={{0,2},{2,0},{1,3},{3,1},{4,6},{6,4},{5,7},{7,5},{8,10},{10,8},{9,1... | collective-permute-start | bytes 6291464 | tf_op jit(solution)/shard_map/ppermute | solution.py:238
  50.8 20.3 %all_to_all.35 = bf16[16,16,1024]{2,1,0:T(8,128)(2,1)S(1)} all-to-all(bf16[16,16,1024]{2,1,0:T(8,128)(2,1)S(1)} %get-tuple-element.76), channel_id=1, replica_groups=mesh['section'=4,'yh'=2,'z'=8,'core'=2,'tok'=2] {'yh','z'}, dimensions={0} | all-to-all | bytes 1048576 | tf_op jit(solution)/shard_map/all_to_all | solution.py:242
  72.6 2.0 %collective-permute-start.7 = (bf16[1024,1024]{1,0:T(8,128)(2,1)S(1)}, bf16[1024,1024]{1,0:T(8,128)(2,1)S(1)}, u32[]{:S(2)}, u32[]{:S(2)}) collective-permute-start(bf16[1024,1024]{1,0:T(8,128)(2,1)S(1)} %collective-permute-done.6), channel_id=1, source_target_pairs={{0,2},{2,0},{1,3},{3,1},{4,6},{6,4},{5,7},{7,5},{8,10},{10,8},{9,1... | collective-permute-start | bytes 6291464 | tf_op jit(solution)/shard_map/ppermute | solution.py:238
  74.7 8.8 %all_to_all.36.parts_ref = bf16[8,128,128]{2,1,0:T(8,128)(2,1)S(1)} all-to-all(bf16[8,128,128]{2,1,0:T(8,128)(2,1)S(1)} %shard_map.108), channel_id=1, replica_groups=mesh['section'=4,'yh'=2,'z'=8,'core'=2,'tok'=2] {'section','tok'}, dimensions={0} | all-to-all | bytes 524288 | tf_op jit(solution)/shard_map/all_to_all | solution.py:242
  83.5 3.0 %shard_map.109 = (f32[128,128]{1,0:T(8,128)S(1)}, bf16[256,1024]{1,0:T(8,128)(2,1)}) custom-call(bf16[8,128,128]{2,1,0:T(8,128)(2,1)S(1)} %all_to_all.36.parts_ref, bf16[256,1024]{1,0:T(8,128)(2,1)S(1)} %copy-done.2, bf16[256,1024]{1,0:T(8,128)(2,1)S(1)} %copy-done.9, f32[1,1024]{1,0:T(1,128)S(1)} %bitcast.28, ...), custom_call_target="tpu_custom_call" | custom-call | flops 1073741824 | bytes 4194304 | tf_op jit(solution)/shard_map/pallas_call | solution.py:34
  86.6 4.4 %all-to-all-start.4 = ((bf16[16,16,1024]{2,1,0:T(8,128)(2,1)}), bf16[16,16,1024]{2,1,0:T(8,128)(2,1)S(1)}, u32[]{:S(2)}, u32[]{:S(2)}) async-start(bf16[16,16,1024]{2,1,0:T(8,128)(2,1)} %bitcast.12), calls=%async_computation.4 | async-start | bytes 1048576 | tf_op jit(solution)/shard_map/all_to_all | solution.py:242
  91.0 2.4 %collective-permute-start.10 = (bf16[256,1024]{1,0:T(8,128)(2,1)S(1)}, bf16[256,1024]{1,0:T(8,128)(2,1)S(1)}, u32[]{:S(2)}, u32[]{:S(2)}) collective-permute-start(bf16[256,1024]{1,0:T(8,128)(2,1)S(1)} %copy-done.9), channel_id=1, source_target_pairs={{0,2},{2,0},{1,3},{3,1},{4,6},{6,4},{5,7},{7,5},{8,10},{10,8},{9,1... | collective-permute-start | bytes 1572872 | tf_op jit(solution)/shard_map/ppermute | solution.py:238
  96.4 3.6 %shard_map.110 = (bf16[256,1024]{1,0:T(8,128)(2,1)}, bf16[256,1024]{1,0:T(8,128)(2,1)}) custom-call(f32[128,128]{1,0:T(8,128)} %copy-done.10, f32[128,128]{1,0:T(8,128)} %copy-done.13, bf16[256,1024]{1,0:T(8,128)(2,1)} %get-tuple-element.82.slot_ref, bf16[256,1024]{1,0:T(8,128)(2,1)} %copy-done.4, f32[1,1024]{1,0:T(1,128)} %bitcast.26), custom_call_target="tpu_custom_call" | custom-call | bytes 1048576 | tf_op jit(solution)/shard_map/pallas_call | solution.py:34
  100.0 5.0 %all-to-all-done.4.parts_ref = bf16[16,16,1024]{2,1,0:T(8,128)(2,1)S(1)} async-done(((bf16[16,16,1024]{2,1,0:T(8,128)(2,1)}), bf16[16,16,1024]{2,1,0:T(8,128)(2,1)S(1)}, u32[]{:S(2)}, u32[]{:S(2)}) %all-to-all-start.4) | async-done | bytes 524320 | tf_op jit(solution)/shard_map/all_to_all | solution.py:242
  105.6 3.7 %collective-permute-start.12 = (bf16[1024,1024]{1,0:T(8,128)(2,1)}, bf16[1024,1024]{1,0:T(8,128)(2,1)S(1)}, u32[]{:S(2)}, u32[]{:S(2)}) collective-permute-start(bf16[1024,1024]{1,0:T(8,128)(2,1)} %copy-done.15), channel_id=1, source_target_pairs={{0,2},{2,0},{1,3},{3,1},{4,6},{6,4},{5,7},{7,5},{8,10},{10,8},{9,1... | collective-permute-start | bytes 6291464 | tf_op jit(solution)/shard_map/ppermute | solution.py:238
  109.4 19.4 %all_to_all.37 = bf16[16,16,1024]{2,1,0:T(8,128)(2,1)S(1)} all-to-all(bf16[16,16,1024]{2,1,0:T(8,128)(2,1)S(1)} %shard_map.111), channel_id=1, replica_groups=mesh['section'=4,'yh'=2,'z'=8,'core'=2,'tok'=2] {'yh','z'}, dimensions={0} | all-to-all | bytes 1048576 | tf_op jit(solution)/shard_map/all_to_all | solution.py:242
  128.8 2.2 %shard_map.112 = bf16[8,128,128]{2,1,0:T(8,128)(2,1)} custom-call(bf16[256,1024]{1,0:T(8,128)(2,1)S(1)} %bitcast.18, s32[128,128]{1,0:T(8,128)S(1)} %get-tuple-element.77.place_ref, bf16[1024,1024]{1,0:T(8,128)(2,1)S(1)} %collective-permute-done.12.w_ref, bf16[1024,1024]{1,0:T(8,128)(2,1)S(1)} %collective-permute-done.13.w2_ref), custom_call_target="tpu_custom_call" | custom-call | flops 1073741824 | bytes 4194304 | tf_op jit(solution)/shard_map/pallas_call | solution.py:34
  131.0 3.1 %collective-permute-start.14 = (bf16[256,1024]{1,0:T(8,128)(2,1)S(1)}, bf16[256,1024]{1,0:T(8,128)(2,1)}, u32[]{:S(2)}, u32[]{:S(2)}) collective-permute-start(bf16[256,1024]{1,0:T(8,128)(2,1)S(1)} %bitcast.19), channel_id=1, source_target_pairs={{0,2},{2,0},{1,3},{3,1},{4,6},{6,4},{5,7},{7,5},{8,10},{10,8},{9,1... | collective-permute-start | bytes 1572872 | tf_op jit(solution)/shard_map/ppermute | solution.py:238
  134.2 3.4 %all-to-all-start.6 = ((bf16[8,128,128]{2,1,0:T(8,128)(2,1)}), bf16[8,128,128]{2,1,0:T(8,128)(2,1)S(1)}, u32[]{:S(2)}, u32[]{:S(2)}) async-start(bf16[8,128,128]{2,1,0:T(8,128)(2,1)} %shard_map.112), calls=%async_computation.6 | async-start | bytes 524288 | tf_op jit(solution)/shard_map/all_to_all | solution.py:242
  137.6 4.2 %shard_map.113 = bf16[1024,1024]{1,0:T(8,128)(2,1)} custom-call(bf16[256,1024]{1,0:T(8,128)(2,1)} %get-tuple-element.100.codes_ref, bf16[256,1024]{1,0:T(8,128)(2,1)} %get-tuple-element.101.codes2_ref, bf16[256,1024]{1,0:T(8,128)(2,1)} %bitcast.20, bf16[256,1024]{1,0:T(8,128)(2,1)} %collective-permute-done.14.grad2_ref), custom_call_target="tpu_custom_call" | custom-call | flops 1073741824 | bytes 4194304 | tf_op jit(solution)/shard_map/pallas_call | solution.py:34
  141.8 2.6 %all-to-all-done.6.parts_ref = bf16[8,128,128]{2,1,0:T(8,128)(2,1)S(1)} async-done(((bf16[8,128,128]{2,1,0:T(8,128)(2,1)}), bf16[8,128,128]{2,1,0:T(8,128)(2,1)S(1)}, u32[]{:S(2)}, u32[]{:S(2)}) %all-to-all-start.6) | async-done | bytes 262176 | tf_op jit(solution)/shard_map/all_to_all | solution.py:242
  145.2 2.1 %shard_map.114 = (f32[1024,1024]{1,0:T(8,128)S(1)}, f32[1,512]{1,0:T(1,128)S(1)}) custom-call(s32[4]{0:T(128)S(1)} %pad_add_fusion.at_ref, bf16[8,128,128]{2,1,0:T(8,128)(2,1)S(1)} %all-to-all-done.6.parts_ref, bf16[256,1024]{1,0:T(8,128)(2,1)S(1)} %copy-done.3, bf16[256,1024]{1,0:T(8,128)(2,1)S(1)} %bitcast.23), custom_call_target="tpu_custom_call" | custom-call | flops 1073741824 | bytes 4194304 | tf_op jit(solution)/shard_map/pallas_call | solution.py:34
  147.3 3.6 %shard_map.115 = (bf16[1024,1024]{1,0:T(8,128)(2,1)}, f32[1,512]{1,0:T(1,128)}) custom-call(s32[4]{0:T(128)S(1)} %pad_add_fusion.at_ref, bf16[8,128,128]{2,1,0:T(8,128)(2,1)S(1)} %collective-permute-done.15.parts_ref, bf16[256,1024]{1,0:T(8,128)(2,1)S(1)} %copy-done.5, bf16[256,1024]{1,0:T(8,128)(2,1)S(1)} %copy-done.8, ...), custom_call_target="tpu_custom_call" | custom-call | flops 1073741824 | bytes 4194304 | tf_op jit(solution)/shard_map/pallas_call | solution.py:34
  (70 shorter events, 18.6 us)
Async XLA Ops:
  3.4 15.9 %collective-permute-start.1 = (bf16[256,1024]{1,0:T(8,128)(2,1)S(1)}, bf16[256,1024]{1,0:T(8,128)(2,1)S(1)}, u32[]{:S(2)}, u32[]{:S(2)}) collective-permute-start(bf16[256,1024]{1,0:T(8,128)(2,1)S(1)} %constant_dynamic-slice_fusion.w_ref), channel_id=1, source_target_pairs={{0,2},{2,0},{1,3},{3,1},{4,6},{6,4},{5,7},{7,5},{8,10},{10,8},{9,1... | collective-permute-start | bytes 1572872 | tf_op jit(solution)/shard_map/ppermute | solution.py:238
  6.6 10.9 %all-to-all-start = ((bf16[8,64,256]{2,1,0:T(8,128)(2,1)}), bf16[8,64,256]{2,1,0:T(8,128)(2,1)S(1)}, u32[]{:S(2)}, u32[]{:S(2)}) async-start(bf16[8,64,256]{2,1,0:T(8,128)(2,1)} %broadcast_in_dim.16), calls=%async_computation | async-start | bytes 524288 | tf_op jit(solution)/shard_map/all_to_all | solution.py:242
  10.1 21.5 %copy-start.12 = (f32[1024]{0:T(1024)S(1)}, f32[1024]{0:T(1024)}, u32[]{:S(2)}) copy-start(f32[1024]{0:T(1024)} %param.13) | copy-start | bytes 12292
  11.1 35.8 %copy-start.11 = (f32[2048]{0:T(1024)S(1)}, f32[2048]{0:T(1024)}, u32[]{:S(2)}) copy-start(f32[2048]{0:T(1024)} %param.11) | copy-start | bytes 24580
  17.5 1.8 %collective-permute-start = (bf16[256,256]{1,0:T(8,128)(2,1)S(1)}, bf16[256,256]{1,0:T(8,128)(2,1)S(1)}, u32[]{:S(2)}, u32[]{:S(2)}) collective-permute-start(bf16[256,256]{1,0:T(8,128)(2,1)S(1)} %get-tuple-element.111), channel_id=1, source_target_pairs={{0,2},{2,0},{1,3},{3,1},{4,6},{6,4},{5,7},{7,5},{8,10},{10,8},{9,1... | collective-permute-start | bytes 393224 | tf_op jit(solution)/shard_map/ppermute | solution.py:238
  20.6 27.0 %collective-permute-start.3 = (bf16[1024,1024]{1,0:T(8,128)(2,1)}, bf16[1024,1024]{1,0:T(8,128)(2,1)}, u32[]{:S(2)}, u32[]{:S(2)}) collective-permute-start(bf16[1024,1024]{1,0:T(8,128)(2,1)} %param.12), channel_id=1, source_target_pairs={{0,2},{2,0},{1,3},{3,1},{4,6},{6,4},{5,7},{7,5},{8,10},{10,8},{9,1... | collective-permute-start | bytes 6291464 | tf_op jit(solution)/shard_map/ppermute | solution.py:238
  21.0 25.8 %all-to-all-start.1 = ((bf16[16,16,1024]{2,1,0:T(8,128)(2,1)}), bf16[16,16,1024]{2,1,0:T(8,128)(2,1)S(1)}, u32[]{:S(2)}, u32[]{:S(2)}) async-start(bf16[16,16,1024]{2,1,0:T(8,128)(2,1)} %bitcast.9), calls=%async_computation.1 | async-start | bytes 1048576 | tf_op jit(solution)/shard_map/all_to_all | solution.py:242
  31.6 12.4 %collective-permute-start.2 = (f32[1,1024]{1,0:T(1,128)S(1)}, f32[1,1024]{1,0:T(1,128)S(1)}, u32[]{:S(2)}, u32[]{:S(2)}) collective-permute-start(f32[1,1024]{1,0:T(1,128)S(1)} %bitcast.27), channel_id=1, source_target_pairs={{0,2},{2,0},{1,3},{3,1},{4,6},{6,4},{5,7},{7,5},{8,10},{10,8},{9,1... | collective-permute-start | bytes 12296 | tf_op jit(solution)/shard_map/ppermute | solution.py:238
  47.5 23.5 %collective-permute-start.4 = (bf16[1024,1024]{1,0:T(8,128)(2,1)}, bf16[1024,1024]{1,0:T(8,128)(2,1)S(1)}, u32[]{:S(2)}, u32[]{:S(2)}) collective-permute-start(bf16[1024,1024]{1,0:T(8,128)(2,1)} %collective-permute-done.3), channel_id=1, source_target_pairs={{0,2},{2,0},{1,3},{3,1},{4,6},{6,4},{5,7},{7,5},{8,10},{10,8},{9,1... | collective-permute-start | bytes 6291464 | tf_op jit(solution)/shard_map/ppermute | solution.py:238
  50.2 20.8 %collective-permute-start.5 = (bf16[1024,1024]{1,0:T(8,128)(2,1)}, bf16[1024,1024]{1,0:T(8,128)(2,1)S(1)}, u32[]{:S(2)}, u32[]{:S(2)}) collective-permute-start(bf16[1024,1024]{1,0:T(8,128)(2,1)} %param.12), channel_id=1, source_target_pairs={{0,2},{2,0},{1,3},{3,1},{4,6},{6,4},{5,7},{7,5},{8,10},{10,8},{9,1... | collective-permute-start | bytes 6291464 | tf_op jit(solution)/shard_map/ppermute | solution.py:238
  50.3 22.2 %collective-permute-start.6 = (bf16[1024,1024]{1,0:T(8,128)(2,1)}, bf16[1024,1024]{1,0:T(8,128)(2,1)S(1)}, u32[]{:S(2)}, u32[]{:S(2)}) collective-permute-start(bf16[1024,1024]{1,0:T(8,128)(2,1)} %param.14), channel_id=1, source_target_pairs={{0,2},{2,0},{1,3},{3,1},{4,6},{6,4},{5,7},{7,5},{8,10},{10,8},{9,1... | collective-permute-start | bytes 6291464 | tf_op jit(solution)/shard_map/ppermute | solution.py:238
  72.6 14.0 %copy-start.15 = (bf16[1024,1024]{1,0:T(8,128)(2,1)}, bf16[1024,1024]{1,0:T(8,128)(2,1)S(1)}, u32[]{:S(2)}) copy-start(bf16[1024,1024]{1,0:T(8,128)(2,1)S(1)} %collective-permute-done.6) | copy-start | bytes 6291460
  72.6 10.9 %collective-permute-start.7 = (bf16[1024,1024]{1,0:T(8,128)(2,1)S(1)}, bf16[1024,1024]{1,0:T(8,128)(2,1)S(1)}, u32[]{:S(2)}, u32[]{:S(2)}) collective-permute-start(bf16[1024,1024]{1,0:T(8,128)(2,1)S(1)} %collective-permute-done.6), channel_id=1, source_target_pairs={{0,2},{2,0},{1,3},{3,1},{4,6},{6,4},{5,7},{7,5},{8,10},{10,8},{9,1... | collective-permute-start | bytes 6291464 | tf_op jit(solution)/shard_map/ppermute | solution.py:238
  74.6 8.9 %collective-permute-start.8 = (bf16[1024,1024]{1,0:T(8,128)(2,1)S(1)}, bf16[1024,1024]{1,0:T(8,128)(2,1)S(1)}, u32[]{:S(2)}, u32[]{:S(2)}) collective-permute-start(bf16[1024,1024]{1,0:T(8,128)(2,1)S(1)} %copy-done.14), channel_id=1, source_target_pairs={{0,2},{2,0},{1,3},{3,1},{4,6},{6,4},{5,7},{7,5},{8,10},{10,8},{9,1... | collective-permute-start | bytes 6291464 | tf_op jit(solution)/shard_map/ppermute | solution.py:238
  86.6 18.3 %all-to-all-start.4 = ((bf16[16,16,1024]{2,1,0:T(8,128)(2,1)}), bf16[16,16,1024]{2,1,0:T(8,128)(2,1)S(1)}, u32[]{:S(2)}, u32[]{:S(2)}) async-start(bf16[16,16,1024]{2,1,0:T(8,128)(2,1)} %bitcast.12), calls=%async_computation.4 | async-start | bytes 1048576 | tf_op jit(solution)/shard_map/all_to_all | solution.py:242
  91.0 3.9 %collective-permute-start.10 = (bf16[256,1024]{1,0:T(8,128)(2,1)S(1)}, bf16[256,1024]{1,0:T(8,128)(2,1)S(1)}, u32[]{:S(2)}, u32[]{:S(2)}) collective-permute-start(bf16[256,1024]{1,0:T(8,128)(2,1)S(1)} %copy-done.9), channel_id=1, source_target_pairs={{0,2},{2,0},{1,3},{3,1},{4,6},{6,4},{5,7},{7,5},{8,10},{10,8},{9,1... | collective-permute-start | bytes 1572872 | tf_op jit(solution)/shard_map/ppermute | solution.py:238
  93.4 6.6 %collective-permute-start.11 = (bf16[256,1024]{1,0:T(8,128)(2,1)S(1)}, bf16[256,1024]{1,0:T(8,128)(2,1)S(1)}, u32[]{:S(2)}, u32[]{:S(2)}) collective-permute-start(bf16[256,1024]{1,0:T(8,128)(2,1)S(1)} %bitcast.22), channel_id=1, source_target_pairs={{0,2},{2,0},{1,3},{3,1},{4,6},{6,4},{5,7},{7,5},{8,10},{10,8},{9,1... | collective-permute-start | bytes 1572872 | tf_op jit(solution)/shard_map/ppermute | solution.py:238
  93.5 2.3 %collective-permute-start.9 = (f32[128,128]{1,0:T(8,128)S(1)}, f32[128,128]{1,0:T(8,128)S(1)}, u32[]{:S(2)}, u32[]{:S(2)}) collective-permute-start(f32[128,128]{1,0:T(8,128)S(1)} %get-tuple-element.90.packed_ref), channel_id=1, source_target_pairs={{0,2},{2,0},{1,3},{3,1},{4,6},{6,4},{5,7},{7,5},{8,10},{10,8},{9,1... | collective-permute-start | bytes 196616 | tf_op jit(solution)/shard_map/ppermute | solution.py:238
  100.0 31.1 %copy-start.7 = (bf16[256,1024]{1,0:T(8,128)(2,1)}, bf16[256,1024]{1,0:T(8,128)(2,1)S(1)}, u32[]{:S(2)}) copy-start(bf16[256,1024]{1,0:T(8,128)(2,1)S(1)} %collective-permute-done.11.x_ref) | copy-start | bytes 1572868
  105.6 23.2 %collective-permute-start.12 = (bf16[1024,1024]{1,0:T(8,128)(2,1)}, bf16[1024,1024]{1,0:T(8,128)(2,1)S(1)}, u32[]{:S(2)}, u32[]{:S(2)}) collective-permute-start(bf16[1024,1024]{1,0:T(8,128)(2,1)} %copy-done.15), channel_id=1, source_target_pairs={{0,2},{2,0},{1,3},{3,1},{4,6},{6,4},{5,7},{7,5},{8,10},{10,8},{9,1... | collective-permute-start | bytes 6291464 | tf_op jit(solution)/shard_map/ppermute | solution.py:238
  109.3 19.5 %collective-permute-start.13 = (bf16[1024,1024]{1,0:T(8,128)(2,1)}, bf16[1024,1024]{1,0:T(8,128)(2,1)S(1)}, u32[]{:S(2)}, u32[]{:S(2)}) collective-permute-start(bf16[1024,1024]{1,0:T(8,128)(2,1)} %param.14), channel_id=1, source_target_pairs={{0,2},{2,0},{1,3},{3,1},{4,6},{6,4},{5,7},{7,5},{8,10},{10,8},{9,1... | collective-permute-start | bytes 6291464 | tf_op jit(solution)/shard_map/ppermute | solution.py:238
  131.0 6.6 %collective-permute-start.14 = (bf16[256,1024]{1,0:T(8,128)(2,1)S(1)}, bf16[256,1024]{1,0:T(8,128)(2,1)}, u32[]{:S(2)}, u32[]{:S(2)}) collective-permute-start(bf16[256,1024]{1,0:T(8,128)(2,1)S(1)} %bitcast.19), channel_id=1, source_target_pairs={{0,2},{2,0},{1,3},{3,1},{4,6},{6,4},{5,7},{7,5},{8,10},{10,8},{9,1... | collective-permute-start | bytes 1572872 | tf_op jit(solution)/shard_map/ppermute | solution.py:238
  134.2 10.2 %all-to-all-start.6 = ((bf16[8,128,128]{2,1,0:T(8,128)(2,1)}), bf16[8,128,128]{2,1,0:T(8,128)(2,1)S(1)}, u32[]{:S(2)}, u32[]{:S(2)}) async-start(bf16[8,128,128]{2,1,0:T(8,128)(2,1)} %shard_map.112), calls=%async_computation.6 | async-start | bytes 524288 | tf_op jit(solution)/shard_map/all_to_all | solution.py:242
  144.4 2.9 %collective-permute-start.15 = (bf16[8,128,128]{2,1,0:T(8,128)(2,1)S(1)}, bf16[8,128,128]{2,1,0:T(8,128)(2,1)S(1)}, u32[]{:S(2)}, u32[]{:S(2)}) collective-permute-start(bf16[8,128,128]{2,1,0:T(8,128)(2,1)S(1)} %all-to-all-done.6.parts_ref), channel_id=1, source_target_pairs={{0,2},{2,0},{1,3},{3,1},{4,6},{6,4},{5,7},{7,5},{8,10},{10,8},{9,1... | collective-permute-start | bytes 786440 | tf_op jit(solution)/shard_map/ppermute | solution.py:238
  (12 other events, 61.7 us)

commit v8 on v7

--- a/solution.py
+++ b/solution.py
@@ -319,8 +319,11 @@
         (at, parts, decoder_bias),
         vmem=SMALL,
     )
-    out, weight, weight2 = lax.optimization_barrier((out, encoder_weight, encoder_weight2))
+    out, weight, weight2, later, later2 = lax.optimization_barrier(
+        (out, encoder_weight, encoder_weight2, decoder_weight, decoder_weight2)
+    )
     weight, weight2 = swap(weight2), swap(weight)
+    later, later2 = swap(later2), swap(later)
     shifted = exchange(out, COLUMN).reshape(rows, width)
 
     flops = 4 * rows * width * latents
@@ -340,10 +343,7 @@
         return packed
 
     encoded = chosen_product(0, shifted, weight, weight2)
-    encoded, shifted, weight, weight2 = lax.optimization_barrier(
-        (encoded, shifted, decoder_weight, decoder_weight2)
-    )
-    weight, weight2 = swap(weight2), swap(weight)
+    encoded, shifted, weight, weight2 = lax.optimization_barrier((encoded, shifted, later, later2))
     shifted2, other_slot = swap(shifted), swap(slot2)
     encoded = exchange(encoded, FEATURES)
     packed, part = call(
@@ -373,8 +373,6 @@
         (at, parts, decoder_bias, whitened),
         vmem=SMALL,
     )
-    out, weight, weight2 = lax.optimization_barrier((out, decoder_weight, decoder_weight2))
-    weight, weight2 = swap(weight2), swap(weight)
     grad = exchange(out, COLUMN).reshape(rows, width)
 
     packed = chosen_product(1, grad, weight, weight2)

time: 152 us -> 150 us (0.987)
  waiting for transfers between devices: 15.2 us -> 13 us
  starting transfers between devices: 42.8 us -> 41 us
  local copies, waits for them, and re-layouts: 4.37 us -> 5.94 us
    ppermute x16 -> x14, starting transfers between devices: 21 us -> 16.1 us  [swap(): return lax.ppermute(x, 'core', [(0, 1), (1, 0)])]
    all_to_all x4, starting transfers between devices: 21.8 us -> 24.9 us  [exchange(): return lax.all_to_all(x, axes, 0, 0)]
    unnamed x32 -> x34, local copies, waits for them, and re-layouts: 2.56 us -> 4.13 us
    all_to_all x4, waiting for transfers between devices: 12.3 us -> 10.8 us  [exchange(): return lax.all_to_all(x, axes, 0, 0)]
  transfers between devices with their start and end apart: 20 -> 18, of which waited for: 7 -> 6; matrix products, arithmetic and copies ran while one was open for 1% -> 1% of each run, Pallas kernels for 18% -> 18%
where the time goes in v8:
time: 150 us
  blocking collectives  48.1 us (32%)
  starting transfers between devices  41 us (27%)
  Pallas kernels  39.4 us (26%)
  waiting for transfers between devices  13 us (9%)
  local copies, waits for them, and re-layouts  5.94 us (4%)
    all_to_all x3, blocking collectives, exchange(): return lax.all_to_all(x, axes, 0, 0)  48.1 us
    pallas_call x13, Pallas kernels, call(): pl.pallas_call(kernel, in_specs=list(ins), out_specs=tuple((place for pla...  39.4 us
    all_to_all x4, starting transfers between devices, exchange(): return lax.all_to_all(x, axes, 0, 0)  24.9 us
    ppermute x14, starting transfers between devices, swap(): return lax.ppermute(x, 'core', [(0, 1), (1, 0)])  16.1 us
    all_to_all x4, waiting for transfers between devices, exchange(): return lax.all_to_all(x, axes, 0, 0)  10.8 us
    unnamed x34, local copies, waits for them, and re-layouts  4.13 us
  transfers between devices with their start and end apart: 18, of which 6 were waited for; matrix products, arithmetic and copies ran while one was open for 1% of the time, Pallas kernels for 18%

profile of v8, /device:TPU:1, one launch (start us, length us, event | category | flops | bytes accessed | tf_op | source)
XLA Modules:
  0.0 149.6 jit_solution(762443291358539754)
XLA Ops:
  2.7 3.2 %collective-permute-start.1 = (bf16[256,1024]{1,0:T(8,128)(2,1)S(1)}, bf16[256,1024]{1,0:T(8,128)(2,1)S(1)}, u32[]{:S(2)}, u32[]{:S(2)}) collective-permute-start(bf16[256,1024]{1,0:T(8,128)(2,1)S(1)} %constant_dynamic-slice_fusion.w_ref), channel_id=1, source_target_pairs={{0,2},{2,0},{1,3},{3,1},{4,6},{6,4},{5,7},{7,5},{8,10},{10,8},{9,1... | collective-permute-start | bytes 1572872 | tf_op jit(solution)/shard_map/ppermute | solution.py:238
  5.9 3.4 %all-to-all-start = ((bf16[8,64,256]{2,1,0:T(8,128)(2,1)}), bf16[8,64,256]{2,1,0:T(8,128)(2,1)S(1)}, u32[]{:S(2)}, u32[]{:S(2)}) async-start(bf16[8,64,256]{2,1,0:T(8,128)(2,1)} %broadcast_in_dim.16), calls=%async_computation | async-start | bytes 524288 | tf_op jit(solution)/shard_map/all_to_all | solution.py:242
  11.8 3.0 %shard_map.104 = (bf16[32,1024]{1,0:T(8,128)(2,1)}, bf16[32,1024]{1,0:T(8,128)(2,1)}) custom-call(s32[256,128]{1,0:T(8,128)} %copy-done.10), custom_call_target="tpu_custom_call" | custom-call | flops 8388608 | bytes 1048576 | tf_op jit(solution)/shard_map/pallas_call | solution.py:34
  14.8 2.0 %all-to-all-done = bf16[8,64,256]{2,1,0:T(8,128)(2,1)S(1)} async-done(((bf16[8,64,256]{2,1,0:T(8,128)(2,1)}), bf16[8,64,256]{2,1,0:T(8,128)(2,1)S(1)}, u32[]{:S(2)}, u32[]{:S(2)}) %all-to-all-start) | async-done | bytes 262176 | tf_op jit(solution)/shard_map/all_to_all | solution.py:242
  20.4 10.6 %all-to-all-start.1 = ((bf16[16,16,1024]{2,1,0:T(8,128)(2,1)}), bf16[16,16,1024]{2,1,0:T(8,128)(2,1)S(1)}, u32[]{:S(2)}, u32[]{:S(2)}) async-start(bf16[16,16,1024]{2,1,0:T(8,128)(2,1)} %bitcast.9), calls=%async_computation.1 | async-start | bytes 1048576 | tf_op jit(solution)/shard_map/all_to_all | solution.py:242
  31.7 11.9 %shard_map.106 = (bf16[256,1024]{1,0:T(8,128)(2,1)}, bf16[256,1024]{1,0:T(8,128)(2,1)}) custom-call(s32[256,128]{1,0:T(8,128)} %copy-done.10, bf16[32,1024]{1,0:T(8,128)(2,1)} %get-tuple-element.67.refs_0_, bf16[32,1024]{1,0:T(8,128)(2,1)} %get-tuple-element.68.refs_1_), custom_call_target="tpu_custom_call" | custom-call | flops 58720256 | bytes 1048576 | tf_op jit(solution)/shard_map/pallas_call | solution.py:34
  43.7 2.5 %all-to-all-done.1.parts_ref = bf16[16,16,1024]{2,1,0:T(8,128)(2,1)S(1)} async-done(((bf16[16,16,1024]{2,1,0:T(8,128)(2,1)}), bf16[16,16,1024]{2,1,0:T(8,128)(2,1)S(1)}, u32[]{:S(2)}, u32[]{:S(2)}) %all-to-all-start.1) | async-done | bytes 524320 | tf_op jit(solution)/shard_map/all_to_all | solution.py:242
  46.8 2.9 %collective-permute-start.5 = (bf16[1024,1024]{1,0:T(8,128)(2,1)}, bf16[1024,1024]{1,0:T(8,128)(2,1)S(1)}, u32[]{:S(2)}, u32[]{:S(2)}) collective-permute-start(bf16[1024,1024]{1,0:T(8,128)(2,1)} %collective-permute-done.3), channel_id=1, source_target_pairs={{0,2},{2,0},{1,3},{3,1},{4,6},{6,4},{5,7},{7,5},{8,10},{10,8},{9,1... | collective-permute-start | bytes 6291464 | tf_op jit(solution)/shard_map/ppermute | solution.py:238
  50.3 19.1 %all_to_all.35 = bf16[16,16,1024]{2,1,0:T(8,128)(2,1)S(1)} all-to-all(bf16[16,16,1024]{2,1,0:T(8,128)(2,1)S(1)} %get-tuple-element.76), channel_id=1, replica_groups=mesh['section'=4,'yh'=2,'z'=8,'core'=2,'tok'=2] {'yh','z'}, dimensions={0} | all-to-all | bytes 1048576 | tf_op jit(solution)/shard_map/all_to_all | solution.py:242
  69.4 1.4 shard_map.108
  70.9 8.2 %all_to_all.36.parts_ref = bf16[8,128,128]{2,1,0:T(8,128)(2,1)S(1)} all-to-all(bf16[8,128,128]{2,1,0:T(8,128)(2,1)S(1)} %shard_map.108), channel_id=1, replica_groups=mesh['section'=4,'yh'=2,'z'=8,'core'=2,'tok'=2] {'section','tok'}, dimensions={0} | all-to-all | bytes 524288 | tf_op jit(solution)/shard_map/all_to_all | solution.py:242
  79.1 2.2 %shard_map.109 = (f32[128,128]{1,0:T(8,128)S(1)}, bf16[256,1024]{1,0:T(8,128)(2,1)S(1)}) custom-call(bf16[8,128,128]{2,1,0:T(8,128)(2,1)S(1)} %all_to_all.36.parts_ref, bf16[256,1024]{1,0:T(8,128)(2,1)S(1)} %copy-done.5, bf16[256,1024]{1,0:T(8,128)(2,1)S(1)} %copy-done.11, f32[1,1024]{1,0:T(1,128)S(1)} %bitcast.26, ...), custom_call_target="tpu_custom_call" | custom-call | flops 1073741824 | bytes 4194304 | tf_op jit(solution)/shard_map/pallas_call | solution.py:34
  82.1 7.5 %all-to-all-start.4 = ((bf16[16,16,1024]{2,1,0:T(8,128)(2,1)}), bf16[16,16,1024]{2,1,0:T(8,128)(2,1)}, u32[]{:S(2)}, u32[]{:S(2)}) async-start(bf16[16,16,1024]{2,1,0:T(8,128)(2,1)} %bitcast.21), calls=%async_computation.4 | async-start | bytes 1048576 | tf_op jit(solution)/shard_map/all_to_all | solution.py:242
  89.6 2.6 %collective-permute-start.10 = (bf16[256,1024]{1,0:T(8,128)(2,1)}, bf16[256,1024]{1,0:T(8,128)(2,1)S(1)}, u32[]{:S(2)}, u32[]{:S(2)}) collective-permute-start(bf16[256,1024]{1,0:T(8,128)(2,1)} %get-tuple-element.84.slot2_ref), channel_id=1, source_target_pairs={{0,2},{2,0},{1,3},{3,1},{4,6},{6,4},{5,7},{7,5},{8,10},{10,8},{9,1... | collective-permute-start | bytes 1572872 | tf_op jit(solution)/shard_map/ppermute | solution.py:238
  95.4 3.6 %shard_map.110 = (bf16[256,1024]{1,0:T(8,128)(2,1)}, bf16[256,1024]{1,0:T(8,128)(2,1)}) custom-call(f32[128,128]{1,0:T(8,128)} %copy-done.12, f32[128,128]{1,0:T(8,128)} %copy-done.16, bf16[256,1024]{1,0:T(8,128)(2,1)} %get-tuple-element.83.slot_ref, bf16[256,1024]{1,0:T(8,128)(2,1)} %copy-done.7, f32[1,1024]{1,0:T(1,128)} %bitcast.24), custom_call_target="tpu_custom_call" | custom-call | bytes 1048576 | tf_op jit(solution)/shard_map/pallas_call | solution.py:34
  99.0 4.5 %all-to-all-done.4.parts_ref = bf16[16,16,1024]{2,1,0:T(8,128)(2,1)} async-done(((bf16[16,16,1024]{2,1,0:T(8,128)(2,1)}), bf16[16,16,1024]{2,1,0:T(8,128)(2,1)}, u32[]{:S(2)}, u32[]{:S(2)}) %all-to-all-start.4) | async-done | bytes 524320 | tf_op jit(solution)/shard_map/all_to_all | solution.py:242
  104.8 20.9 %all_to_all.37 = bf16[16,16,1024]{2,1,0:T(8,128)(2,1)} all-to-all(bf16[16,16,1024]{2,1,0:T(8,128)(2,1)S(1)} %shard_map.111), channel_id=1, replica_groups=mesh['section'=4,'yh'=2,'z'=8,'core'=2,'tok'=2] {'yh','z'}, dimensions={0} | all-to-all | bytes 1048576 | tf_op jit(solution)/shard_map/all_to_all | solution.py:242
  125.7 3.2 %shard_map.112 = bf16[8,128,128]{2,1,0:T(8,128)(2,1)} custom-call(bf16[256,1024]{1,0:T(8,128)(2,1)} %bitcast.13.x_ref.grad_ref, s32[128,128]{1,0:T(8,128)S(1)} %get-tuple-element.77.place_ref, bf16[1024,1024]{1,0:T(8,128)(2,1)S(1)} %collective-permute-done.7.w_ref, bf16[1024,1024]{1,0:T(8,128)(2,1)S(1)} %copy-done.2), custom_call_target="tpu_custom_call" | custom-call | flops 1073741824 | bytes 4194304 | tf_op jit(solution)/shard_map/pallas_call | solution.py:34
  128.9 3.3 %collective-permute-start.12 = (bf16[256,1024]{1,0:T(8,128)(2,1)}, bf16[256,1024]{1,0:T(8,128)(2,1)S(1)}, u32[]{:S(2)}, u32[]{:S(2)}) collective-permute-start(bf16[256,1024]{1,0:T(8,128)(2,1)} %bitcast.13.x_ref.grad_ref), channel_id=1, source_target_pairs={{0,2},{2,0},{1,3},{3,1},{4,6},{6,4},{5,7},{7,5},{8,10},{10,8},{9,1... | collective-permute-start | bytes 1572872 | tf_op jit(solution)/shard_map/ppermute | solution.py:238
  132.2 3.4 %all-to-all-start.6 = ((bf16[8,128,128]{2,1,0:T(8,128)(2,1)}), bf16[8,128,128]{2,1,0:T(8,128)(2,1)S(1)}, u32[]{:S(2)}, u32[]{:S(2)}) async-start(bf16[8,128,128]{2,1,0:T(8,128)(2,1)} %shard_map.112), calls=%async_computation.6 | async-start | bytes 524288 | tf_op jit(solution)/shard_map/all_to_all | solution.py:242
  136.5 4.1 %shard_map.113 = bf16[1024,1024]{1,0:T(8,128)(2,1)} custom-call(bf16[256,1024]{1,0:T(8,128)(2,1)} %get-tuple-element.98.codes_ref, bf16[256,1024]{1,0:T(8,128)(2,1)} %get-tuple-element.99.codes2_ref, bf16[256,1024]{1,0:T(8,128)(2,1)} %bitcast.13.x_ref.grad_ref, bf16[256,1024]{1,0:T(8,128)(2,1)} %copy-done.15), custom_call_target="tpu_custom_call" | custom-call | flops 1073741824 | bytes 4194304 | tf_op jit(solution)/shard_map/pallas_call | solution.py:34
  140.6 1.8 %all-to-all-done.6.parts_ref = bf16[8,128,128]{2,1,0:T(8,128)(2,1)S(1)} async-done(((bf16[8,128,128]{2,1,0:T(8,128)(2,1)}), bf16[8,128,128]{2,1,0:T(8,128)(2,1)S(1)}, u32[]{:S(2)}, u32[]{:S(2)}) %all-to-all-start.6) | async-done | bytes 262176 | tf_op jit(solution)/shard_map/all_to_all | solution.py:242
  143.2 2.1 %shard_map.114 = (f32[1024,1024]{1,0:T(8,128)S(1)}, f32[1,512]{1,0:T(1,128)S(1)}) custom-call(s32[4]{0:T(128)S(1)} %pad_add_fusion.at_ref, bf16[8,128,128]{2,1,0:T(8,128)(2,1)S(1)} %all-to-all-done.6.parts_ref, bf16[256,1024]{1,0:T(8,128)(2,1)S(1)} %copy-done.6, bf16[256,1024]{1,0:T(8,128)(2,1)S(1)} %bitcast.20), custom_call_target="tpu_custom_call" | custom-call | flops 1073741824 | bytes 4194304 | tf_op jit(solution)/shard_map/pallas_call | solution.py:34
  145.3 4.1 %shard_map.115 = (bf16[1024,1024]{1,0:T(8,128)(2,1)}, f32[1,512]{1,0:T(1,128)}) custom-call(s32[4]{0:T(128)S(1)} %pad_add_fusion.at_ref, bf16[8,128,128]{2,1,0:T(8,128)(2,1)S(1)} %collective-permute-done.13.parts_ref, bf16[256,1024]{1,0:T(8,128)(2,1)S(1)} %copy-done.8, bf16[256,1024]{1,0:T(8,128)(2,1)} %collective-permute-done.11.x_ref, ...), custom_call_target="tpu_custom_call" | custom-call | flops 1073741824 | bytes 4194304 | tf_op jit(solution)/shard_map/pallas_call | solution.py:34
  (68 shorter events, 17.0 us)
Async XLA Ops:
  2.7 15.9 %collective-permute-start.1 = (bf16[256,1024]{1,0:T(8,128)(2,1)S(1)}, bf16[256,1024]{1,0:T(8,128)(2,1)S(1)}, u32[]{:S(2)}, u32[]{:S(2)}) collective-permute-start(bf16[256,1024]{1,0:T(8,128)(2,1)S(1)} %constant_dynamic-slice_fusion.w_ref), channel_id=1, source_target_pairs={{0,2},{2,0},{1,3},{3,1},{4,6},{6,4},{5,7},{7,5},{8,10},{10,8},{9,1... | collective-permute-start | bytes 1572872 | tf_op jit(solution)/shard_map/ppermute | solution.py:238
  5.9 10.9 %all-to-all-start = ((bf16[8,64,256]{2,1,0:T(8,128)(2,1)}), bf16[8,64,256]{2,1,0:T(8,128)(2,1)S(1)}, u32[]{:S(2)}, u32[]{:S(2)}) async-start(bf16[8,64,256]{2,1,0:T(8,128)(2,1)} %broadcast_in_dim.16), calls=%async_computation | async-start | bytes 524288 | tf_op jit(solution)/shard_map/all_to_all | solution.py:242
  9.3 21.7 %copy-start.14 = (f32[1024]{0:T(1024)S(1)}, f32[1024]{0:T(1024)}, u32[]{:S(2)}) copy-start(f32[1024]{0:T(1024)} %param.13) | copy-start | bytes 12292
  10.4 35.7 %copy-start.13 = (f32[2048]{0:T(1024)S(1)}, f32[2048]{0:T(1024)}, u32[]{:S(2)}) copy-start(f32[2048]{0:T(1024)} %param.11) | copy-start | bytes 24580
  16.8 1.8 %collective-permute-start = (bf16[256,256]{1,0:T(8,128)(2,1)S(1)}, bf16[256,256]{1,0:T(8,128)(2,1)S(1)}, u32[]{:S(2)}, u32[]{:S(2)}) collective-permute-start(bf16[256,256]{1,0:T(8,128)(2,1)S(1)} %get-tuple-element.109), channel_id=1, source_target_pairs={{0,2},{2,0},{1,3},{3,1},{4,6},{6,4},{5,7},{7,5},{8,10},{10,8},{9,1... | collective-permute-start | bytes 393224 | tf_op jit(solution)/shard_map/ppermute | solution.py:238
  19.8 26.9 %collective-permute-start.3 = (bf16[1024,1024]{1,0:T(8,128)(2,1)}, bf16[1024,1024]{1,0:T(8,128)(2,1)}, u32[]{:S(2)}, u32[]{:S(2)}) collective-permute-start(bf16[1024,1024]{1,0:T(8,128)(2,1)} %param.12), channel_id=1, source_target_pairs={{0,2},{2,0},{1,3},{3,1},{4,6},{6,4},{5,7},{7,5},{8,10},{10,8},{9,1... | collective-permute-start | bytes 6291464 | tf_op jit(solution)/shard_map/ppermute | solution.py:238
  20.3 26.5 %collective-permute-start.4 = (bf16[1024,1024]{1,0:T(8,128)(2,1)}, bf16[1024,1024]{1,0:T(8,128)(2,1)}, u32[]{:S(2)}, u32[]{:S(2)}) collective-permute-start(bf16[1024,1024]{1,0:T(8,128)(2,1)} %param.14), channel_id=1, source_target_pairs={{0,2},{2,0},{1,3},{3,1},{4,6},{6,4},{5,7},{7,5},{8,10},{10,8},{9,1... | collective-permute-start | bytes 6291464 | tf_op jit(solution)/shard_map/ppermute | solution.py:238
  20.4 25.7 %all-to-all-start.1 = ((bf16[16,16,1024]{2,1,0:T(8,128)(2,1)}), bf16[16,16,1024]{2,1,0:T(8,128)(2,1)S(1)}, u32[]{:S(2)}, u32[]{:S(2)}) async-start(bf16[16,16,1024]{2,1,0:T(8,128)(2,1)} %bitcast.9), calls=%async_computation.1 | async-start | bytes 1048576 | tf_op jit(solution)/shard_map/all_to_all | solution.py:242
  31.0 12.6 %collective-permute-start.2 = (f32[1,1024]{1,0:T(1,128)S(1)}, f32[1,1024]{1,0:T(1,128)S(1)}, u32[]{:S(2)}, u32[]{:S(2)}) collective-permute-start(f32[1,1024]{1,0:T(1,128)S(1)} %bitcast.25), channel_id=1, source_target_pairs={{0,2},{2,0},{1,3},{3,1},{4,6},{6,4},{5,7},{7,5},{8,10},{10,8},{9,1... | collective-permute-start | bytes 12296 | tf_op jit(solution)/shard_map/ppermute | solution.py:238
  46.8 22.6 %collective-permute-start.5 = (bf16[1024,1024]{1,0:T(8,128)(2,1)}, bf16[1024,1024]{1,0:T(8,128)(2,1)S(1)}, u32[]{:S(2)}, u32[]{:S(2)}) collective-permute-start(bf16[1024,1024]{1,0:T(8,128)(2,1)} %collective-permute-done.3), channel_id=1, source_target_pairs={{0,2},{2,0},{1,3},{3,1},{4,6},{6,4},{5,7},{7,5},{8,10},{10,8},{9,1... | collective-permute-start | bytes 6291464 | tf_op jit(solution)/shard_map/ppermute | solution.py:238
  49.7 19.7 %collective-permute-start.6 = (bf16[1024,1024]{1,0:T(8,128)(2,1)}, bf16[1024,1024]{1,0:T(8,128)(2,1)S(1)}, u32[]{:S(2)}, u32[]{:S(2)}) collective-permute-start(bf16[1024,1024]{1,0:T(8,128)(2,1)} %param.12), channel_id=1, source_target_pairs={{0,2},{2,0},{1,3},{3,1},{4,6},{6,4},{5,7},{7,5},{8,10},{10,8},{9,1... | collective-permute-start | bytes 6291464 | tf_op jit(solution)/shard_map/ppermute | solution.py:238
  49.8 21.0 %collective-permute-start.7 = (bf16[1024,1024]{1,0:T(8,128)(2,1)}, bf16[1024,1024]{1,0:T(8,128)(2,1)S(1)}, u32[]{:S(2)}, u32[]{:S(2)}) collective-permute-start(bf16[1024,1024]{1,0:T(8,128)(2,1)} %collective-permute-done.4), channel_id=1, source_target_pairs={{0,2},{2,0},{1,3},{3,1},{4,6},{6,4},{5,7},{7,5},{8,10},{10,8},{9,1... | collective-permute-start | bytes 6291464 | tf_op jit(solution)/shard_map/ppermute | solution.py:238
  50.2 20.6 %collective-permute-start.8 = (bf16[1024,1024]{1,0:T(8,128)(2,1)}, bf16[1024,1024]{1,0:T(8,128)(2,1)S(1)}, u32[]{:S(2)}, u32[]{:S(2)}) collective-permute-start(bf16[1024,1024]{1,0:T(8,128)(2,1)} %param.14), channel_id=1, source_target_pairs={{0,2},{2,0},{1,3},{3,1},{4,6},{6,4},{5,7},{7,5},{8,10},{10,8},{9,1... | collective-permute-start | bytes 6291464 | tf_op jit(solution)/shard_map/ppermute | solution.py:238
  69.4 9.7 %copy-start.5 = (bf16[256,1024]{1,0:T(8,128)(2,1)S(1)}, bf16[256,1024]{1,0:T(8,128)(2,1)}, u32[]{:S(2)}) copy-start(bf16[256,1024]{1,0:T(8,128)(2,1)} %get-tuple-element.83.slot_ref) | copy-start | bytes 1572868
  70.8 10.4 %copy-start.1 = (bf16[1024,1024]{1,0:T(8,128)(2,1)}, bf16[1024,1024]{1,0:T(8,128)(2,1)S(1)}, u32[]{:S(2)}) copy-start(bf16[1024,1024]{1,0:T(8,128)(2,1)S(1)} %collective-permute-done.8.w2_ref) | copy-start | bytes 6291460
  82.1 11.9 %copy-start.12 = (f32[128,128]{1,0:T(8,128)}, f32[128,128]{1,0:T(8,128)S(1)}, u32[]{:S(2)}) copy-start(f32[128,128]{1,0:T(8,128)S(1)} %get-tuple-element.91.packed_ref) | copy-start | bytes 196612
  82.1 21.4 %all-to-all-start.4 = ((bf16[16,16,1024]{2,1,0:T(8,128)(2,1)}), bf16[16,16,1024]{2,1,0:T(8,128)(2,1)}, u32[]{:S(2)}, u32[]{:S(2)}) async-start(bf16[16,16,1024]{2,1,0:T(8,128)(2,1)} %bitcast.21), calls=%async_computation.4 | async-start | bytes 1048576 | tf_op jit(solution)/shard_map/all_to_all | solution.py:242
  89.6 4.3 %collective-permute-start.10 = (bf16[256,1024]{1,0:T(8,128)(2,1)}, bf16[256,1024]{1,0:T(8,128)(2,1)S(1)}, u32[]{:S(2)}, u32[]{:S(2)}) collective-permute-start(bf16[256,1024]{1,0:T(8,128)(2,1)} %get-tuple-element.84.slot2_ref), channel_id=1, source_target_pairs={{0,2},{2,0},{1,3},{3,1},{4,6},{6,4},{5,7},{7,5},{8,10},{10,8},{9,1... | collective-permute-start | bytes 1572872 | tf_op jit(solution)/shard_map/ppermute | solution.py:238
  92.2 6.8 %collective-permute-start.11 = (bf16[256,1024]{1,0:T(8,128)(2,1)}, bf16[256,1024]{1,0:T(8,128)(2,1)}, u32[]{:S(2)}, u32[]{:S(2)}) collective-permute-start(bf16[256,1024]{1,0:T(8,128)(2,1)} %bitcast.19), channel_id=1, source_target_pairs={{0,2},{2,0},{1,3},{3,1},{4,6},{6,4},{5,7},{7,5},{8,10},{10,8},{9,1... | collective-permute-start | bytes 1572872 | tf_op jit(solution)/shard_map/ppermute | solution.py:238
  92.3 1.7 %collective-permute-start.9 = (f32[128,128]{1,0:T(8,128)S(1)}, f32[128,128]{1,0:T(8,128)S(1)}, u32[]{:S(2)}, u32[]{:S(2)}) collective-permute-start(f32[128,128]{1,0:T(8,128)S(1)} %get-tuple-element.91.packed_ref), channel_id=1, source_target_pairs={{0,2},{2,0},{1,3},{3,1},{4,6},{6,4},{5,7},{7,5},{8,10},{10,8},{9,1... | collective-permute-start | bytes 196616 | tf_op jit(solution)/shard_map/ppermute | solution.py:238
  103.5 22.2 %copy-start.2 = (bf16[1024,1024]{1,0:T(8,128)(2,1)S(1)}, bf16[1024,1024]{1,0:T(8,128)(2,1)}, u32[]{:S(2)}) copy-start(bf16[1024,1024]{1,0:T(8,128)(2,1)} %copy-done.1) | copy-start | bytes 6291460
  128.9 6.8 %collective-permute-start.12 = (bf16[256,1024]{1,0:T(8,128)(2,1)}, bf16[256,1024]{1,0:T(8,128)(2,1)S(1)}, u32[]{:S(2)}, u32[]{:S(2)}) collective-permute-start(bf16[256,1024]{1,0:T(8,128)(2,1)} %bitcast.13.x_ref.grad_ref), channel_id=1, source_target_pairs={{0,2},{2,0},{1,3},{3,1},{4,6},{6,4},{5,7},{7,5},{8,10},{10,8},{9,1... | collective-permute-start | bytes 1572872 | tf_op jit(solution)/shard_map/ppermute | solution.py:238
  132.2 10.2 %all-to-all-start.6 = ((bf16[8,128,128]{2,1,0:T(8,128)(2,1)}), bf16[8,128,128]{2,1,0:T(8,128)(2,1)S(1)}, u32[]{:S(2)}, u32[]{:S(2)}) async-start(bf16[8,128,128]{2,1,0:T(8,128)(2,1)} %shard_map.112), calls=%async_computation.6 | async-start | bytes 524288 | tf_op jit(solution)/shard_map/all_to_all | solution.py:242
  142.4 2.9 %collective-permute-start.13 = (bf16[8,128,128]{2,1,0:T(8,128)(2,1)S(1)}, bf16[8,128,128]{2,1,0:T(8,128)(2,1)S(1)}, u32[]{:S(2)}, u32[]{:S(2)}) collective-permute-start(bf16[8,128,128]{2,1,0:T(8,128)(2,1)S(1)} %all-to-all-done.6.parts_ref), channel_id=1, source_target_pairs={{0,2},{2,0},{1,3},{3,1},{4,6},{6,4},{5,7},{7,5},{8,10},{10,8},{9,1... | collective-permute-start | bytes 786440 | tf_op jit(solution)/shard_map/ppermute | solution.py:238
  (11 other events, 36.0 us)

commit v9 on v8

--- a/solution.py
+++ b/solution.py
@@ -20,7 +20,7 @@
 SMALL, MIDDLE, MOST = 12, 24, 24
 COPIES = pltpu.SemaphoreType.DMA
 ROW_BLOCKS = 8
-EARLY_ROWS = 32
+EARLY_ROWS = 16
 FEATURES = ("section", "tok")
 COLUMN = ("yh", "z")
 CORE, TOK, FIRST, FIRST2 = range(4)
@@ -373,6 +373,8 @@
         (at, parts, decoder_bias, whitened),
         vmem=SMALL,
     )
+    out, weight, weight2 = lax.optimization_barrier((out, decoder_weight, decoder_weight2))
+    weight, weight2 = swap(weight2), swap(weight)
     grad = exchange(out, COLUMN).reshape(rows, width)
 
     packed = chosen_product(1, grad, weight, weight2)

time: 150 us -> 151 us (level)
  local copies, waits for them, and re-layouts: 5.94 us -> 3.55 us
  waiting for transfers between devices: 13 us -> 15.1 us
  starting transfers between devices: 41 us -> 42.7 us
    ppermute x14 -> x16, starting transfers between devices: 16.1 us -> 19.3 us  [swap(): return lax.ppermute(x, 'core', [(0, 1), (1, 0)])]
    unnamed x34 -> x28, local copies, waits for them, and re-layouts: 4.13 us -> 1.75 us
  transfers between devices with their start and end apart: 18 -> 20, of which waited for: 6 -> 7; matrix products, arithmetic and copies ran while one was open for 1% -> 1% of each run, Pallas kernels for 18% -> 18%
where the time goes in v9:
time: 151 us; the launch traced here: 150 us
  blocking collectives  48.6 us (32%)
  starting transfers between devices  42.7 us (28%)
  Pallas kernels  38 us (25%)
  waiting for transfers between devices  15.1 us (10%)
  local copies, waits for them, and re-layouts  3.55 us (2%)
    all_to_all x3, blocking collectives, exchange(): return lax.all_to_all(x, axes, 0, 0)  48.6 us
    pallas_call x13, Pallas kernels, call(): pl.pallas_call(kernel, in_specs=list(ins), out_specs=tuple((place for pla...  38 us
    all_to_all x4, starting transfers between devices, exchange(): return lax.all_to_all(x, axes, 0, 0)  23.5 us
    ppermute x16, starting transfers between devices, swap(): return lax.ppermute(x, 'core', [(0, 1), (1, 0)])  19.3 us
    all_to_all x4, waiting for transfers between devices, exchange(): return lax.all_to_all(x, axes, 0, 0)  12.3 us
  transfers between devices with their start and end apart: 20, of which 7 were waited for; matrix products, arithmetic and copies ran while one was open for 1% of the time, Pallas kernels for 18%

profile of v9, /device:TPU:1, one launch (start us, length us, event | category | flops | bytes accessed | tf_op | source)
XLA Modules:
  0.0 150.0 jit_solution(48931049652302402)
XLA Ops:
  2.7 3.2 %collective-permute-start.1 = (bf16[256,1024]{1,0:T(8,128)(2,1)S(1)}, bf16[256,1024]{1,0:T(8,128)(2,1)S(1)}, u32[]{:S(2)}, u32[]{:S(2)}) collective-permute-start(bf16[256,1024]{1,0:T(8,128)(2,1)S(1)} %constant_dynamic-slice_fusion.w_ref), channel_id=1, source_target_pairs={{0,2},{2,0},{1,3},{3,1},{4,6},{6,4},{5,7},{7,5},{8,10},{10,8},{9,1... | collective-permute-start | bytes 1572872 | tf_op jit(solution)/shard_map/ppermute | solution.py:238
  5.9 3.4 %all-to-all-start = ((bf16[8,64,256]{2,1,0:T(8,128)(2,1)}), bf16[8,64,256]{2,1,0:T(8,128)(2,1)S(1)}, u32[]{:S(2)}, u32[]{:S(2)}) async-start(bf16[8,64,256]{2,1,0:T(8,128)(2,1)} %broadcast_in_dim.16), calls=%async_computation | async-start | bytes 524288 | tf_op jit(solution)/shard_map/all_to_all | solution.py:242
  11.8 2.2 %shard_map.104 = (bf16[16,1024]{1,0:T(8,128)(2,1)}, bf16[16,1024]{1,0:T(8,128)(2,1)}) custom-call(s32[256,128]{1,0:T(8,128)} %copy-done.9), custom_call_target="tpu_custom_call" | custom-call | flops 4194304 | bytes 1048576 | tf_op jit(solution)/shard_map/pallas_call | solution.py:34
  14.1 2.7 %all-to-all-done = bf16[8,64,256]{2,1,0:T(8,128)(2,1)S(1)} async-done(((bf16[8,64,256]{2,1,0:T(8,128)(2,1)}), bf16[8,64,256]{2,1,0:T(8,128)(2,1)S(1)}, u32[]{:S(2)}, u32[]{:S(2)}) %all-to-all-start) | async-done | bytes 262176 | tf_op jit(solution)/shard_map/all_to_all | solution.py:242
  20.4 10.6 %all-to-all-start.1 = ((bf16[16,16,1024]{2,1,0:T(8,128)(2,1)}), bf16[16,16,1024]{2,1,0:T(8,128)(2,1)S(1)}, u32[]{:S(2)}, u32[]{:S(2)}) async-start(bf16[16,16,1024]{2,1,0:T(8,128)(2,1)} %bitcast.9), calls=%async_computation.1 | async-start | bytes 1048576 | tf_op jit(solution)/shard_map/all_to_all | solution.py:242
  31.7 12.6 %shard_map.106 = (bf16[256,1024]{1,0:T(8,128)(2,1)}, bf16[256,1024]{1,0:T(8,128)(2,1)}) custom-call(s32[256,128]{1,0:T(8,128)} %copy-done.9, bf16[16,1024]{1,0:T(8,128)(2,1)} %get-tuple-element.70.refs_0_, bf16[16,1024]{1,0:T(8,128)(2,1)} %get-tuple-element.71.refs_1_), custom_call_target="tpu_custom_call" | custom-call | flops 62914560 | bytes 1048576 | tf_op jit(solution)/shard_map/pallas_call | solution.py:34
  44.3 1.8 %all-to-all-done.1.parts_ref = bf16[16,16,1024]{2,1,0:T(8,128)(2,1)S(1)} async-done(((bf16[16,16,1024]{2,1,0:T(8,128)(2,1)}), bf16[16,16,1024]{2,1,0:T(8,128)(2,1)S(1)}, u32[]{:S(2)}, u32[]{:S(2)}) %all-to-all-start.1) | async-done | bytes 524320 | tf_op jit(solution)/shard_map/all_to_all | solution.py:242
  46.8 2.9 %collective-permute-start.5 = (bf16[1024,1024]{1,0:T(8,128)(2,1)}, bf16[1024,1024]{1,0:T(8,128)(2,1)S(1)}, u32[]{:S(2)}, u32[]{:S(2)}) collective-permute-start(bf16[1024,1024]{1,0:T(8,128)(2,1)} %collective-permute-done.3), channel_id=1, source_target_pairs={{0,2},{2,0},{1,3},{3,1},{4,6},{6,4},{5,7},{7,5},{8,10},{10,8},{9,1... | collective-permute-start | bytes 6291464 | tf_op jit(solution)/shard_map/ppermute | solution.py:238
  50.3 20.9 %all_to_all.35 = bf16[16,16,1024]{2,1,0:T(8,128)(2,1)S(1)} all-to-all(bf16[16,16,1024]{2,1,0:T(8,128)(2,1)S(1)} %get-tuple-element.79), channel_id=1, replica_groups=mesh['section'=4,'yh'=2,'z'=8,'core'=2,'tok'=2] {'yh','z'}, dimensions={0} | all-to-all | bytes 1048576 | tf_op jit(solution)/shard_map/all_to_all | solution.py:242
  72.7 8.3 %all_to_all.36.parts_ref = bf16[8,128,128]{2,1,0:T(8,128)(2,1)S(1)} all-to-all(bf16[8,128,128]{2,1,0:T(8,128)(2,1)S(1)} %shard_map.108), channel_id=1, replica_groups=mesh['section'=4,'yh'=2,'z'=8,'core'=2,'tok'=2] {'section','tok'}, dimensions={0} | all-to-all | bytes 524288 | tf_op jit(solution)/shard_map/all_to_all | solution.py:242
  81.0 3.0 %shard_map.109 = (f32[128,128]{1,0:T(8,128)S(1)}, bf16[256,1024]{1,0:T(8,128)(2,1)}) custom-call(bf16[8,128,128]{2,1,0:T(8,128)(2,1)S(1)} %all_to_all.36.parts_ref, bf16[256,1024]{1,0:T(8,128)(2,1)S(1)} %copy-done.2, bf16[256,1024]{1,0:T(8,128)(2,1)S(1)} %copy-done.8, f32[1,1024]{1,0:T(1,128)S(1)} %bitcast.28, ...), custom_call_target="tpu_custom_call" | custom-call | flops 1073741824 | bytes 4194304 | tf_op jit(solution)/shard_map/pallas_call | solution.py:34
  83.9 6.1 %all-to-all-start.4 = ((bf16[16,16,1024]{2,1,0:T(8,128)(2,1)}), bf16[16,16,1024]{2,1,0:T(8,128)(2,1)S(1)}, u32[]{:S(2)}, u32[]{:S(2)}) async-start(bf16[16,16,1024]{2,1,0:T(8,128)(2,1)} %bitcast.12), calls=%async_computation.4 | async-start | bytes 1048576 | tf_op jit(solution)/shard_map/all_to_all | solution.py:242
  90.0 2.3 %collective-permute-start.10 = (bf16[256,1024]{1,0:T(8,128)(2,1)S(1)}, bf16[256,1024]{1,0:T(8,128)(2,1)S(1)}, u32[]{:S(2)}, u32[]{:S(2)}) collective-permute-start(bf16[256,1024]{1,0:T(8,128)(2,1)S(1)} %copy-done.8), channel_id=1, source_target_pairs={{0,2},{2,0},{1,3},{3,1},{4,6},{6,4},{5,7},{7,5},{8,10},{10,8},{9,1... | collective-permute-start | bytes 1572872 | tf_op jit(solution)/shard_map/ppermute | solution.py:238
  95.3 3.6 %shard_map.110 = (bf16[256,1024]{1,0:T(8,128)(2,1)}, bf16[256,1024]{1,0:T(8,128)(2,1)}) custom-call(f32[128,128]{1,0:T(8,128)} %copy-done.10, f32[128,128]{1,0:T(8,128)} %copy-done.13, bf16[256,1024]{1,0:T(8,128)(2,1)} %get-tuple-element.86.slot_ref, bf16[256,1024]{1,0:T(8,128)(2,1)} %copy-done.4, f32[1,1024]{1,0:T(1,128)} %bitcast.26), custom_call_target="tpu_custom_call" | custom-call | bytes 1048576 | tf_op jit(solution)/shard_map/pallas_call | solution.py:34
  98.9 5.2 %all-to-all-done.4.parts_ref = bf16[16,16,1024]{2,1,0:T(8,128)(2,1)S(1)} async-done(((bf16[16,16,1024]{2,1,0:T(8,128)(2,1)}), bf16[16,16,1024]{2,1,0:T(8,128)(2,1)S(1)}, u32[]{:S(2)}, u32[]{:S(2)}) %all-to-all-start.4) | async-done | bytes 524320 | tf_op jit(solution)/shard_map/all_to_all | solution.py:242
  104.8 3.5 %collective-permute-start.12 = (bf16[1024,1024]{1,0:T(8,128)(2,1)}, bf16[1024,1024]{1,0:T(8,128)(2,1)S(1)}, u32[]{:S(2)}, u32[]{:S(2)}) collective-permute-start(bf16[1024,1024]{1,0:T(8,128)(2,1)} %collective-permute-done.4), channel_id=1, source_target_pairs={{0,2},{2,0},{1,3},{3,1},{4,6},{6,4},{5,7},{7,5},{8,10},{10,8},{9,1... | collective-permute-start | bytes 6291464 | tf_op jit(solution)/shard_map/ppermute | solution.py:238
  108.4 19.4 %all_to_all.37 = bf16[16,16,1024]{2,1,0:T(8,128)(2,1)S(1)} all-to-all(bf16[16,16,1024]{2,1,0:T(8,128)(2,1)S(1)} %shard_map.111), channel_id=1, replica_groups=mesh['section'=4,'yh'=2,'z'=8,'core'=2,'tok'=2] {'yh','z'}, dimensions={0} | all-to-all | bytes 1048576 | tf_op jit(solution)/shard_map/all_to_all | solution.py:242
  127.8 2.2 %shard_map.112 = bf16[8,128,128]{2,1,0:T(8,128)(2,1)} custom-call(bf16[256,1024]{1,0:T(8,128)(2,1)S(1)} %bitcast.18, s32[128,128]{1,0:T(8,128)S(1)} %get-tuple-element.80.place_ref, bf16[1024,1024]{1,0:T(8,128)(2,1)S(1)} %collective-permute-done.12.w_ref, bf16[1024,1024]{1,0:T(8,128)(2,1)S(1)} %collective-permute-done.13.w2_ref), custom_call_target="tpu_custom_call" | custom-call | flops 1073741824 | bytes 4194304 | tf_op jit(solution)/shard_map/pallas_call | solution.py:34
  130.0 3.1 %collective-permute-start.14 = (bf16[256,1024]{1,0:T(8,128)(2,1)S(1)}, bf16[256,1024]{1,0:T(8,128)(2,1)}, u32[]{:S(2)}, u32[]{:S(2)}) collective-permute-start(bf16[256,1024]{1,0:T(8,128)(2,1)S(1)} %bitcast.19), channel_id=1, source_target_pairs={{0,2},{2,0},{1,3},{3,1},{4,6},{6,4},{5,7},{7,5},{8,10},{10,8},{9,1... | collective-permute-start | bytes 1572872 | tf_op jit(solution)/shard_map/ppermute | solution.py:238
  133.1 3.4 %all-to-all-start.6 = ((bf16[8,128,128]{2,1,0:T(8,128)(2,1)}), bf16[8,128,128]{2,1,0:T(8,128)(2,1)S(1)}, u32[]{:S(2)}, u32[]{:S(2)}) async-start(bf16[8,128,128]{2,1,0:T(8,128)(2,1)} %shard_map.112), calls=%async_computation.6 | async-start | bytes 524288 | tf_op jit(solution)/shard_map/all_to_all | solution.py:242
  136.6 4.2 %shard_map.113 = bf16[1024,1024]{1,0:T(8,128)(2,1)} custom-call(bf16[256,1024]{1,0:T(8,128)(2,1)} %get-tuple-element.104.codes_ref, bf16[256,1024]{1,0:T(8,128)(2,1)} %get-tuple-element.105.codes2_ref, bf16[256,1024]{1,0:T(8,128)(2,1)} %bitcast.20, bf16[256,1024]{1,0:T(8,128)(2,1)} %collective-permute-done.14.grad2_ref), custom_call_target="tpu_custom_call" | custom-call | flops 1073741824 | bytes 4194304 | tf_op jit(solution)/shard_map/pallas_call | solution.py:34
  140.8 2.6 %all-to-all-done.6.parts_ref = bf16[8,128,128]{2,1,0:T(8,128)(2,1)S(1)} async-done(((bf16[8,128,128]{2,1,0:T(8,128)(2,1)}), bf16[8,128,128]{2,1,0:T(8,128)(2,1)S(1)}, u32[]{:S(2)}, u32[]{:S(2)}) %all-to-all-start.6) | async-done | bytes 262176 | tf_op jit(solution)/shard_map/all_to_all | solution.py:242
  144.1 2.1 %shard_map.114 = (f32[1024,1024]{1,0:T(8,128)S(1)}, f32[1,512]{1,0:T(1,128)S(1)}) custom-call(s32[4]{0:T(128)S(1)} %pad_add_fusion.at_ref, bf16[8,128,128]{2,1,0:T(8,128)(2,1)S(1)} %all-to-all-done.6.parts_ref, bf16[256,1024]{1,0:T(8,128)(2,1)S(1)} %copy-done.3, bf16[256,1024]{1,0:T(8,128)(2,1)S(1)} %bitcast.23), custom_call_target="tpu_custom_call" | custom-call | flops 1073741824 | bytes 4194304 | tf_op jit(solution)/shard_map/pallas_call | solution.py:34
  146.3 3.6 %shard_map.115 = (bf16[1024,1024]{1,0:T(8,128)(2,1)}, f32[1,512]{1,0:T(1,128)}) custom-call(s32[4]{0:T(128)S(1)} %pad_add_fusion.at_ref, bf16[8,128,128]{2,1,0:T(8,128)(2,1)S(1)} %collective-permute-done.15.parts_ref, bf16[256,1024]{1,0:T(8,128)(2,1)S(1)} %copy-done.5, bf16[256,1024]{1,0:T(8,128)(2,1)S(1)} %copy-done.7, ...), custom_call_target="tpu_custom_call" | custom-call | flops 1073741824 | bytes 4194304 | tf_op jit(solution)/shard_map/pallas_call | solution.py:34
  (66 shorter events, 16.2 us)
Async XLA Ops:
  2.7 15.9 %collective-permute-start.1 = (bf16[256,1024]{1,0:T(8,128)(2,1)S(1)}, bf16[256,1024]{1,0:T(8,128)(2,1)S(1)}, u32[]{:S(2)}, u32[]{:S(2)}) collective-permute-start(bf16[256,1024]{1,0:T(8,128)(2,1)S(1)} %constant_dynamic-slice_fusion.w_ref), channel_id=1, source_target_pairs={{0,2},{2,0},{1,3},{3,1},{4,6},{6,4},{5,7},{7,5},{8,10},{10,8},{9,1... | collective-permute-start | bytes 1572872 | tf_op jit(solution)/shard_map/ppermute | solution.py:238
  5.9 10.9 %all-to-all-start = ((bf16[8,64,256]{2,1,0:T(8,128)(2,1)}), bf16[8,64,256]{2,1,0:T(8,128)(2,1)S(1)}, u32[]{:S(2)}, u32[]{:S(2)}) async-start(bf16[8,64,256]{2,1,0:T(8,128)(2,1)} %broadcast_in_dim.16), calls=%async_computation | async-start | bytes 524288 | tf_op jit(solution)/shard_map/all_to_all | solution.py:242
  9.3 21.7 %copy-start.12 = (f32[1024]{0:T(1024)S(1)}, f32[1024]{0:T(1024)}, u32[]{:S(2)}) copy-start(f32[1024]{0:T(1024)} %param.13) | copy-start | bytes 12292
  10.4 35.7 %copy-start.11 = (f32[2048]{0:T(1024)S(1)}, f32[2048]{0:T(1024)}, u32[]{:S(2)}) copy-start(f32[2048]{0:T(1024)} %param.11) | copy-start | bytes 24580
  16.8 1.8 %collective-permute-start = (bf16[256,256]{1,0:T(8,128)(2,1)S(1)}, bf16[256,256]{1,0:T(8,128)(2,1)S(1)}, u32[]{:S(2)}, u32[]{:S(2)}) collective-permute-start(bf16[256,256]{1,0:T(8,128)(2,1)S(1)} %get-tuple-element.115), channel_id=1, source_target_pairs={{0,2},{2,0},{1,3},{3,1},{4,6},{6,4},{5,7},{7,5},{8,10},{10,8},{9,1... | collective-permute-start | bytes 393224 | tf_op jit(solution)/shard_map/ppermute | solution.py:238
  19.8 26.9 %collective-permute-start.3 = (bf16[1024,1024]{1,0:T(8,128)(2,1)}, bf16[1024,1024]{1,0:T(8,128)(2,1)}, u32[]{:S(2)}, u32[]{:S(2)}) collective-permute-start(bf16[1024,1024]{1,0:T(8,128)(2,1)} %param.12), channel_id=1, source_target_pairs={{0,2},{2,0},{1,3},{3,1},{4,6},{6,4},{5,7},{7,5},{8,10},{10,8},{9,1... | collective-permute-start | bytes 6291464 | tf_op jit(solution)/shard_map/ppermute | solution.py:238
  20.3 26.5 %collective-permute-start.4 = (bf16[1024,1024]{1,0:T(8,128)(2,1)}, bf16[1024,1024]{1,0:T(8,128)(2,1)}, u32[]{:S(2)}, u32[]{:S(2)}) collective-permute-start(bf16[1024,1024]{1,0:T(8,128)(2,1)} %param.14), channel_id=1, source_target_pairs={{0,2},{2,0},{1,3},{3,1},{4,6},{6,4},{5,7},{7,5},{8,10},{10,8},{9,1... | collective-permute-start | bytes 6291464 | tf_op jit(solution)/shard_map/ppermute | solution.py:238
  20.4 25.7 %all-to-all-start.1 = ((bf16[16,16,1024]{2,1,0:T(8,128)(2,1)}), bf16[16,16,1024]{2,1,0:T(8,128)(2,1)S(1)}, u32[]{:S(2)}, u32[]{:S(2)}) async-start(bf16[16,16,1024]{2,1,0:T(8,128)(2,1)} %bitcast.9), calls=%async_computation.1 | async-start | bytes 1048576 | tf_op jit(solution)/shard_map/all_to_all | solution.py:242
  31.0 13.3 %collective-permute-start.2 = (f32[1,1024]{1,0:T(1,128)S(1)}, f32[1,1024]{1,0:T(1,128)S(1)}, u32[]{:S(2)}, u32[]{:S(2)}) collective-permute-start(f32[1,1024]{1,0:T(1,128)S(1)} %bitcast.27), channel_id=1, source_target_pairs={{0,2},{2,0},{1,3},{3,1},{4,6},{6,4},{5,7},{7,5},{8,10},{10,8},{9,1... | collective-permute-start | bytes 12296 | tf_op jit(solution)/shard_map/ppermute | solution.py:238
  46.8 24.4 %collective-permute-start.5 = (bf16[1024,1024]{1,0:T(8,128)(2,1)}, bf16[1024,1024]{1,0:T(8,128)(2,1)S(1)}, u32[]{:S(2)}, u32[]{:S(2)}) collective-permute-start(bf16[1024,1024]{1,0:T(8,128)(2,1)} %collective-permute-done.3), channel_id=1, source_target_pairs={{0,2},{2,0},{1,3},{3,1},{4,6},{6,4},{5,7},{7,5},{8,10},{10,8},{9,1... | collective-permute-start | bytes 6291464 | tf_op jit(solution)/shard_map/ppermute | solution.py:238
  49.7 21.6 %collective-permute-start.6 = (bf16[1024,1024]{1,0:T(8,128)(2,1)}, bf16[1024,1024]{1,0:T(8,128)(2,1)S(1)}, u32[]{:S(2)}, u32[]{:S(2)}) collective-permute-start(bf16[1024,1024]{1,0:T(8,128)(2,1)} %param.12), channel_id=1, source_target_pairs={{0,2},{2,0},{1,3},{3,1},{4,6},{6,4},{5,7},{7,5},{8,10},{10,8},{9,1... | collective-permute-start | bytes 6291464 | tf_op jit(solution)/shard_map/ppermute | solution.py:238
  49.8 22.9 %collective-permute-start.7 = (bf16[1024,1024]{1,0:T(8,128)(2,1)}, bf16[1024,1024]{1,0:T(8,128)(2,1)S(1)}, u32[]{:S(2)}, u32[]{:S(2)}) collective-permute-start(bf16[1024,1024]{1,0:T(8,128)(2,1)} %collective-permute-done.4), channel_id=1, source_target_pairs={{0,2},{2,0},{1,3},{3,1},{4,6},{6,4},{5,7},{7,5},{8,10},{10,8},{9,1... | collective-permute-start | bytes 6291464 | tf_op jit(solution)/shard_map/ppermute | solution.py:238
  50.2 22.5 %collective-permute-start.8 = (bf16[1024,1024]{1,0:T(8,128)(2,1)}, bf16[1024,1024]{1,0:T(8,128)(2,1)S(1)}, u32[]{:S(2)}, u32[]{:S(2)}) collective-permute-start(bf16[1024,1024]{1,0:T(8,128)(2,1)} %param.14), channel_id=1, source_target_pairs={{0,2},{2,0},{1,3},{3,1},{4,6},{6,4},{5,7},{7,5},{8,10},{10,8},{9,1... | collective-permute-start | bytes 6291464 | tf_op jit(solution)/shard_map/ppermute | solution.py:238
  83.9 10.8 %copy-start.10 = (f32[128,128]{1,0:T(8,128)}, f32[128,128]{1,0:T(8,128)S(1)}, u32[]{:S(2)}) copy-start(f32[128,128]{1,0:T(8,128)S(1)} %get-tuple-element.94.packed_ref) | copy-start | bytes 196612
  83.9 20.2 %all-to-all-start.4 = ((bf16[16,16,1024]{2,1,0:T(8,128)(2,1)}), bf16[16,16,1024]{2,1,0:T(8,128)(2,1)S(1)}, u32[]{:S(2)}, u32[]{:S(2)}) async-start(bf16[16,16,1024]{2,1,0:T(8,128)(2,1)} %bitcast.12), calls=%async_computation.4 | async-start | bytes 1048576 | tf_op jit(solution)/shard_map/all_to_all | solution.py:242
  90.0 3.8 %collective-permute-start.10 = (bf16[256,1024]{1,0:T(8,128)(2,1)S(1)}, bf16[256,1024]{1,0:T(8,128)(2,1)S(1)}, u32[]{:S(2)}, u32[]{:S(2)}) collective-permute-start(bf16[256,1024]{1,0:T(8,128)(2,1)S(1)} %copy-done.8), channel_id=1, source_target_pairs={{0,2},{2,0},{1,3},{3,1},{4,6},{6,4},{5,7},{7,5},{8,10},{10,8},{9,1... | collective-permute-start | bytes 1572872 | tf_op jit(solution)/shard_map/ppermute | solution.py:238
  92.3 6.6 %collective-permute-start.11 = (bf16[256,1024]{1,0:T(8,128)(2,1)S(1)}, bf16[256,1024]{1,0:T(8,128)(2,1)S(1)}, u32[]{:S(2)}, u32[]{:S(2)}) collective-permute-start(bf16[256,1024]{1,0:T(8,128)(2,1)S(1)} %bitcast.22), channel_id=1, source_target_pairs={{0,2},{2,0},{1,3},{3,1},{4,6},{6,4},{5,7},{7,5},{8,10},{10,8},{9,1... | collective-permute-start | bytes 1572872 | tf_op jit(solution)/shard_map/ppermute | solution.py:238
  92.4 2.3 %collective-permute-start.9 = (f32[128,128]{1,0:T(8,128)S(1)}, f32[128,128]{1,0:T(8,128)S(1)}, u32[]{:S(2)}, u32[]{:S(2)}) collective-permute-start(f32[128,128]{1,0:T(8,128)S(1)} %get-tuple-element.94.packed_ref), channel_id=1, source_target_pairs={{0,2},{2,0},{1,3},{3,1},{4,6},{6,4},{5,7},{7,5},{8,10},{10,8},{9,1... | collective-permute-start | bytes 196616 | tf_op jit(solution)/shard_map/ppermute | solution.py:238
  98.9 31.1 %copy-start.6 = (bf16[256,1024]{1,0:T(8,128)(2,1)}, bf16[256,1024]{1,0:T(8,128)(2,1)S(1)}, u32[]{:S(2)}) copy-start(bf16[256,1024]{1,0:T(8,128)(2,1)S(1)} %collective-permute-done.11.x_ref) | copy-start | bytes 1572868
  104.8 23.0 %collective-permute-start.12 = (bf16[1024,1024]{1,0:T(8,128)(2,1)}, bf16[1024,1024]{1,0:T(8,128)(2,1)S(1)}, u32[]{:S(2)}, u32[]{:S(2)}) collective-permute-start(bf16[1024,1024]{1,0:T(8,128)(2,1)} %collective-permute-done.4), channel_id=1, source_target_pairs={{0,2},{2,0},{1,3},{3,1},{4,6},{6,4},{5,7},{7,5},{8,10},{10,8},{9,1... | collective-permute-start | bytes 6291464 | tf_op jit(solution)/shard_map/ppermute | solution.py:238
  108.3 19.5 %collective-permute-start.13 = (bf16[1024,1024]{1,0:T(8,128)(2,1)}, bf16[1024,1024]{1,0:T(8,128)(2,1)S(1)}, u32[]{:S(2)}, u32[]{:S(2)}) collective-permute-start(bf16[1024,1024]{1,0:T(8,128)(2,1)} %param.14), channel_id=1, source_target_pairs={{0,2},{2,0},{1,3},{3,1},{4,6},{6,4},{5,7},{7,5},{8,10},{10,8},{9,1... | collective-permute-start | bytes 6291464 | tf_op jit(solution)/shard_map/ppermute | solution.py:238
  130.0 6.6 %collective-permute-start.14 = (bf16[256,1024]{1,0:T(8,128)(2,1)S(1)}, bf16[256,1024]{1,0:T(8,128)(2,1)}, u32[]{:S(2)}, u32[]{:S(2)}) collective-permute-start(bf16[256,1024]{1,0:T(8,128)(2,1)S(1)} %bitcast.19), channel_id=1, source_target_pairs={{0,2},{2,0},{1,3},{3,1},{4,6},{6,4},{5,7},{7,5},{8,10},{10,8},{9,1... | collective-permute-start | bytes 1572872 | tf_op jit(solution)/shard_map/ppermute | solution.py:238
  133.1 10.2 %all-to-all-start.6 = ((bf16[8,128,128]{2,1,0:T(8,128)(2,1)}), bf16[8,128,128]{2,1,0:T(8,128)(2,1)S(1)}, u32[]{:S(2)}, u32[]{:S(2)}) async-start(bf16[8,128,128]{2,1,0:T(8,128)(2,1)} %shard_map.112), calls=%async_computation.6 | async-start | bytes 524288 | tf_op jit(solution)/shard_map/all_to_all | solution.py:242
  143.3 2.9 %collective-permute-start.15 = (bf16[8,128,128]{2,1,0:T(8,128)(2,1)S(1)}, bf16[8,128,128]{2,1,0:T(8,128)(2,1)S(1)}, u32[]{:S(2)}, u32[]{:S(2)}) collective-permute-start(bf16[8,128,128]{2,1,0:T(8,128)(2,1)S(1)} %all-to-all-done.6.parts_ref), channel_id=1, source_target_pairs={{0,2},{2,0},{1,3},{3,1},{4,6},{6,4},{5,7},{7,5},{8,10},{10,8},{9,1... | collective-permute-start | bytes 786440 | tf_op jit(solution)/shard_map/ppermute | solution.py:238
  (10 other events, 43.6 us)
